TPU v7x, 32 devices: a whole 2x2x4 slice. The times are simulated.
32 devices in a mesh: ctx: 8 (over y, x, core), shard: 4 (over z).
Axes of the slice: x: 2, y: 2, z: 4, core: 2. Of those that a mesh axis runs over, the one named last changes fastest.
Arguments:
- tokens: bfloat16 [4, 1024, 2048], P('shard', 'ctx'), may hold values from -6 to 6
- lengths: int32 [4, 9], P('shard'), may hold values from 1 to 512, as said below
- cotangent: bfloat16 [4, 1024, 2048], P('shard', 'ctx'), may hold values from -6 to 6
- w_qkv: bfloat16 [2048, 3072], P(('ctx', 'shard')), may hold values from -0.5 to 0.5
- w_out: bfloat16 [2048, 2048], P(('ctx', 'shard')), may hold values from -2 to 2
- w_gate_up: bfloat16 [2048, 16384], P(('ctx', 'shard')), may hold values from -0.125 to 0.125
- w_down: bfloat16 [8192, 2048], P(('ctx', 'shard')), may hold values from -0.25 to 0.25
- gain_attn: bfloat16 [2048], P(('ctx', 'shard')), may hold values from 0.5 to 1.5
- gain_mlp: bfloat16 [2048], P(('ctx', 'shard')), may hold values from 0.5 to 1.5
Outputs:
- mixed: bfloat16 [4, 1024, 2048], P('shard', 'ctx')
- grad_tokens: float32 [4, 1024, 2048], P('shard', 'ctx')
- grad_qkv: float32 [2048, 3072], P(('ctx', 'shard'))
- grad_out: float32 [2048, 2048], P(('ctx', 'shard'))
- grad_gate_up: float32 [2048, 16384], P(('ctx', 'shard'))
- grad_down: float32 [8192, 2048], P(('ctx', 'shard'))
- grad_gain_attn: float32 [2048], P(('ctx', 'shard'))
- grad_gain_mlp: float32 [2048], P(('ctx', 'shard'))
- clip: float32 [32], replicated
Inputs may be any that keep to these rules, and one draw needn't show every extreme that they name: Each row is the prompt's length 512, then the lengths of 8 continuations that fill the rest of the group.
All inputs are finite; a program needn't handle non-finite values.
Results may differ from a plain program's by a relative error of at most 0.02.
Values may be sent and summed in bfloat16 or wider, within the bound.
A program may use at most 448 MiB of HBM per device.

v0:
```python
import math

import jax
import jax.numpy as jnp
from jax import lax
from jax.sharding import PartitionSpec as P

HEADS = 32
KV_HEADS = 8
HEAD_DIM = 64


SCALE = 0.015625
BRANCH = 0.22
EPSILON = 1e-05
CLIP_TARGET = 4.0
NEGATIVE = -1e30


def segment_ids(positions, lengths_row):
    bounds = jnp.cumsum(lengths_row)[:-1]
    return jnp.sum((positions[:, None] >= bounds[None, :]).astype(jnp.int32), axis=1)


def visible(q_pos, q_seg, k_pos, k_seg):
    earlier = k_pos[None, :] <= q_pos[:, None]
    shared = (k_seg[None, :] == 0) | (k_seg[None, :] == q_seg[:, None])
    return earlier & shared


def rms_scale(rows):
    return lax.rsqrt(jnp.mean(rows * rows, axis=-1, keepdims=True) + EPSILON)


def norm_backward(d_normed, rows, scale, gain):
    unit = rows * scale
    d_unit = d_normed * gain
    gain_term = jnp.sum(d_normed * unit, axis=0)
    d_rows = scale * (d_unit - unit * jnp.mean(d_unit * unit, axis=-1, keepdims=True))
    return (d_rows, gain_term)


def key_blocks(keys, values, start):
    count = keys.shape[0]
    size = math.gcd(count, 512)
    key_four = keys.reshape(count // size, size, KV_HEADS, HEAD_DIM)
    value_four = values.reshape(count // size, size, KV_HEADS, HEAD_DIM)
    positions = (start + jnp.arange(count, dtype=jnp.int32)).reshape(count // size, size)
    return (key_four, value_four, positions)


def attend_keys(state, queries, keys, values, start, q_pos, q_seg, lengths_row):
    key_four, value_four, positions = key_blocks(keys, values, start)

    def attend_step(carry, item):
        key_block, value_block, k_pos = item
        peak, total, accum = carry
        live = visible(q_pos, q_seg, k_pos, segment_ids(k_pos, lengths_row))[:, None, None, :]
        scores = (
            jnp.einsum("tgrd,kgd->tgrk", queries, key_block, preferred_element_type=jnp.float32)
            * SCALE
        )
        scores = jnp.where(live, scores, NEGATIVE)
        new_peak = jnp.maximum(peak, jnp.max(scores, axis=-1))
        weights = jnp.where(live, jnp.exp(scores - new_peak[..., None]), 0.0)
        factor = jnp.exp(peak - new_peak)
        total = total * factor + jnp.sum(weights, axis=-1)
        accum = accum * factor[..., None] + jnp.einsum(
            "tgrk,kgd->tgrd",
            weights.astype(jnp.bfloat16),
            value_block,
            preferred_element_type=jnp.float32,
        )
        return ((new_peak, total, accum), None)

    state, unused = lax.scan(attend_step, state, (key_four, value_four, positions))
    return state


def key_gradients(queries, d_heads, delta, log_total, keys, values, q_pos, q_seg, lengths_row):
    count = keys.shape[0]
    key_four, value_four, positions = key_blocks(keys, values, 0)

    def key_step(q_grad, item):
        key_block, value_block, k_pos = item
        live = visible(q_pos, q_seg, k_pos, segment_ids(k_pos, lengths_row))[:, None, None, :]
        scores = (
            jnp.einsum("tgrd,kgd->tgrk", queries, key_block, preferred_element_type=jnp.float32)
            * SCALE
        )
        probs = jnp.where(live, jnp.exp(scores - log_total[..., None]), 0.0)
        d_probs = jnp.einsum(
            "tgrd,kgd->tgrk", d_heads, value_block, preferred_element_type=jnp.float32
        )
        d_scores = (probs * (d_probs - delta[..., None])).astype(jnp.bfloat16)
        q_grad = (
            q_grad
            + jnp.einsum("tgrk,kgd->tgrd", d_scores, key_block, preferred_element_type=jnp.float32)
            * SCALE
        )
        k_grad = (
            jnp.einsum("tgrk,tgrd->kgd", d_scores, queries, preferred_element_type=jnp.float32)
            * SCALE
        )
        v_grad = jnp.einsum(
            "tgrk,tgrd->kgd",
            probs.astype(jnp.bfloat16),
            d_heads,
            preferred_element_type=jnp.float32,
        )
        return (q_grad, (k_grad, v_grad))

    start_grad = jnp.zeros(queries.shape, jnp.float32)
    q_grad, (k_terms, v_terms) = lax.scan(key_step, start_grad, (key_four, value_four, positions))
    return (
        q_grad,
        k_terms.reshape(count, KV_HEADS * HEAD_DIM),
        v_terms.reshape(count, KV_HEADS * HEAD_DIM),
    )


def contract_rows(left, right):
    return lax.dot_general(
        left, right, (((0,), (0,)), ((), ())), preferred_element_type=jnp.float32
    )


def per_device(tokens, lengths, cotangent, w_qkv, w_out, w_gate_up, w_down, gain_attn, gain_mlp):
    count = tokens.shape[1]
    width = tokens.shape[2]
    repeat = HEADS // KV_HEADS
    q_width = HEADS * HEAD_DIM
    kv_width = KV_HEADS * HEAD_DIM
    rows = tokens.reshape(count, width).astype(jnp.float32)
    lengths_row = lengths[0]
    full_qkv, full_out, gain_one, gain_two = (
        lax.all_gather(w_qkv, ("ctx", "shard"), axis=0, tiled=True),
        lax.all_gather(w_out, ("ctx", "shard"), axis=0, tiled=True),
        lax.all_gather(gain_attn, ("ctx", "shard"), axis=0, tiled=True),
        lax.all_gather(gain_mlp, ("ctx", "shard"), axis=0, tiled=True),
    )
    gain_one = gain_one.astype(jnp.float32)
    gain_two = gain_two.astype(jnp.float32)
    scale_one = rms_scale(rows)
    normed_one = (rows * scale_one * gain_one).astype(jnp.bfloat16)
    projected = jnp.dot(normed_one, full_qkv, preferred_element_type=jnp.float32).astype(
        jnp.bfloat16
    )
    queries = projected[:, :q_width].reshape(count, KV_HEADS, repeat, HEAD_DIM)
    keys = projected[:, q_width : q_width + kv_width]
    values = projected[:, q_width + kv_width :]
    q_pos = lax.axis_index("ctx") * count + jnp.arange(count, dtype=jnp.int32)
    q_seg = segment_ids(q_pos, lengths_row)
    initial = (
        jnp.full((count, KV_HEADS, repeat), NEGATIVE, jnp.float32),
        jnp.zeros((count, KV_HEADS, repeat), jnp.float32),
        jnp.zeros((count, KV_HEADS, repeat, HEAD_DIM), jnp.float32),
    )
    peak, total, accum = attend_keys(
        initial,
        queries,
        lax.all_gather(keys, "ctx", axis=0, tiled=True),
        lax.all_gather(values, "ctx", axis=0, tiled=True),
        jnp.int32(0),
        q_pos,
        q_seg,
        lengths_row,
    )
    attn_heads = (accum / total[..., None]).astype(jnp.bfloat16)
    log_total = peak + jnp.log(total)
    head_peak = lax.pmax(jnp.max(peak, axis=0).reshape(HEADS), ("ctx", "shard"))
    clip = CLIP_TARGET / jnp.maximum(head_peak, CLIP_TARGET)
    attn_out = attn_heads.reshape(count, q_width)
    mid = rows + BRANCH * jnp.dot(attn_out, full_out, preferred_element_type=jnp.float32)
    full_gate_up, full_down = (
        lax.all_gather(w_gate_up, ("ctx", "shard"), axis=0, tiled=True),
        lax.all_gather(w_down, ("ctx", "shard"), axis=0, tiled=True),
    )
    scale_two = rms_scale(mid)
    normed_two = (mid * scale_two * gain_two).astype(jnp.bfloat16)
    gate_up = jnp.dot(normed_two, full_gate_up, preferred_element_type=jnp.float32)
    ff_width = gate_up.shape[1] // 2
    gate = gate_up[:, :ff_width]
    up = gate_up[:, ff_width:]
    sigma = jax.nn.sigmoid(gate)
    active = gate * sigma
    hidden = (active * up).astype(jnp.bfloat16)
    result = mid + BRANCH * jnp.dot(hidden, full_down, preferred_element_type=jnp.float32)
    mixed = result.astype(jnp.bfloat16).reshape(1, count, width)
    grad_rows = cotangent.reshape(count, width).astype(jnp.float32)
    full_gate_up, full_down = (
        lax.all_gather(w_gate_up, ("ctx", "shard"), axis=0, tiled=True),
        lax.all_gather(w_down, ("ctx", "shard"), axis=0, tiled=True),
    )
    d_mlp = (BRANCH * grad_rows).astype(jnp.bfloat16)
    d_hidden = jnp.dot(d_mlp, full_down.T, preferred_element_type=jnp.float32)
    d_gate = d_hidden * up * sigma * (1.0 + gate * (1.0 - sigma))
    d_up = d_hidden * active
    d_gate_up = jnp.concatenate([d_gate, d_up], axis=1).astype(jnp.bfloat16)
    d_normed_two = jnp.dot(d_gate_up, full_gate_up.T, preferred_element_type=jnp.float32)
    grad_gate_up = lax.psum_scatter(
        contract_rows(normed_two, d_gate_up), ("ctx", "shard"), scatter_dimension=0, tiled=True
    )
    down_term = contract_rows(hidden, d_mlp)
    d_mid_norm, gain_two_term = norm_backward(d_normed_two, mid, scale_two, gain_two)
    d_mid = grad_rows + d_mid_norm
    full_qkv, full_out = (
        lax.all_gather(w_qkv, ("ctx", "shard"), axis=0, tiled=True),
        lax.all_gather(w_out, ("ctx", "shard"), axis=0, tiled=True),
    )
    d_attn = (BRANCH * d_mid).astype(jnp.bfloat16)
    out_term = contract_rows(attn_out, d_attn)
    d_heads = (
        jnp.dot(d_attn, full_out.T, preferred_element_type=jnp.float32)
        .astype(jnp.bfloat16)
        .reshape(count, KV_HEADS, repeat, HEAD_DIM)
    )
    delta = jnp.sum(d_heads.astype(jnp.float32) * attn_heads.astype(jnp.float32), axis=-1)
    all_keys, all_values = (
        lax.all_gather(keys, "ctx", axis=0, tiled=True),
        lax.all_gather(values, "ctx", axis=0, tiled=True),
    )
    q_grad, k_terms, v_terms = key_gradients(
        queries, d_heads, delta, log_total, all_keys, all_values, q_pos, q_seg, lengths_row
    )
    k_grad, v_grad = (
        lax.psum_scatter(
            k_terms.astype(jnp.bfloat16), "ctx", scatter_dimension=0, tiled=True
        ).astype(jnp.float32),
        lax.psum_scatter(
            v_terms.astype(jnp.bfloat16), "ctx", scatter_dimension=0, tiled=True
        ).astype(jnp.float32),
    )
    d_qkv = jnp.concatenate(
        [
            q_grad.reshape(count, q_width).astype(jnp.bfloat16),
            k_grad.astype(jnp.bfloat16),
            v_grad.astype(jnp.bfloat16),
        ],
        axis=1,
    )
    qkv_term = contract_rows(normed_one, d_qkv)
    d_normed_one = jnp.dot(d_qkv, full_qkv.T, preferred_element_type=jnp.float32)
    d_rows_norm, gain_one_term = norm_backward(d_normed_one, rows, scale_one, gain_one)
    grad_tokens = (d_mid + d_rows_norm).reshape(1, count, width)
    grad_qkv, grad_out, grad_down, grad_gain_attn, grad_gain_mlp = (
        lax.psum_scatter(qkv_term, ("ctx", "shard"), scatter_dimension=0, tiled=True),
        lax.psum_scatter(out_term, ("ctx", "shard"), scatter_dimension=0, tiled=True),
        lax.psum_scatter(down_term, ("ctx", "shard"), scatter_dimension=0, tiled=True),
        lax.psum_scatter(gain_one_term, ("ctx", "shard"), scatter_dimension=0, tiled=True),
        lax.psum_scatter(gain_two_term, ("ctx", "shard"), scatter_dimension=0, tiled=True),
    )
    return (
        mixed,
        grad_tokens,
        grad_qkv,
        grad_out,
        grad_gate_up,
        grad_down,
        grad_gain_attn,
        grad_gain_mlp,
        clip,
    )


def solution(mesh):
    placed = (
        P("shard", "ctx", None),
        P("shard", None),
        P("shard", "ctx", None),
        P(("ctx", "shard"), None),
        P(("ctx", "shard"), None),
        P(("ctx", "shard"), None),
        P(("ctx", "shard"), None),
        P(("ctx", "shard")),
        P(("ctx", "shard")),
    )
    return jax.shard_map(
        per_device,
        mesh=mesh,
        in_specs=placed,
        out_specs=(
            P("shard", "ctx", None),
            P("shard", "ctx", None),
            P(("ctx", "shard"), None),
            P(("ctx", "shard"), None),
            P(("ctx", "shard"), None),
            P(("ctx", "shard"), None),
            P(("ctx", "shard")),
            P(("ctx", "shard")),
            P(),
        ),
        check_vma=False,
    )
```

profile of v0, /device:TPU:0, one launch (start us, length us, event | category | flops | bytes accessed | tf_op | source)
XLA Modules:
  0.0 5832.7 jit_solution(2209792832073008658)
XLA Ops:
  9.7 42.8 all-reduce.6
  53.7 56.9 all-gather.7.cloned.1.call-done
  110.6 6.7 convolution_convert_fusion
  121.5 18.4 all-gather.9.cloned.1.call-done
  146.3 19.6 all-gather.11.cloned.1.call-done
  173.1 30.2 while.34
  178.0 4.7 fusion.143
  192.9 4.9 fusion.143
  205.5 40.6 all-gather.13.cloned.1.call-done
  246.1 5.0 multiply_reduce_fusion.3
  251.8 352.1 %all-gather.15.cloned.1.call-done = bf16[2048,16384]{1,0:T(8,128)(2,1)} async-done(((bf16[64,16384]{1,0:T(8,128)(2,1)}), bf16[2048,16384]{1,0:T(8,128)(2,1)}) %all-gather.15.cloned.1.call-update) | async-done | bytes 67108880 | tf_op jit(solution)/shard_map/all_gather | solution.py:176
  603.9 27.3 fusion.95
  631.1 168.5 %all-gather.17.cloned.1.call-done = bf16[8192,2048]{1,0:T(8,128)(2,1)} async-done(((bf16[256,2048]{1,0:T(8,128)(2,1)}), bf16[8192,2048]{1,0:T(8,128)(2,1)}) %all-gather.17.cloned.1.call-update) | async-done | bytes 33554448 | tf_op jit(solution)/shard_map/all_gather | solution.py:177
  799.6 21.6 multiply_convert_fusion.1
  821.2 30.5 multiply_reduce_fusion
  854.2 7.1 convolution_convert_fusion.1
  864.1 40.5 while.35
  877.1 4.6 fusion.159
  919.9 8.0 fusion.84
  929.3 17.3 reduce-scatter.22.cloned.1.call-done
  947.7 38.8 reduce-scatter.20.cloned.1.call-done
  987.5 11.5 fusion.82
  1000.0 25.0 fusion.78
  1025.1 46.4 fusion.59
  1072.3 43.8 pmax.7
  1116.7 16.7 fusion.64
  1133.4 9.2 fusion.76
  1142.6 44.1 all-reduce.5
  1189.1 166.2 %reduce-scatter.16.cloned.1.call-done = f32[64,2048]{1,0:T(8,128)} async-done(((f32[2048,2048]{1,0:T(8,128)}), f32[64,2048]{1,0:T(8,128)}) %reduce-scatter.16.cloned.1.call-update) | async-done | bytes 524304 | tf_op jit(solution)/shard_map/reduce_scatter | solution.py:248
  1355.3 250.2 %reduce-scatter.14.cloned.1.call-done = f32[64,3072]{1,0:T(8,128)} async-done(((f32[2048,3072]{1,0:T(8,128)}), f32[64,3072]{1,0:T(8,128)}) %reduce-scatter.14.cloned.1.call-update) | async-done | bytes 786448 | tf_op jit(solution)/shard_map/reduce_scatter | solution.py:247
  1605.6 1413.3 %reduce-scatter.18.cloned.1.call-done = f32[256,2048]{1,0:T(8,128)} async-done(((f32[8192,2048]{1,0:T(8,128)}), f32[256,2048]{1,0:T(8,128)}) %reduce-scatter.18.cloned.1.call-update) | async-done | bytes 2097168 | tf_op jit(solution)/shard_map/reduce_scatter | solution.py:249
  3018.9 2806.7 %reduce-scatter.24.cloned.1.call-done = f32[64,16384]{1,0:T(8,128)} async-done(((f32[2048,16384]{1,0:T(8,128)}), f32[64,16384]{1,0:T(8,128)}) %reduce-scatter.24.cloned.1.call-update) | async-done | bytes 4194320
  (169 shorter events, 109.2 us)
Async XLA Ops:
  7.2 103.4 %all-gather.7.cloned.1.call-start = ((), (), s32[]{:S(2)}) async-start(), calls=%async_computation.6 | async-start | bytes 12976128 | tf_op jit(solution)/shard_map/all_gather | solution.py:137
  7.9 132.0 %all-gather.9.cloned.1.call-start = ((), (), s32[]{:S(2)}) async-start(), calls=%async_computation.7 | async-start | bytes 1179648 | tf_op jit(solution)/shard_map/all_gather | solution.py:162
  52.5 64.8 %copy-start.15 = (f32[2048]{0:T(1024)}, f32[2048]{0:T(1024)S(1)}, u32[]{:S(2)}) copy-start(f32[2048]{0:T(1024)S(1)} %convert_element_type.105) | copy-start | bytes 24580
  53.7 63.6 %copy-start.18 = (f32[128]{0:T(128)}, f32[128]{0:T(128)S(1)}, u32[]{:S(2)}) copy-start(f32[128]{0:T(128)S(1)} %add_rsqrt_fusion.1) | copy-start | bytes 1540
  53.7 67.2 %copy-start.21 = (s32[1,9]{1,0:T(1,128)S(1)}, s32[1,9]{1,0:T(1,128)}, u32[]{:S(2)}) copy-start(s32[1,9]{1,0:T(1,128)} %param.14) | copy-start | bytes 112
  118.0 47.9 all-gather.11.cloned.1.call-start
  118.8 127.4 %all-gather.13.cloned.1.call-start = ((), (), s32[]{:S(2)}) async-start(), calls=%async_computation.9 | async-start | bytes 8650752 | tf_op jit(solution)/shard_map/all_gather | solution.py:138
  119.3 484.5 %all-gather.15.cloned.1.call-start = ((), (), s32[]{:S(2)}) async-start(), calls=%async_computation.10 | async-start | bytes 69206016 | tf_op jit(solution)/shard_map/all_gather | solution.py:176
  119.9 679.7 %all-gather.17.cloned.1.call-start = ((), (), s32[]{:S(2)}) async-start(), calls=%async_computation.11 | async-start | bytes 34603008 | tf_op jit(solution)/shard_map/all_gather | solution.py:177
  120.5 826.1 %reduce-scatter.22.cloned.1.call-start = ((), (), s32[]{:S(2)}) async-start(), calls=%async_computation.16 | async-start | bytes 1179648
  173.1 73.0 %copy-start.4 = (bf16[1,128,2048]{2,1,0:T(8,128)(2,1)S(1)}, bf16[1,128,2048]{2,1,0:T(8,128)(2,1)}, u32[]{:S(2)}) copy-start(bf16[1,128,2048]{2,1,0:T(8,128)(2,1)} %param.13) | copy-start | bytes 1572868
  178.0 5.9 copy-start
  192.9 6.1 copy-start
  603.9 195.8 %copy-start.10 = (bf16[1,128,2048]{2,1,0:T(8,128)(2,1)S(1)}, bf16[1,128,2048]{2,1,0:T(8,128)(2,1)}, u32[]{:S(2)}) copy-start(bf16[1,128,2048]{2,1,0:T(8,128)(2,1)} %param.15) | copy-start | bytes 1572868
  864.3 4.6 copy-start.12
  873.0 8.7 copy-start.2
  873.0 8.7 copy-start.13
  884.3 4.6 copy-start.12
  893.0 9.0 copy-start.2
  893.0 9.0 copy-start.13
  904.6 15.3 copy-start.7
  904.6 15.3 copy-start.9
  912.3 74.1 %reduce-scatter.20.cloned.1.call-start = ((), (), s32[]{:S(2)}) async-start(), calls=%async_computation.15 | async-start | bytes 1179648
  919.9 435.5 %reduce-scatter.16.cloned.1.call-start = ((), (), s32[]{:S(2)}) async-start(), calls=%async_computation.13 | async-start | bytes 17301504 | tf_op jit(solution)/shard_map/reduce_scatter | solution.py:248
  928.0 59.4 %copy-start.5 = (bf16[1,128,2048]{2,1,0:T(8,128)(2,1)S(1)}, bf16[1,128,2048]{2,1,0:T(8,128)(2,1)}, u32[]{:S(2)}) copy-start(bf16[1,128,2048]{2,1,0:T(8,128)(2,1)} %param.13) | copy-start | bytes 1572868
  928.0 59.5 %copy-start.16 = (f32[2048]{0:T(1024)S(1)}, f32[2048]{0:T(1024)}, u32[]{:S(2)}) copy-start(f32[2048]{0:T(1024)} %copy-done.15) | copy-start | bytes 24580
  928.0 59.5 %copy-start.19 = (f32[128]{0:T(128)S(1)}, f32[128]{0:T(128)}, u32[]{:S(2)}) copy-start(f32[128]{0:T(128)} %copy-done.18) | copy-start | bytes 1540
  928.0 677.5 %reduce-scatter.14.cloned.1.call-start = ((), (), s32[]{:S(2)}) async-start(), calls=%async_computation.12 | async-start | bytes 25952256 | tf_op jit(solution)/shard_map/reduce_scatter | solution.py:247
  999.0 2019.9 %reduce-scatter.18.cloned.1.call-start = ((), (), s32[]{:S(2)}) async-start(), calls=%async_computation.14 | async-start | bytes 69206016 | tf_op jit(solution)/shard_map/reduce_scatter | solution.py:249
  1025.1 4800.5 %reduce-scatter.24.cloned.1.call-start = ((), (), s32[]{:S(2)}) async-start(), calls=%async_computation.17 | async-start | bytes 138412032
  1133.4 9.2 copy-start.17
  1133.4 54.4 copy-start.8
  (8 other events, 12.5 us)
Sparse Core Ops, SparseCore 0:
  10.9 99.6 all-gather.6
  118.2 21.7 all-gather.8
  142.4 23.4 all-gather.10
  168.7 77.3 all-gather.12
  248.9 354.8 all-gather.14
  606.6 192.9 all-gather.16
  912.4 34.1 reduce-scatter.21
  950.4 35.9 reduce-scatter.19
  989.3 365.9 reduce-scatter.15
  1362.2 243.3 reduce-scatter.13
  1608.6 1410.2 reduce-scatter.17
  3021.8 2803.7 reduce-scatter.23
where the time goes:
time: 5840 us; the launch traced here: 5830 us
  waiting for transfers between devices  5350 us (92%)
  matrix products  264 us (5%)
  blocking collectives  131 us (2%)
    unnamed x15, waiting for transfers between devices  2870 us
    reduce_scatter x1, waiting for transfers between devices, per_device(): lax.psum_scatter(down_term, ('ctx', 'shard'), scatter_dimension=0, tiled=...  1410 us
    all_gather x1, waiting for transfers between devices, per_device(): lax.all_gather(w_gate_up, ('ctx', 'shard'), axis=0, tiled=True)  352 us
    reduce_scatter x1, waiting for transfers between devices, per_device(): lax.psum_scatter(qkv_term, ('ctx', 'shard'), scatter_dimension=0, tiled=T...  250 us
    all_gather x1, waiting for transfers between devices, per_device(): lax.all_gather(w_down, ('ctx', 'shard'), axis=0, tiled=True)  168 us
    reduce_scatter x1, waiting for transfers between devices, per_device(): lax.psum_scatter(out_term, ('ctx', 'shard'), scatter_dimension=0, tiled=T...  166 us
  transfers between devices with their start and end apart: 12, of which 12 were waited for; matrix products, arithmetic and copies ran while one was open for 4% of the time, Pallas kernels for 0%

commit v1 on v0

v1 whole, which is shorter than its diff:
```python
import functools
import math

import jax
import jax.numpy as jnp
from jax import lax
from jax.experimental import pallas as pl
from jax.experimental.pallas import tpu as pltpu
from jax.sharding import PartitionSpec as P

HEADS = 32
KV_HEADS = 8
HEAD_DIM = 64


SCALE = 0.015625
BRANCH = 0.22
EPSILON = 1e-05
CLIP_TARGET = 4.0
NEGATIVE = -1e30
MIB = 1024 * 1024
EVERY = ("ctx", "shard")


def segment_ids(positions, lengths_row):
    bounds = jnp.cumsum(lengths_row)[:-1]
    return jnp.sum((positions[:, None] >= bounds[None, :]).astype(jnp.int32), axis=1)


def rms_scale(rows):
    return lax.rsqrt(jnp.mean(rows * rows, axis=-1, keepdims=True) + EPSILON)


def norm_backward(d_normed, rows, scale, gain):
    unit = rows * scale
    d_unit = d_normed * gain
    gain_term = jnp.sum(d_normed * unit, axis=0)
    d_rows = scale * (d_unit - unit * jnp.mean(d_unit * unit, axis=-1, keepdims=True))
    return (d_rows, gain_term)


def dot(left, right, dims):
    return lax.dot_general(left, right, ((dims[0], dims[1]), ((), ())), preferred_element_type=jnp.float32)


def seen_mask(row0, rows, cols, q_seg, k_seg):
    q_pos = row0 + lax.broadcasted_iota(jnp.int32, (rows, cols), 0)
    k_pos = lax.broadcasted_iota(jnp.int32, (rows, cols), 1)
    return (k_pos <= q_pos) & ((k_seg == 0) | (k_seg == q_seg))


def attend_kernel(heads, block, q_ref, k_ref, v_ref, q_seg_ref, k_seg_ref, o_ref, lse_ref, top_ref):
    size = q_ref.shape[0]
    tops = [jnp.full((1, 1), NEGATIVE, jnp.float32)] * heads
    for i in range(size // block):
        rows, cols = pl.ds(i * block, block), (i + 1) * block
        live = seen_mask(i * block, block, cols, q_seg_ref[rows, :], k_seg_ref[:, :cols])
        keys, values = k_ref[:cols, :], v_ref[:cols, :]
        for h in range(heads):
            span = slice(h * HEAD_DIM, (h + 1) * HEAD_DIM)
            scores = dot(q_ref[rows, span], keys, ((1,), (1,))) * SCALE
            scores = jnp.where(live, scores, NEGATIVE)
            peak = jnp.max(scores, axis=-1, keepdims=True)
            weights = jnp.exp(scores - peak)
            total = jnp.sum(weights, axis=-1, keepdims=True)
            out = dot(weights.astype(jnp.bfloat16), values, ((1,), (0,)))
            o_ref[rows, span] = (out / total).astype(jnp.bfloat16)
            lse_ref[rows, h : h + 1] = peak + jnp.log(total)
            tops[h] = jnp.maximum(tops[h], jnp.max(peak, axis=0, keepdims=True))
    for h in range(heads):
        top_ref[:, h : h + 1] = tops[h]


def attend(queries, keys, values, q_seg, k_seg):
    size, width = queries.shape
    heads = width // HEAD_DIM
    return pl.pallas_call(
        functools.partial(attend_kernel, heads, math.gcd(size, 256)),
        out_shape=(
            jax.ShapeDtypeStruct((size, width), jnp.bfloat16),
            jax.ShapeDtypeStruct((size, heads), jnp.float32),
            jax.ShapeDtypeStruct((1, heads), jnp.float32),
        ),
        compiler_params=pltpu.CompilerParams(vmem_limit_bytes=48 * MIB),
    )(queries, keys, values, q_seg, k_seg)


def attend_back_kernel(
    heads, block, q_ref, k_ref, v_ref, o_ref, do_ref, lse_ref, q_seg_ref, k_seg_ref, dq_ref, dk_ref, dv_ref, dk_sum, dv_sum
):
    size = q_ref.shape[0]
    dk_sum[...] = jnp.zeros_like(dk_sum)
    dv_sum[...] = jnp.zeros_like(dv_sum)
    for i in range(size // block):
        rows, cols = pl.ds(i * block, block), (i + 1) * block
        live = seen_mask(i * block, block, cols, q_seg_ref[rows, :], k_seg_ref[:, :cols])
        keys, values = k_ref[:cols, :], v_ref[:cols, :]
        for h in range(heads):
            span = slice(h * HEAD_DIM, (h + 1) * HEAD_DIM)
            queries, d_out = q_ref[rows, span], do_ref[rows, span]
            delta = jnp.sum(d_out.astype(jnp.float32) * o_ref[rows, span].astype(jnp.float32), axis=-1, keepdims=True)
            scores = dot(queries, keys, ((1,), (1,))) * SCALE
            probs = jnp.where(live, jnp.exp(scores - lse_ref[rows, h : h + 1]), 0.0)
            d_probs = dot(d_out, values, ((1,), (1,)))
            d_scores = (probs * (d_probs - delta)).astype(jnp.bfloat16)
            dq_ref[rows, span] = (dot(d_scores, keys, ((1,), (0,))) * SCALE).astype(jnp.bfloat16)
            dk_sum[:cols, :] += dot(d_scores, queries, ((0,), (0,)))
            dv_sum[:cols, :] += dot(probs.astype(jnp.bfloat16), d_out, ((0,), (0,)))
    dk_ref[...] = (dk_sum[...] * SCALE).astype(jnp.bfloat16)
    dv_ref[...] = dv_sum[...].astype(jnp.bfloat16)


def attend_back(queries, keys, values, out, d_out, lse, q_seg, k_seg):
    size, width = queries.shape
    heads = width // HEAD_DIM
    like_kv = jax.ShapeDtypeStruct((size, HEAD_DIM), jnp.bfloat16)
    return pl.pallas_call(
        functools.partial(attend_back_kernel, heads, math.gcd(size, 256)),
        out_shape=(jax.ShapeDtypeStruct((size, width), jnp.bfloat16), like_kv, like_kv),
        scratch_shapes=[pltpu.VMEM((size, HEAD_DIM), jnp.float32)] * 2,
        compiler_params=pltpu.CompilerParams(vmem_limit_bytes=48 * MIB),
    )(queries, keys, values, out, d_out, lse, q_seg, k_seg)


def split_heads(w, parts):
    rows = w.shape[0]
    q_width, kv_width = HEADS * HEAD_DIM, KV_HEADS * HEAD_DIM
    copies = max(1, parts // KV_HEADS)
    q = w[:, :q_width].reshape(rows, parts, q_width // parts)
    k = w[:, q_width : q_width + kv_width].reshape(rows, parts // copies, 1, -1)
    v = w[:, q_width + kv_width :].reshape(rows, parts // copies, 1, -1)
    k, v = (jnp.broadcast_to(a, (rows, parts // copies, copies, a.shape[3])).reshape(rows, parts, -1) for a in (k, v))
    return jnp.concatenate([q, k, v], axis=2)


def join_heads(grads, parts):
    rows = grads.shape[0]
    copies = max(1, parts // KV_HEADS)
    q_part = HEADS * HEAD_DIM // parts
    kv_part = (grads.shape[2] - q_part) // 2
    q = grads[:, :, :q_part].reshape(rows, -1)
    k, v = (
        jnp.sum(grads[:, :, at : at + kv_part].reshape(rows, parts // copies, copies, kv_part), axis=2).reshape(rows, -1)
        for at in (q_part, q_part + kv_part)
    )
    return jnp.concatenate([q, k, v], axis=1)


def per_device(n_ctx, n_shard, tokens, lengths, cotangent, w_qkv, w_out, w_gate_up, w_down, gain_attn, gain_mlp):
    count, width = tokens.shape[1:]
    n = n_ctx * n_shard
    w_rows = w_qkv.shape[0]
    ff_part = w_down.shape[0]
    q_part = HEADS * HEAD_DIM // n_ctx
    rows = tokens.reshape(count, width).astype(jnp.float32)
    grad_rows = cotangent.reshape(count, width).astype(jnp.float32)
    size = count * n_ctx
    positions = jnp.arange(size, dtype=jnp.int32)
    seg = segment_ids(positions, lengths[0])
    q_seg, k_seg = seg.reshape(size, 1), seg.reshape(1, size)

    gains = lax.all_gather(jnp.stack([gain_attn, gain_mlp]), EVERY, axis=1, tiled=True).astype(jnp.float32)
    gain_one, gain_two = gains[0], gains[1]

    qkv_cols = lax.all_to_all(split_heads(w_qkv, n_ctx), "ctx", split_axis=1, concat_axis=1, tiled=True)
    qkv_cols = qkv_cols.reshape(w_rows, n_ctx, -1).transpose(1, 0, 2)
    qkv_mine = lax.all_gather(qkv_cols, "shard", axis=1, tiled=True).reshape(width, -1)
    out_mine = lax.all_gather(w_out, "shard", axis=0, tiled=True)
    gate_up_mine = lax.all_to_all(w_gate_up.reshape(w_rows, 2, n, ff_part), EVERY, split_axis=2, concat_axis=0, tiled=True)
    gate_up_mine = gate_up_mine.reshape(width, 2 * ff_part)

    scale_one = rms_scale(rows)
    normed_one = lax.all_gather((rows * scale_one * gain_one).astype(jnp.bfloat16), "ctx", axis=0, tiled=True)
    projected = dot(normed_one, qkv_mine, ((1,), (0,))).astype(jnp.bfloat16)
    kv_part = (projected.shape[1] - q_part) // 2
    queries, keys, values = (
        projected[:, :q_part],
        projected[:, q_part : q_part + kv_part],
        projected[:, q_part + kv_part :],
    )
    attn_out, lse, tops = attend(queries, keys, values, q_seg, k_seg)
    out_term = dot(attn_out, out_mine, ((1,), (0,))).astype(jnp.bfloat16)
    attn_proj = lax.psum_scatter(out_term, "ctx", scatter_dimension=0, tiled=True)
    mid = rows + BRANCH * attn_proj.astype(jnp.float32)
    head_top = lax.all_gather(lax.pmax(tops, "shard"), "ctx", axis=1, tiled=True).reshape(HEADS)
    clip = CLIP_TARGET / jnp.maximum(head_top, CLIP_TARGET)

    scale_two = rms_scale(mid)
    d_mlp = lax.all_gather((BRANCH * grad_rows).astype(jnp.bfloat16), EVERY, axis=0, tiled=True)
    normed_two = lax.all_gather((mid * scale_two * gain_two).astype(jnp.bfloat16), EVERY, axis=0, tiled=True)
    gate_up = dot(normed_two, gate_up_mine, ((1,), (0,)))
    gate, up = gate_up[:, :ff_part], gate_up[:, ff_part:]
    sigma = jax.nn.sigmoid(gate)
    active = gate * sigma
    hidden = (active * up).astype(jnp.bfloat16)
    down_term = dot(hidden, w_down, ((1,), (0,))).astype(jnp.bfloat16)
    d_hidden = dot(d_mlp, w_down, ((1,), (1,)))
    d_gate = d_hidden * up * sigma * (1.0 + gate * (1.0 - sigma))
    d_up = d_hidden * active
    d_gate_up = jnp.concatenate([d_gate, d_up], axis=1).astype(jnp.bfloat16)
    normed_term = dot(d_gate_up, gate_up_mine, ((1,), (1,))).astype(jnp.bfloat16)
    grad_down = dot(hidden, d_mlp, ((0,), (0,)))
    gate_up_grad = dot(normed_two, d_gate_up, ((0,), (0,))).astype(jnp.bfloat16)
    mlp_proj = lax.psum_scatter(down_term, EVERY, scatter_dimension=0, tiled=True)
    mixed = (mid + BRANCH * mlp_proj.astype(jnp.float32)).astype(jnp.bfloat16).reshape(1, count, width)
    d_normed_two = lax.psum_scatter(normed_term, EVERY, scatter_dimension=0, tiled=True).astype(jnp.float32)
    grad_gate_up = lax.all_to_all(gate_up_grad.reshape(n * w_rows, 2, 1, ff_part), EVERY, split_axis=0, concat_axis=2, tiled=True)
    grad_gate_up = grad_gate_up.reshape(w_rows, 2 * n * ff_part).astype(jnp.float32)
    d_mid_norm, gain_two_term = norm_backward(d_normed_two, mid, scale_two, gain_two)
    d_mid = grad_rows + d_mid_norm

    d_attn = lax.all_gather((BRANCH * d_mid).astype(jnp.bfloat16), "ctx", axis=0, tiled=True)
    grad_out = lax.psum_scatter(dot(attn_out, d_attn, ((0,), (0,))), "shard", scatter_dimension=0, tiled=True)
    d_heads = dot(d_attn, out_mine, ((1,), (1,))).astype(jnp.bfloat16)
    d_q, d_k, d_v = attend_back(queries, keys, values, attn_out, d_heads, lse, q_seg, k_seg)
    d_qkv = jnp.concatenate([d_q, d_k, d_v], axis=1)
    qkv_term = dot(d_qkv, qkv_mine, ((1,), (1,))).astype(jnp.bfloat16)
    d_normed_one = lax.psum_scatter(qkv_term, "ctx", scatter_dimension=0, tiled=True).astype(jnp.float32)
    qkv_grad = dot(normed_one, d_qkv, ((0,), (0,))).reshape(n_ctx, n_shard * w_rows, -1)
    qkv_grad = lax.psum_scatter(qkv_grad, "shard", scatter_dimension=1, tiled=True)
    qkv_grad = lax.all_to_all(qkv_grad, "ctx", split_axis=0, concat_axis=0, tiled=True)
    grad_qkv = join_heads(qkv_grad.transpose(1, 0, 2), n_ctx)
    d_rows_norm, gain_one_term = norm_backward(d_normed_one, rows, scale_one, gain_one)
    grad_tokens = (d_mid + d_rows_norm).reshape(1, count, width)
    gain_terms = lax.psum_scatter(jnp.stack([gain_one_term, gain_two_term]), EVERY, scatter_dimension=1, tiled=True)
    return (mixed, grad_tokens, grad_qkv, grad_out, grad_gate_up, grad_down, gain_terms[0], gain_terms[1], clip)


def solution(mesh):
    by_token, by_row = P("shard", "ctx", None), P(EVERY, None)
    return jax.shard_map(
        functools.partial(per_device, mesh.shape["ctx"], mesh.shape["shard"]),
        mesh=mesh,
        in_specs=(by_token, P("shard", None), by_token, by_row, by_row, by_row, by_row, P(EVERY), P(EVERY)),
        out_specs=(by_token, by_token, by_row, by_row, by_row, by_row, P(EVERY), P(EVERY), P()),
        check_vma=False,
    )
```

time: 5840 us -> 1640 us (0.28)
  waiting for transfers between devices: 5350 us -> 1210 us
  matrix products: 264 us -> 116 us
    unnamed x15 -> x14, waiting for transfers between devices: 2870 us -> 133 us
    reduce_scatter x3 -> x6, waiting for transfers between devices: 1830 us -> 848 us  [the longest x1 365 us: per_device(): lax.psum_scatter(down_term, EVERY, scatter_dimension=0, tiled=True)]
    all_gather x6, waiting for transfers between devices: 656 us -> 228 us  [the longest x1 102 us: per_device(): lax.all_gather((BRANCH * grad_rows).astype(jnp.bfloat16), EVERY, axis=0,...]
    dot_general x26 -> x12, matrix products: 264 us -> 116 us  [dot(): lax.dot_general(left, right, ((dims[0], dims[1]), ((), ())), preferred_el...]
    all_to_all x0 -> x2, blocking collectives: none -> 97.4 us  [the longest x1 84.1 us: per_device(): lax.all_to_all(w_gate_up.reshape(w_rows, 2, n, ff_part), EVERY, split_axi...]
    unnamed x2 -> x1, blocking collectives: 86.8 us -> 12.5 us
    all_gather x0 -> x1, blocking collectives: none -> 66.4 us  [per_device(): lax.all_gather(jnp.stack([gain_attn, gain_mlp]), EVERY, axis=1, tiled=True)]
  transfers between devices with their start and end apart: 12 -> 15, of which waited for: 12 -> 13; matrix products, arithmetic and copies ran while one was open for 4% -> 7% of each run, Pallas kernels for 0% -> 0%
where the time goes in v1:
time: 1640 us; the launch traced here: 1630 us
  waiting for transfers between devices  1210 us (74%)
  blocking collectives  188 us (11%)
  matrix products  116 us (7%)
  local copies, waits for them, and re-layouts  41.3 us (3%)
  starting transfers between devices  18.7 us (1%)
  other arithmetic  18.7 us (1%)
  Pallas kernels  17.4 us (1%)
    reduce_scatter x1, waiting for transfers between devices, per_device(): lax.psum_scatter(down_term, EVERY, scatter_dimension=0, tiled=True)  365 us
    reduce_scatter x1, waiting for transfers between devices, per_device(): lax.psum_scatter(normed_term, EVERY, scatter_dimension=0, tiled=True)  362 us
    unnamed x14, waiting for transfers between devices  133 us
    dot_general x12, matrix products, dot(): lax.dot_general(left, right, ((dims[0], dims[1]), ((), ())), preferred_el...  116 us
    all_gather x1, waiting for transfers between devices, per_device(): lax.all_gather((BRANCH * grad_rows).astype(jnp.bfloat16), EVERY, axis=0,...  102 us
    all_to_all x1, blocking collectives, per_device(): lax.all_to_all(w_gate_up.reshape(w_rows, 2, n, ff_part), EVERY, split_axi...  84.1 us
    all_gather x1, blocking collectives, per_device(): lax.all_gather(jnp.stack([gain_attn, gain_mlp]), EVERY, axis=1, tiled=True)  66.4 us
    all_gather x1, waiting for transfers between devices, per_device(): lax.all_gather((mid * scale_two * gain_two).astype(jnp.bfloat16), EVERY,...  53.7 us
  transfers between devices with their start and end apart: 15, of which 13 were waited for; matrix products, arithmetic and copies ran while one was open for 7% of the time, Pallas kernels for 0%

profile of v1, /device:TPU:0, one launch (start us, length us, event | category | flops | bytes accessed | tf_op | source)
XLA Modules:
  0.0 1630.1 jit_solution(12235758635182772366)
XLA Ops:
  9.7 13.3 all_to_all.34
  24.1 66.4 %all-gather = bf16[32,64,2]{1,2,0:T(2,128)(2,1)S(1)} all-gather(bf16[1,64,2]{1,2,0:T(2,128)(2,1)S(1)} %maximum_bitcast_fusion), channel_id=1, replica_groups=mesh['ctx'=8,'shard'=4] {'ctx','shard'}, dimensions={0}, use_global_device_ids=true | all-gather | bytes 8448 | tf_op jit(solution)/shard_map/all_gather | solution.py:162
  96.0 29.8 %all-gather.8.cloned.1.call-done = bf16[1024,2048]{1,0:T(8,128)(2,1)} async-done(((bf16[128,2048]{1,0:T(8,128)(2,1)}), bf16[1024,2048]{1,0:T(8,128)(2,1)}) %all-gather.8.cloned.1.call-update) | async-done | bytes 4194320 | tf_op jit(solution)/shard_map/all_gather | solution.py:173
  125.8 5.0 convolution_convert_fusion.5
  131.0 6.9 shard_map.160
  138.7 16.6 %all-gather.12.cloned.1.call-done = bf16[256,2048]{1,0:T(8,128)(2,1)} async-done(((bf16[64,2048]{1,0:T(8,128)(2,1)}), bf16[256,2048]{1,0:T(8,128)(2,1)}) %all-gather.12.cloned.1.call-update) | async-done | bytes 1048592 | tf_op jit(solution)/shard_map/all_gather | solution.py:168
  159.9 50.9 %reduce-scatter.10.cloned.1.call-done = bf16[128,2048]{1,0:T(8,128)(2,1)} async-done(((bf16[1024,2048]{1,0:T(8,128)(2,1)}), bf16[128,2048]{1,0:T(8,128)(2,1)}) %reduce-scatter.10.cloned.1.call-update) | async-done | bytes 524304 | tf_op jit(solution)/shard_map/reduce_scatter | solution.py:183
  221.2 84.1 %all_to_all.35 = bf16[64,2,32,256]{3,1,0,2:T(2,128)(2,1)S(1)} all-to-all(bf16[64,2,32,256]{3,1,0,2:T(2,128)(2,1)S(1)} %copy.77), channel_id=1, replica_groups=mesh['ctx'=8,'shard'=4] {'ctx','shard'}, dimensions={2} | all-to-all | bytes 4194304 | tf_op jit(solution)/shard_map/all_to_all | solution.py:169
  307.1 53.7 %all-gather.14.cloned.1.call-done = bf16[4096,2048]{1,0:T(8,128)(2,1)} async-done(((bf16[128,2048]{1,0:T(8,128)(2,1)}), bf16[4096,2048]{1,0:T(8,128)(2,1)}) %all-gather.14.cloned.1.call-update) | async-done | bytes 16777232 | tf_op jit(solution)/shard_map/all_gather | solution.py:190
  360.8 15.2 fusion.30
  376.0 101.7 %all-gather.16.cloned.1.call-done = bf16[4096,2048]{1,0:T(8,128)(2,1)} async-done(((bf16[128,2048]{1,0:T(8,128)(2,1)}), bf16[4096,2048]{1,0:T(8,128)(2,1)}) %all-gather.16.cloned.1.call-update) | async-done | bytes 16777232 | tf_op jit(solution)/shard_map/all_gather | solution.py:189
  477.8 20.5 %multiply_convert_fusion.1 = (bf16[4096,256]{0,1:T(8,128)(2,1)S(1)}, bf16[4096,256]{0,1:T(8,128)(2,1)}, bf16[4096,256]{0,1:T(8,128)(2,1)}) fusion(f32[4096,512]{0,1:T(8,128)} %fusion.30, bf16[4096,2048]{1,0:T(8,128)(2,1)} %all-gather.16.cloned.1.call-done, bf16[256,2048]{1,0:T(8,128)(2,1)S(1)} %copy-done), kind=kOutput, calls=%fused_computation.5 | convolution fusion | flops 4310695936 | bytes 32505856 | tf_op jit(solution)/shard_map/dot_general | solution.py:43
  499.6 14.1 convolution_convert_fusion
  513.7 362.5 %reduce-scatter.14.cloned.1.call-done = bf16[128,2048]{1,0:T(8,128)(2,1)} async-done(((bf16[4096,2048]{1,0:T(8,128)(2,1)}), bf16[128,2048]{1,0:T(8,128)(2,1)}) %reduce-scatter.14.cloned.1.call-update) | async-done | bytes 524304 | tf_op jit(solution)/shard_map/reduce_scatter | solution.py:206
  880.9 8.8 reduce-scatter.16.cloned.1.call-start
  889.7 26.0 %all-gather.18.cloned.1.call-done = bf16[1024,2048]{1,0:T(8,128)(2,1)} async-done(((bf16[128,2048]{1,0:T(8,128)(2,1)}), bf16[1024,2048]{1,0:T(8,128)(2,1)}) %all-gather.18.cloned.1.call-update) | async-done | bytes 4194320 | tf_op jit(solution)/shard_map/all_gather | solution.py:212
  919.7 10.5 shard_map.161
  936.8 6.3 fusion.20
  943.2 10.1 convolution_convert_fusion.1
  953.2 14.6 convolution_convert_fusion.4
  967.8 6.2 copy.82
  974.0 4.9 all-to-all-start.3
  979.0 24.0 %reduce-scatter.16.cloned.1.call-done = bf16[128,2048]{1,0:T(8,128)(2,1)} async-done(((bf16[1024,2048]{1,0:T(8,128)(2,1)}), bf16[128,2048]{1,0:T(8,128)(2,1)}) %reduce-scatter.16.cloned.1.call-update) | async-done | bytes 524304 | tf_op jit(solution)/shard_map/reduce_scatter | solution.py:218
  1012.1 11.8 pmax.7
  1024.1 12.5 all-reduce
  1037.1 12.3 fusion.32
  1049.4 5.4 all-to-all-done.3
  1061.6 5.1 reshape.131
  1066.7 8.8 reduce-scatter.18.cloned.1.call-done
  1079.7 364.5 %reduce-scatter.12.cloned.1.call-done = bf16[128,2048]{1,0:T(8,128)(2,1)} async-done(((bf16[4096,2048]{1,0:T(8,128)(2,1)}), bf16[128,2048]{1,0:T(8,128)(2,1)}) %reduce-scatter.12.cloned.1.call-update) | async-done | bytes 524304 | tf_op jit(solution)/shard_map/reduce_scatter | solution.py:204
  1447.5 132.1 %reduce-scatter.22.cloned.1.call-done = f32[64,2]{1,0:T(8,128)} async-done(((f32[2048,2]{1,0:T(8,128)}), f32[64,2]{1,0:T(8,128)}) %reduce-scatter.22.cloned.1.call-update) | async-done | bytes 528
  1585.5 37.6 %reduce-scatter.20.cloned.1.call-done = f32[64,2048]{1,0:T(8,128)} async-done(((f32[256,2048]{1,0:T(8,128)}), f32[64,2048]{1,0:T(8,128)}) %reduce-scatter.20.cloned.1.call-update) | async-done | bytes 524304 | tf_op jit(solution)/shard_map/reduce_scatter | solution.py:213
  (125 shorter events, 72.5 us)
Async XLA Ops:
  7.2 470.6 %copy-start = (bf16[256,2048]{1,0:T(8,128)(2,1)S(1)}, bf16[256,2048]{1,0:T(8,128)(2,1)}, u32[]{:S(2)}) copy-start(bf16[256,2048]{1,0:T(8,128)(2,1)} %param.15) | copy-start | bytes 3145732
  7.2 16.9 %copy-start.14 = (bf16[64]{0:T(256)(128)(2,1)S(1)}, bf16[64]{0:T(256)(128)(2,1)}, u32[]{:S(2)}) copy-start(bf16[64]{0:T(256)(128)(2,1)} %param.17) | copy-start | bytes 388
  7.2 16.9 %copy-start.15 = (bf16[64]{0:T(256)(128)(2,1)S(1)}, bf16[64]{0:T(256)(128)(2,1)}, u32[]{:S(2)}) copy-start(bf16[64]{0:T(256)(128)(2,1)} %param.16) | copy-start | bytes 388
  7.2 83.4 %copy-start.7 = (bf16[1,128,2048]{2,1,0:T(8,128)(2,1)S(1)}, bf16[1,128,2048]{2,1,0:T(8,128)(2,1)}, u32[]{:S(2)}) copy-start(bf16[1,128,2048]{2,1,0:T(8,128)(2,1)} %param.9) | copy-start | bytes 1572868
  7.2 85.4 %copy-start.16 = (s32[1,9]{1,0:T(1,128)S(1)}, s32[1,9]{1,0:T(1,128)}, u32[]{:S(2)}) copy-start(s32[1,9]{1,0:T(1,128)} %param.10) | copy-start | bytes 112
  7.2 86.0 %all-gather.10.cloned.1.call-start = ((), (), s32[]{:S(2)}) async-start(), calls=%async_computation.12 | async-start | bytes 1966080 | tf_op jit(solution)/shard_map/all_gather | solution.py:167
  24.1 101.7 %all-gather.8.cloned.1.call-start = ((), (), s32[]{:S(2)}) async-start(), calls=%async_computation.11 | async-start | bytes 4718592 | tf_op jit(solution)/shard_map/all_gather | solution.py:173
  91.9 63.4 %all-gather.12.cloned.1.call-start = ((), (), s32[]{:S(2)}) async-start(), calls=%async_computation.13 | async-start | bytes 1310720 | tf_op jit(solution)/shard_map/all_gather | solution.py:168
  92.6 118.2 %reduce-scatter.10.cloned.1.call-start = ((), (), s32[]{:S(2)}) async-start(), calls=%async_computation.14 | async-start | bytes 4718592 | tf_op jit(solution)/shard_map/reduce_scatter | solution.py:183
  159.8 201.0 %all-gather.14.cloned.1.call-start = ((), (), s32[]{:S(2)}) async-start(), calls=%async_computation.15 | async-start | bytes 17301504 | tf_op jit(solution)/shard_map/all_gather | solution.py:190
  214.6 263.2 %all-gather.16.cloned.1.call-start = ((), (), s32[]{:S(2)}) async-start(), calls=%async_computation.17 | async-start | bytes 17301504 | tf_op jit(solution)/shard_map/all_gather | solution.py:189
  216.8 659.3 %reduce-scatter.14.cloned.1.call-start = ((), (), s32[]{:S(2)}) async-start(), calls=%async_computation.18 | async-start | bytes 17301504 | tf_op jit(solution)/shard_map/reduce_scatter | solution.py:206
  477.8 21.8 %copy-start.12 = (bf16[256,8,2,256]{3,1,2,0:T(8,128)(2,1)S(1)}, bf16[256,8,2,256]{3,1,2,0:T(8,128)(2,1)}, u32[]{:S(2)}) copy-start(bf16[256,8,2,256]{3,1,2,0:T(8,128)(2,1)} %copy.93) | copy-start | bytes 6291460
  498.3 1.3 copy-start.18
  513.7 402.1 %all-gather.18.cloned.1.call-start = ((), (), s32[]{:S(2)}) async-start(), calls=%async_computation.19 | async-start | bytes 4718592 | tf_op jit(solution)/shard_map/all_gather | solution.py:212
  880.9 122.1 %reduce-scatter.16.cloned.1.call-start = ((), (), s32[]{:S(2)}) async-start(), calls=%async_computation.20 | async-start | bytes 4718592 | tf_op jit(solution)/shard_map/reduce_scatter | solution.py:218
  915.8 3.9 copy-start.2
  915.8 15.3 copy-start.13
  930.2 0.9 copy-start.5
  935.7 1.0 copy-start.4
  935.7 1.1 copy-start.6
  935.7 139.7 %reduce-scatter.18.cloned.1.call-start = ((), (), s32[]{:S(2)}) async-start(), calls=%async_computation.21 | async-start | bytes 3932160 | tf_op jit(solution)/shard_map/reduce_scatter | solution.py:220
  943.1 501.1 %reduce-scatter.12.cloned.1.call-start = ((), (), s32[]{:S(2)}) async-start(), calls=%async_computation.16 | async-start | bytes 17301504 | tf_op jit(solution)/shard_map/reduce_scatter | solution.py:204
  967.8 35.2 %copy-start.8 = (bf16[1,128,2048]{2,1,0:T(8,128)(2,1)S(1)}, bf16[1,128,2048]{2,1,0:T(8,128)(2,1)}, u32[]{:S(2)}) copy-start(bf16[1,128,2048]{2,1,0:T(8,128)(2,1)} %param.9) | copy-start | bytes 1572868
  974.0 80.7 %all-to-all-start.3 = ((bf16[2048,2,1,256]{3,1,2,0:T(2,128)(2,1)}), bf16[2048,2,1,256]{3,1,2,0:T(2,128)(2,1)}, u32[]{:S(2)}, u32[]{:S(2)}) async-start(bf16[2048,2,1,256]{3,1,2,0:T(2,128)(2,1)} %copy.82), calls=%async_computation.9 | async-start | bytes 4194304 | tf_op jit(solution)/shard_map/all_to_all | solution.py:207
  979.0 600.7 %reduce-scatter.22.cloned.1.call-start = ((), (), s32[]{:S(2)}) async-start(), calls=%async_computation.23 | async-start | bytes 1081344
  1006.0 4.9 copy-start.17
  1006.0 617.1 %reduce-scatter.20.cloned.1.call-start = ((), (), s32[]{:S(2)}) async-start(), calls=%async_computation.22 | async-start | bytes 2621440 | tf_op jit(solution)/shard_map/reduce_scatter | solution.py:213
  1061.6 382.7 %copy-start.9 = (bf16[128,2048]{1,0:T(8,128)(2,1)S(1)}, bf16[128,2048]{1,0:T(8,128)(2,1)}, u32[]{:S(2)}) copy-start(bf16[128,2048]{1,0:T(8,128)(2,1)} %reduce-scatter.10.cloned.1.call-done) | copy-start | bytes 1572868
  1061.6 382.7 %copy-start.10 = (bf16[1,128,2048]{2,1,0:T(8,128)(2,1)S(1)}, bf16[1,128,2048]{2,1,0:T(8,128)(2,1)}, u32[]{:S(2)}) copy-start(bf16[1,128,2048]{2,1,0:T(8,128)(2,1)} %param.11) | copy-start | bytes 1572868
  1061.6 382.7 %copy-start.11 = (bf16[128,2048]{1,0:T(8,128)(2,1)S(1)}, bf16[128,2048]{1,0:T(8,128)(2,1)}, u32[]{:S(2)}) copy-start(bf16[128,2048]{1,0:T(8,128)(2,1)} %reduce-scatter.14.cloned.1.call-done) | copy-start | bytes 1572868
  1075.5 506.2 %all-to-all-start.2 = ((f32[8,64,384]{2,1,0:T(8,128)}), f32[8,64,384]{2,1,0:T(8,128)}, u32[]{:S(2)}, u32[]{:S(2)}) async-start(f32[8,64,384]{2,1,0:T(8,128)} %reduce-scatter.18.cloned.1.call-done), calls=%async_computation.7 | async-start | bytes 1572864 | tf_op jit(solution)/shard_map/all_to_all | solution.py:221
  (2 other events, 1.6 us)
Sparse Core Ops, SparseCore 0:
  24.2 36.6 all-gather.9
  92.0 33.7 all-gather.7
  127.4 27.9 all-gather.11
  160.0 50.8 reduce-scatter.9
  214.7 146.0 all-gather.13
  364.7 113.0 all-gather.15
  513.8 362.3 reduce-scatter.13
  881.0 34.6 all-gather.17
  935.9 67.1 reduce-scatter.15
  1005.2 70.2 reduce-scatter.17
  1077.8 366.4 reduce-scatter.11
  1446.3 133.2 reduce-scatter.21
  1582.6 40.4 reduce-scatter.19

commit v2 on v1

--- a/solution.py
+++ b/solution.py
@@ -122,6 +122,434 @@
     )(queries, keys, values, out, d_out, lse, q_seg, k_seg)
 
 
+def remote(src, dst, send_sem, recv_sem, device):
+    return pltpu.make_async_remote_copy(
+        src_ref=src, dst_ref=dst, send_sem=send_sem, recv_sem=recv_sem, device_id=device, device_id_type=pl.DeviceIdType.MESH
+    )
+
+
+def greet(devices, extra):
+    barrier = pltpu.get_barrier_semaphore()
+    count = len(devices)
+    for device in devices:
+        pl.semaphore_signal(barrier, inc=1, device_id=device, device_id_type=pl.DeviceIdType.MESH)
+    for condition, device in extra:
+
+        @pl.when(condition)
+        def _():
+            pl.semaphore_signal(barrier, inc=1, device_id=device, device_id_type=pl.DeviceIdType.MESH)
+
+        count = count + condition.astype(jnp.int32)
+    pl.semaphore_wait(barrier, count)
+
+
+def add_rows(target, sources, rows, keep=None, step=32):
+    @pl.loop(0, rows // step)
+    def _(i):
+        part = pl.ds(pl.multiple_of(i * step, step), step)
+        total = target[part, :].astype(jnp.float32)
+        for source in sources:
+            total = total + source[part, :].astype(jnp.float32)
+        if keep is None:
+            target[part, :] = total.astype(jnp.bfloat16)
+        else:
+            keep[part, :] = total
+
+
+def mlp_kernel(
+    line, blk, part, normed_ref, d_mlp_ref, gate_up_ref, down_ref,
+    mlp_ref, d_normed_ref, gate_up_grad_ref, down_grad_ref,
+    act, land, line_land, w_gu, w_down, acc_gu, acc_down, hid, d_gu, sib_gu, sib_down,
+    z_send, z_recv, p_send, p_recv, f_send, f_recv, r2_send, r2_recv, r3_send, r3_recv, r4_send, r4_recv,
+    w_send, w_recv, g_send, g_recv, own_sem, out_sem,
+):
+    c, z = lax.axis_index("ctx"), lax.axis_index("shard")
+    q, core = c // 2, c % 2
+    half = blk // 2
+    width = w_down.shape[1]
+    slot_rows = 4 * blk
+    cx, cy, sibling = (c + 2 - 4 * (q % 2), z), (c + 4 - 8 * (q // 2), z), (c + 1 - 2 * core, z)
+    qx, qy = q + 1 - 2 * (q % 2), q + 2 - 4 * (q // 2)
+    qd = 3 - q
+    up, down = (c, z + 1), (c, z - 1)
+    has_up, has_down = z < line - 1, z > 0
+
+    def source(k):
+        if line == 1:
+            return z * 0
+        mirrored = z >= line // 2
+        near = jnp.where(mirrored, line - 1 - z, z)
+        turn = (k + 1) // 2
+        both = near - turn if k % 2 == 1 else near + turn
+        at = jnp.where(k <= 2 * near, both, k)
+        return jnp.where(mirrored, line - 1 - at, at)
+
+    def block(at, chip):
+        return pl.multiple_of((at * 4 + chip) * blk, blk)
+
+    def rows(tensor, at, chip, first=0, count=blk):
+        return act.at[tensor, pl.ds(pl.multiple_of(block(at, chip) + first, half), count), :]
+
+    greet([cx, cy, sibling], [(has_up, up), (has_down, down)])
+
+    own = [
+        pltpu.make_async_copy(normed_ref, rows(0, z, q), own_sem.at[0]),
+        pltpu.make_async_copy(d_mlp_ref, rows(1, z, q), own_sem.at[1]),
+    ]
+    mine = [pl.ds(pl.multiple_of(core * part + extra, part), part) for extra in (0, 2 * part)]
+    own_weights = [
+        pltpu.make_async_copy(gate_up_ref.at[:, :part], w_gu.at[:, mine[0]], own_sem.at[2]),
+        pltpu.make_async_copy(gate_up_ref.at[:, part:], w_gu.at[:, mine[1]], own_sem.at[3]),
+        pltpu.make_async_copy(down_ref, w_down.at[mine[0], :], own_sem.at[4]),
+    ]
+    to_sibling = [
+        remote(gate_up_ref.at[:, :part], w_gu.at[:, mine[0]], w_send.at[0], w_recv.at[0], sibling),
+        remote(gate_up_ref.at[:, part:], w_gu.at[:, mine[1]], w_send.at[1], w_recv.at[1], sibling),
+        remote(down_ref, w_down.at[mine[0], :], w_send.at[2], w_recv.at[2], sibling),
+    ]
+    theirs = [pl.ds(pl.multiple_of((1 - core) * part + extra, part), part) for extra in (0, 2 * part)]
+    from_sibling = [
+        remote(gate_up_ref.at[:, :part], w_gu.at[:, theirs[0]], w_send.at[0], w_recv.at[0], sibling),
+        remote(gate_up_ref.at[:, part:], w_gu.at[:, theirs[1]], w_send.at[1], w_recv.at[1], sibling),
+        remote(down_ref, w_down.at[theirs[0], :], w_send.at[2], w_recv.at[2], sibling),
+    ]
+
+    def line_copy(tensor, at, way):
+        ref = rows(tensor, at, q)
+        return remote(ref, ref, z_send.at[tensor, at, way], z_recv.at[tensor, at], (up, down)[way])
+
+    def plane_copies(tensor, at):
+        copies = []
+        for i, (device, first) in enumerate(((cx, 0), (cy, half), (cx, half), (cy, 0))):
+            ref = rows(tensor, at, q, first, half)
+            copies.append(remote(ref, ref, p_send.at[tensor, at, i], p_recv.at[tensor, at, i], device))
+        return copies
+
+    def plane_arrivals(tensor, at):
+        arrivals = []
+        for i, (device, chip, first) in enumerate(((cx, qx, 0), (cy, qy, half), (cx, qx, half), (cy, qy, 0))):
+            ref = rows(tensor, at, chip, first, half)
+            arrivals.append(remote(ref, ref, p_send.at[tensor, at, i], p_recv.at[tensor, at, i], device))
+        return arrivals
+
+    def onward_copies(tensor, at):
+        first, second = rows(tensor, at, qx, 0, half), rows(tensor, at, qy, half, half)
+        return [
+            remote(first, first, f_send.at[tensor, at, 0], f_recv.at[tensor, at, 0], cy),
+            remote(second, second, f_send.at[tensor, at, 1], f_recv.at[tensor, at, 1], cx),
+        ]
+
+    def onward_arrivals(tensor, at):
+        first, second = rows(tensor, at, qd, 0, half), rows(tensor, at, qd, half, half)
+        return [
+            remote(first, first, f_send.at[tensor, at, 0], f_recv.at[tensor, at, 0], cy),
+            remote(second, second, f_send.at[tensor, at, 1], f_recv.at[tensor, at, 1], cx),
+        ]
+
+    def send_line(tensor, at, condition, way):
+        @pl.when(condition)
+        def _():
+            line_copy(tensor, at, way).start()
+
+    def wait_line(tensor, at, condition, way):
+        @pl.when(condition)
+        def _():
+            line_copy(tensor, at, way).wait_send()
+
+    def step_a(k):
+        at = source(k)
+        for tensor in (0, 1):
+            if k > 0:
+                line_copy(tensor, at, 0).wait_recv()
+                send_line(tensor, at, (at < z) & has_up, 0)
+                send_line(tensor, at, (at > z) & has_down, 1)
+            for copy in plane_copies(tensor, at):
+                copy.start()
+
+    def step_b(k):
+        at = source(k)
+        for tensor in (0, 1):
+            arrivals = plane_arrivals(tensor, at)
+            onward = onward_copies(tensor, at)
+            for i in (0, 1):
+                arrivals[i].wait_recv()
+                onward[i].start()
+
+    def step_c(k):
+        at = source(k)
+        for tensor in (0, 1):
+            for copy in plane_arrivals(tensor, at)[2:] + onward_arrivals(tensor, at):
+                copy.wait_recv()
+            for copy in plane_copies(tensor, at) + onward_copies(tensor, at):
+                copy.wait_send()
+            wait_line(tensor, at, (at <= z) & has_up, 0)
+            wait_line(tensor, at, (at >= z) & has_down, 1)
+
+    def compute(k):
+        slot = pl.ds(pl.multiple_of(source(k) * slot_rows, slot_rows), slot_rows)
+        tile = 256 if part % 256 == 0 else part
+
+        @pl.loop(0, 2 * part // tile)
+        def _(j):
+            span = pl.ds(pl.multiple_of(j * tile, tile), tile)
+            upper = pl.ds(pl.multiple_of(j * tile + 2 * part, tile), tile)
+            gate = dot(act[0, slot, :], w_gu[:, span], ((1,), (0,)))
+            above = dot(act[0, slot, :], w_gu[:, upper], ((1,), (0,)))
+            d_hidden = dot(act[1, slot, :], w_down[span, :], ((1,), (1,)))
+            sigma = jax.nn.sigmoid(gate)
+            active = gate * sigma
+            hid[:, span] = (active * above).astype(jnp.bfloat16)
+            d_gu[:, span] = (d_hidden * above * sigma * (1.0 + gate * (1.0 - sigma))).astype(jnp.bfloat16)
+            d_gu[:, upper] = (d_hidden * active).astype(jnp.bfloat16)
+
+        @pl.loop(0, width // 256)
+        def _(j):
+            span = pl.ds(pl.multiple_of(j * 256, 256), 256)
+            down_term = dot(hid[...], act[1, slot, span], ((0,), (0,)))
+            gate_up_term = dot(act[0, slot, span], d_gu[...], ((0,), (0,)))
+            if k > 0:
+                down_term = down_term + acc_down[:, span]
+                gate_up_term = gate_up_term + acc_gu[span, :]
+            acc_down[:, span] = down_term
+            acc_gu[span, :] = gate_up_term
+            act[1, slot, span] = dot(hid[...], w_down[:, span], ((1,), (0,))).astype(jnp.bfloat16)
+            act[0, slot, span] = dot(d_gu[...], w_gu[span, :], ((1,), (1,))).astype(jnp.bfloat16)
+
+    def landing(tensor, at, first, count):
+        return land.at[tensor, at, pl.ds(first, count), :]
+
+    def second_copies(tensor, at):
+        return [
+            remote(rows(tensor, at, qd, 0, half), landing(tensor, at, 2 * blk, half), r2_send.at[tensor, at, 0], r2_recv.at[tensor, at, 0], cy),
+            remote(rows(tensor, at, qd, half, half), landing(tensor, at, 2 * blk + half, half), r2_send.at[tensor, at, 1], r2_recv.at[tensor, at, 1], cx),
+        ]
+
+    def third_copies(tensor, at):
+        copies = []
+        for i, (device, chip, first, lands) in enumerate(((cx, qx, 0, 0), (cy, qy, half, blk + half), (cx, qx, half, half), (cy, qy, 0, blk))):
+            copies.append(
+                remote(rows(tensor, at, chip, first, half), landing(tensor, at, lands, half), r3_send.at[tensor, at, i], r3_recv.at[tensor, at, i], device)
+            )
+        return copies
+
+    def reduce_a(k):
+        at = source(k)
+        for tensor in (1, 0):
+            for copy in second_copies(tensor, at) + third_copies(tensor, at)[2:]:
+                copy.start()
+
+    def reduce_b(k):
+        at = source(k)
+        for tensor in (1, 0):
+            for i, (chip, first) in enumerate(((qx, 0), (qy, half))):
+                second_copies(tensor, at)[i].wait_recv()
+                add_rows(rows(tensor, at, chip, first, half), [landing(tensor, at, 2 * blk + first, half)], half)
+                third_copies(tensor, at)[i].start()
+
+    def sum_copy(tensor, at, way):
+        place = jnp.where((way == 1) & (at == z - 1), line, at)
+        return remote(rows(tensor, at, q), line_land.at[tensor, place], r4_send.at[tensor, at], r4_recv.at[tensor, place], (up, down)[way])
+
+    def reduce_c(k):
+        at = source(k)
+        results = (d_normed_ref, mlp_ref)
+        for tensor in (1, 0):
+            for copy in third_copies(tensor, at):
+                copy.wait_recv()
+            mine_rows = rows(tensor, at, q)
+            plane = [landing(tensor, at, 0, blk), landing(tensor, at, blk, blk)]
+            if k > 0:
+                joined = ((at > z) & has_down) | ((at < z) & has_up)
+
+                @pl.when(joined)
+                def _():
+                    arrival = remote(mine_rows, line_land.at[tensor, at], r4_send.at[tensor, at], r4_recv.at[tensor, at], sibling)
+                    arrival.wait_recv()
+                    add_rows(mine_rows, plane + [line_land.at[tensor, at]], blk)
+
+                @pl.when(jnp.logical_not(joined))
+                def _():
+                    add_rows(mine_rows, plane, blk)
+
+                @pl.when(at > z)
+                def _():
+                    sum_copy(tensor, at, 0).start()
+
+                @pl.when(at < z)
+                def _():
+                    sum_copy(tensor, at, 1).start()
+
+            else:
+                add_rows(mine_rows, plane, blk, results[tensor])
+                for condition, place in ((has_down, at), (has_up, line)):
+
+                    @pl.when(condition)
+                    def _():
+                        remote(mine_rows, line_land.at[tensor, place], r4_send.at[tensor, at], r4_recv.at[tensor, place], sibling).wait_recv()
+                        add_rows(results[tensor], [line_land.at[tensor, place]], blk, results[tensor])
+
+    def reduce_end(k):
+        at = source(k)
+        for tensor in (1, 0):
+            for copy in second_copies(tensor, at) + third_copies(tensor, at):
+                copy.wait_send()
+            if k > 0:
+                sum_copy(tensor, at, 0).wait_send()
+
+    def exchange_grads():
+        gate_half, up_half = theirs[0], theirs[1]
+
+        @pl.loop(0, width // 256)
+        def _(j):
+            span = pl.ds(pl.multiple_of(j * 256, 256), 256)
+            w_gu[span, :part] = acc_gu[span, gate_half].astype(jnp.bfloat16)
+            w_gu[span, part : 2 * part] = acc_gu[span, up_half].astype(jnp.bfloat16)
+
+        w_down[:part, :] = acc_down[theirs[0], :].astype(jnp.bfloat16)
+        for copy in grad_copies:
+            copy.start()
+
+    grad_copies = [
+        remote(w_gu.at[:, : 2 * part], sib_gu, g_send.at[0], g_recv.at[0], sibling),
+        remote(w_down.at[:part, :], sib_down, g_send.at[1], g_recv.at[1], sibling),
+    ]
+    grad_outs = [
+        pltpu.make_async_copy(w_gu.at[:, 2 * part :], gate_up_grad_ref, out_sem.at[0]),
+        pltpu.make_async_copy(acc_down.at[mine[0], :], down_grad_ref, out_sem.at[1]),
+    ]
+
+    def finish_grads():
+        for copy in grad_copies:
+            copy.wait_recv()
+
+        @pl.loop(0, width // 256)
+        def _(j):
+            span = pl.ds(pl.multiple_of(j * 256, 256), 256)
+            for i in (0, 1):
+                cols = slice(i * part, (i + 1) * part)
+                w_gu[span, 2 * part + i * part : 2 * part + (i + 1) * part] = (
+                    acc_gu[span, mine[i]] + sib_gu[span, cols].astype(jnp.float32)
+                ).astype(jnp.bfloat16)
+
+        acc_down[mine[0], :] = acc_down[mine[0], :] + sib_down[...].astype(jnp.float32)
+        for copy in grad_outs:
+            copy.start()
+
+    for copy in own:
+        copy.start()
+    for copy in own:
+        copy.wait()
+    for tensor in (0, 1):
+        send_line(tensor, z, has_up, 0)
+        send_line(tensor, z, has_down, 1)
+    step_a(0)
+    for copy in to_sibling + own_weights:
+        copy.start()
+    for k in range(line):
+        if k + 1 < line:
+            step_a(k + 1)
+        step_b(k)
+        if k == 0:
+            for copy in own_weights:
+                copy.wait()
+            for copy in from_sibling:
+                copy.wait_recv()
+            for copy in to_sibling:
+                copy.wait_send()
+        else:
+            step_c(k - 1)
+            compute(k - 1)
+            reduce_a(k - 1)
+    step_c(line - 1)
+    compute(line - 1)
+    reduce_a(line - 1)
+    exchange_grads()
+    backwards = range(line - 1, -1, -1)
+    for k in backwards:
+        reduce_b(k)
+    finish_grads()
+    for k in backwards:
+        reduce_c(k)
+    for k in backwards:
+        reduce_end(k)
+    for copy in grad_copies:
+        copy.wait_send()
+    for copy in grad_outs:
+        copy.wait()
+
+
+def mlp_exchange(line, normed, d_mlp, gate_up, down):
+    blk, width = normed.shape
+    part = down.shape[0]
+    any_spec, vmem_spec = pl.BlockSpec(memory_space=pl.ANY), pl.BlockSpec(memory_space=pltpu.VMEM)
+    bf16, f32, dma = jnp.bfloat16, jnp.float32, pltpu.SemaphoreType.DMA
+    return pl.pallas_call(
+        functools.partial(mlp_kernel, line, blk, part),
+        out_shape=(
+            jax.ShapeDtypeStruct((blk, width), f32),
+            jax.ShapeDtypeStruct((blk, width), f32),
+            jax.ShapeDtypeStruct((width, 2 * part), bf16),
+            jax.ShapeDtypeStruct((part, width), f32),
+        ),
+        in_specs=[any_spec] * 4,
+        out_specs=(vmem_spec, vmem_spec, any_spec, any_spec),
+        scratch_shapes=[
+            pltpu.VMEM((2, line * 4 * blk, width), bf16),
+            pltpu.VMEM((2, line, 3 * blk, width), bf16),
+            pltpu.VMEM((2, line + 1, blk, width), bf16),
+            pltpu.VMEM((width, 4 * part), bf16),
+            pltpu.VMEM((2 * part, width), bf16),
+            pltpu.VMEM((width, 4 * part), f32),
+            pltpu.VMEM((2 * part, width), f32),
+            pltpu.VMEM((4 * blk, 2 * part), bf16),
+            pltpu.VMEM((4 * blk, 4 * part), bf16),
+            pltpu.VMEM((width, 2 * part), bf16),
+            pltpu.VMEM((part, width), bf16),
+            dma((2, line, 2)),
+            dma((2, line)),
+            dma((2, line, 4)),
+            dma((2, line, 4)),
+            dma((2, line, 2)),
+            dma((2, line, 2)),
+            dma((2, line, 2)),
+            dma((2, line, 2)),
+            dma((2, line, 4)),
+            dma((2, line, 4)),
+            dma((2, line)),
+            dma((2, line + 1)),
+            dma((3,)),
+            dma((3,)),
+            dma((2,)),
+            dma((2,)),
+            dma((5,)),
+            dma((2,)),
+        ],
+        compiler_params=pltpu.CompilerParams(collective_id=0, has_side_effects=True, vmem_limit_bytes=63 * MIB),
+    )(normed, d_mlp, gate_up, down)
+
+
+def mlp_lax(normed_two, d_mlp, gate_up_mine, w_down):
+    ff_part = w_down.shape[0]
+    d_mlp = lax.all_gather(d_mlp, EVERY, axis=0, tiled=True)
+    normed_two = lax.all_gather(normed_two, EVERY, axis=0, tiled=True)
+    gate_up = dot(normed_two, gate_up_mine, ((1,), (0,)))
+    gate, up = gate_up[:, :ff_part], gate_up[:, ff_part:]
+    sigma = jax.nn.sigmoid(gate)
+    active = gate * sigma
+    hidden = (active * up).astype(jnp.bfloat16)
+    down_term = dot(hidden, w_down, ((1,), (0,))).astype(jnp.bfloat16)
+    d_hidden = dot(d_mlp, w_down, ((1,), (1,)))
+    d_gate = d_hidden * up * sigma * (1.0 + gate * (1.0 - sigma))
+    d_up = d_hidden * active
+    d_gate_up = jnp.concatenate([d_gate, d_up], axis=1).astype(jnp.bfloat16)
+    normed_term = dot(d_gate_up, gate_up_mine, ((1,), (1,))).astype(jnp.bfloat16)
+    grad_down = dot(hidden, d_mlp, ((0,), (0,)))
+    gate_up_grad = dot(normed_two, d_gate_up, ((0,), (0,))).astype(jnp.bfloat16)
+    mlp_proj = lax.psum_scatter(down_term, EVERY, scatter_dimension=0, tiled=True).astype(jnp.float32)
+    d_normed_two = lax.psum_scatter(normed_term, EVERY, scatter_dimension=0, tiled=True).astype(jnp.float32)
+    return (mlp_proj, d_normed_two, gate_up_grad, grad_down)
+
+
 def split_heads(w, parts):
     rows = w.shape[0]
     q_width, kv_width = HEADS * HEAD_DIM, KV_HEADS * HEAD_DIM
@@ -186,24 +614,11 @@
     clip = CLIP_TARGET / jnp.maximum(head_top, CLIP_TARGET)
 
     scale_two = rms_scale(mid)
-    d_mlp = lax.all_gather((BRANCH * grad_rows).astype(jnp.bfloat16), EVERY, axis=0, tiled=True)
-    normed_two = lax.all_gather((mid * scale_two * gain_two).astype(jnp.bfloat16), EVERY, axis=0, tiled=True)
-    gate_up = dot(normed_two, gate_up_mine, ((1,), (0,)))
-    gate, up = gate_up[:, :ff_part], gate_up[:, ff_part:]
-    sigma = jax.nn.sigmoid(gate)
-    active = gate * sigma
-    hidden = (active * up).astype(jnp.bfloat16)
-    down_term = dot(hidden, w_down, ((1,), (0,))).astype(jnp.bfloat16)
-    d_hidden = dot(d_mlp, w_down, ((1,), (1,)))
-    d_gate = d_hidden * up * sigma * (1.0 + gate * (1.0 - sigma))
-    d_up = d_hidden * active
-    d_gate_up = jnp.concatenate([d_gate, d_up], axis=1).astype(jnp.bfloat16)
-    normed_term = dot(d_gate_up, gate_up_mine, ((1,), (1,))).astype(jnp.bfloat16)
-    grad_down = dot(hidden, d_mlp, ((0,), (0,)))
-    gate_up_grad = dot(normed_two, d_gate_up, ((0,), (0,))).astype(jnp.bfloat16)
-    mlp_proj = lax.psum_scatter(down_term, EVERY, scatter_dimension=0, tiled=True)
-    mixed = (mid + BRANCH * mlp_proj.astype(jnp.float32)).astype(jnp.bfloat16).reshape(1, count, width)
-    d_normed_two = lax.psum_scatter(normed_term, EVERY, scatter_dimension=0, tiled=True).astype(jnp.float32)
+    d_mlp = (BRANCH * grad_rows).astype(jnp.bfloat16)
+    normed_two = (mid * scale_two * gain_two).astype(jnp.bfloat16)
+    mlp = functools.partial(mlp_exchange, n_shard) if n_ctx == 8 else mlp_lax
+    mlp_proj, d_normed_two, gate_up_grad, grad_down = mlp(normed_two, d_mlp, gate_up_mine, w_down)
+    mixed = (mid + BRANCH * mlp_proj).astype(jnp.bfloat16).reshape(1, count, width)
     grad_gate_up = lax.all_to_all(gate_up_grad.reshape(n * w_rows, 2, 1, ff_part), EVERY, split_axis=0, concat_axis=2, tiled=True)
     grad_gate_up = grad_gate_up.reshape(w_rows, 2 * n * ff_part).astype(jnp.float32)
     d_mid_norm, gain_two_term = norm_backward(d_normed_two, mid, scale_two, gain_two)

time: 1640 us -> 935 us (0.57)
  waiting for transfers between devices: 1210 us -> 365 us
  Pallas kernels: 17.4 us -> 337 us
  matrix products: 116 us -> 28.4 us
  blocking collectives: 188 us -> 104 us
    reduce_scatter x2 -> x0, waiting for transfers between devices: 727 us -> none  [the longest x1 365 us: per_device(): lax.psum_scatter(down_term, EVERY, scatter_dimension=0, tiled=True)]
    pallas_call x0 -> x1, Pallas kernels: none -> 320 us  [mlp_exchange(): pl.pallas_call(functools.partial(mlp_kernel, line, blk, part), out_shape=...]
    all_gather x2 -> x0, waiting for transfers between devices: 155 us -> none  [the longest x1 102 us: per_device(): lax.all_gather((BRANCH * grad_rows).astype(jnp.bfloat16), EVERY, axis=0,...]
    dot_general x12 -> x6, matrix products: 116 us -> 28.4 us  [dot(): lax.dot_general(left, right, ((dims[0], dims[1]), ((), ())), preferred_el...]
    all_to_all x1 -> x0, blocking collectives: 84.1 us -> none  [per_device(): lax.all_to_all(w_gate_up.reshape(w_rows, 2, n, ff_part), EVERY, split_axi...]
    reduce_scatter x1, waiting for transfers between devices: 50.9 us -> 0.01 us  [per_device(): lax.psum_scatter(out_term, 'ctx', scatter_dimension=0, tiled=True)]
    all_to_all x0 -> x1, waiting for transfers between devices: none -> 46.5 us  [per_device(): lax.all_to_all(w_gate_up.reshape(w_rows, 2, n, ff_part), EVERY, split_axi...]
    reduce_scatter x1, waiting for transfers between devices: 24 us -> 50.5 us  [per_device(): lax.psum_scatter(qkv_term, 'ctx', scatter_dimension=0, tiled=True)]
  transfers between devices with their start and end apart: 15 -> 12, of which waited for: 13 -> 8; matrix products, arithmetic and copies ran while one was open for 7% -> 6% of each run, Pallas kernels for 0% -> 1%
where the time goes in v2:
time: 935 us; the launch traced here: 924 us
  waiting for transfers between devices  365 us (39%)
  Pallas kernels  337 us (36%)
  blocking collectives  104 us (11%)
  local copies, waits for them, and re-layouts  40.9 us (4%)
  matrix products  28.4 us (3%)
  other arithmetic  20 us (2%)
  between operations  15.4 us (2%)
  starting transfers between devices  13.2 us (1%)
    pallas_call x1, Pallas kernels, mlp_exchange(): pl.pallas_call(functools.partial(mlp_kernel, line, blk, part), out_shape=...  320 us
    unnamed x10, waiting for transfers between devices  131 us
    all_gather x1, blocking collectives, per_device(): lax.all_gather(jnp.stack([gain_attn, gain_mlp]), EVERY, axis=1, tiled=True)  66.4 us
    reduce_scatter x1, waiting for transfers between devices, per_device(): lax.psum_scatter(qkv_term, 'ctx', scatter_dimension=0, tiled=True)  50.5 us
    all_to_all x1, waiting for transfers between devices, per_device(): lax.all_to_all(w_gate_up.reshape(w_rows, 2, n, ff_part), EVERY, split_axi...  46.5 us
    reduce_scatter x1, waiting for transfers between devices, per_device(): lax.psum_scatter(dot(attn_out, d_attn, ((0,), (0,))), 'shard', scatter_di...  38.1 us
    all_gather x1, waiting for transfers between devices, per_device(): lax.all_gather((BRANCH * d_mid).astype(jnp.bfloat16), 'ctx', axis=0, tile...  35.3 us
    all_gather x1, waiting for transfers between devices, per_device(): lax.all_gather((rows * scale_one * gain_one).astype(jnp.bfloat16), 'ctx',...  31 us
  transfers between devices with their start and end apart: 12, of which 8 were waited for; matrix products, arithmetic and copies ran while one was open for 6% of the time, Pallas kernels for 1%

profile of v2, /device:TPU:0, one launch (start us, length us, event | category | flops | bytes accessed | tf_op | source)
XLA Modules:
  0.0 924.0 jit_solution(12681423287754774782)
XLA Ops:
  9.6 13.3 %all_to_all.34 = bf16[64,8,384]{2,0,1:T(8,128)(2,1)S(1)} all-to-all(bf16[64,8,384]{2,0,1:T(8,128)(2,1)S(1)} %copy.70), channel_id=1, replica_groups=mesh['ctx'=8,'shard'=4] {'ctx'}, dimensions={1} | all-to-all | bytes 786432 | tf_op jit(solution)/shard_map/all_to_all | solution.py:593
  24.0 66.4 %all-gather = bf16[32,64,2]{1,2,0:T(2,128)(2,1)S(1)} all-gather(bf16[1,64,2]{1,2,0:T(2,128)(2,1)S(1)} %maximum_bitcast_fusion), channel_id=1, replica_groups=mesh['ctx'=8,'shard'=4] {'ctx','shard'}, dimensions={0}, use_global_device_ids=true | all-gather | bytes 8448 | tf_op jit(solution)/shard_map/all_gather | solution.py:590
  94.7 31.0 %all-gather.6.cloned.1.call-done = bf16[1024,2048]{1,0:T(8,128)(2,1)} async-done(((bf16[128,2048]{1,0:T(8,128)(2,1)}), bf16[1024,2048]{1,0:T(8,128)(2,1)}) %all-gather.6.cloned.1.call-update) | async-done | bytes 4194320 | tf_op jit(solution)/shard_map/all_gather | solution.py:601
  125.7 4.5 convolution_convert_fusion.2
  131.0 6.9 shard_map.160
  139.4 15.8 %all-gather.10.cloned.1.call-done = bf16[256,2048]{1,0:T(8,128)(2,1)} async-done(((bf16[64,2048]{1,0:T(8,128)(2,1)}), bf16[256,2048]{1,0:T(8,128)(2,1)}) %all-gather.10.cloned.1.call-update) | async-done | bytes 1048592 | tf_op jit(solution)/shard_map/all_gather | solution.py:596
  155.2 4.5 convolution_convert_fusion.1
  161.9 3.7 copy.75
  165.6 4.2 all-to-all-start.1
  170.8 46.5 %all-to-all-done.1 = bf16[64,2,32,256]{3,1,0,2:T(2,128)(2,1)} async-done(((bf16[64,2,32,256]{3,1,0,2:T(2,128)(2,1)}), bf16[64,2,32,256]{3,1,0,2:T(2,128)(2,1)}, u32[]{:S(2)}, u32[]{:S(2)}) %all-to-all-start.1) | async-done | bytes 2097184 | tf_op jit(solution)/shard_map/all_to_all | solution.py:597
  217.3 3.4 copy.90
  224.1 320.0 %shard_map.161 = (f32[128,2048]{1,0:T(8,128)}, f32[128,2048]{1,0:T(8,128)}, bf16[2048,512]{1,0:T(8,128)(2,1)}, f32[256,2048]{1,0:T(8,128)}) custom-call(bf16[128,2048]{1,0:T(8,128)(2,1)} %multiply_convert_fusion.1.normed_ref, bf16[128,2048]{1,0:T(8,128)(2,1)} %fusion.8.d_mlp_ref, bf16[2048,512]{1,0:T(8,128)(2,1)} %bitcast.103, bf16[256,2048]{1,0:T(8,128)(2,1)} %down_ref.1), custom_call_target="tpu_custom_call" | custom-call | tf_op jit(solution)/shard_map/pallas_call | solution.py:486
  546.3 2.3 multiply_convert_fusion
  548.8 35.3 %all-gather.12.cloned.1.call-done = bf16[1024,2048]{1,0:T(8,128)(2,1)} async-done(((bf16[128,2048]{1,0:T(8,128)(2,1)}), bf16[1024,2048]{1,0:T(8,128)(2,1)}) %all-gather.12.cloned.1.call-update) | async-done | bytes 4194320 | tf_op jit(solution)/shard_map/all_gather | solution.py:627
  584.1 3.8 convolution_convert_fusion.3.do_ref
  587.9 10.3 %shard_map.162 = (bf16[1024,256]{1,0:T(8,128)(2,1)S(1)}, bf16[1024,64]{1,0:T(8,128)(2,1)S(1)}, bf16[1024,64]{1,0:T(8,128)(2,1)S(1)}) custom-call(bf16[1024,256]{1,0:T(8,128)(2,1)S(1)} %copy-done.1, bf16[1024,64]{1,0:T(8,128)(2,1)S(1)} %copy-done.5, bf16[1024,64]{1,0:T(8,128)(2,1)S(1)} %get-tuple-element.37.v_ref, bf16[1024,256]{1,0:T(8,128)(2,1)S(1)} %copy-done.3, ...), custom_call_target="tpu_custom_call" | custom-call | tf_op jit(solution)/shard_map/pallas_call | solution.py:117
  599.2 4.6 convolution_convert_fusion
  605.0 6.3 fusion.14
  611.3 4.0 reshape.128
  615.4 4.8 all-to-all-start.3
  620.3 50.5 %reduce-scatter.10.cloned.1.call-done = bf16[128,2048]{1,0:T(8,128)(2,1)} async-done(((bf16[1024,2048]{1,0:T(8,128)(2,1)}), bf16[128,2048]{1,0:T(8,128)(2,1)}) %reduce-scatter.10.cloned.1.call-update) | async-done | bytes 524304 | tf_op jit(solution)/shard_map/reduce_scatter | solution.py:633
  673.7 4.8 fusion.22
  680.4 11.4 %pmax.7 = f32[1,4]{1,0:T(1,128)S(1)} all-reduce(f32[1,4]{1,0:T(1,128)S(1)} %get-tuple-element.28), channel_id=1, replica_groups=mesh['ctx'=8,'shard'=4] {'shard'}, use_global_device_ids=true, to_apply=%region_13.14 | all-reduce | flops 4 | bytes 32 | tf_op jit(solution)/shard_map/pmax | solution.py:613
  691.9 12.9 %all-reduce = f32[32]{0:T(128)S(1)} all-reduce(f32[32]{0:T(128)S(1)} %bitcast_dynamic-update-slice_fusion), channel_id=1, replica_groups=mesh['ctx'=8,'shard'=4] {'ctx'}, use_global_device_ids=true, to_apply=%add | all-reduce | flops 32 | bytes 256
  705.3 3.4 convert_bitcast_fusion
  708.7 4.4 copy.81
  713.1 5.0 reshape.131
  718.1 16.1 %reduce-scatter.12.cloned.1.call-done = f32[8,64,384]{2,1,0:T(8,128)} async-done(((f32[8,256,384]{2,1,0:T(8,128)}), f32[8,64,384]{2,1,0:T(8,128)}) %reduce-scatter.12.cloned.1.call-update) | async-done | bytes 786448 | tf_op jit(solution)/shard_map/reduce_scatter | solution.py:635
  734.3 3.7 all-to-all-start.2
  738.0 3.4 fusion.7
  741.4 130.7 %reduce-scatter.16.cloned.1.call-done = f32[64,2]{1,0:T(8,128)} async-done(((f32[2048,2]{1,0:T(8,128)}), f32[64,2]{1,0:T(8,128)}) %reduce-scatter.16.cloned.1.call-update) | async-done | bytes 528
  877.6 38.1 %reduce-scatter.14.cloned.1.call-done = f32[64,2048]{1,0:T(8,128)} async-done(((f32[256,2048]{1,0:T(8,128)}), f32[64,2048]{1,0:T(8,128)}) %reduce-scatter.14.cloned.1.call-update) | async-done | bytes 524304 | tf_op jit(solution)/shard_map/reduce_scatter | solution.py:628
  (131 shorter events, 32.5 us)
Async XLA Ops:
  7.2 85.9 %all-gather.8.cloned.1.call-start = ((), (), s32[]{:S(2)}) async-start(), calls=%async_computation.10 | async-start | bytes 1966080 | tf_op jit(solution)/shard_map/all_gather | solution.py:595
  9.4 14.6 %copy-start.26 = (bf16[64]{0:T(256)(128)(2,1)S(1)}, bf16[64]{0:T(256)(128)(2,1)}, u32[]{:S(2)}) copy-start(bf16[64]{0:T(256)(128)(2,1)} %param.17) | copy-start | bytes 388
  9.4 14.6 %copy-start.27 = (bf16[64]{0:T(256)(128)(2,1)S(1)}, bf16[64]{0:T(256)(128)(2,1)}, u32[]{:S(2)}) copy-start(bf16[64]{0:T(256)(128)(2,1)} %param.16) | copy-start | bytes 388
  9.4 81.2 %copy-start.14 = (bf16[1,128,2048]{2,1,0:T(8,128)(2,1)S(1)}, bf16[1,128,2048]{2,1,0:T(8,128)(2,1)}, u32[]{:S(2)}) copy-start(bf16[1,128,2048]{2,1,0:T(8,128)(2,1)} %param.9) | copy-start | bytes 1572868
  9.6 82.9 %copy-start.28 = (s32[1,9]{1,0:T(1,128)S(1)}, s32[1,9]{1,0:T(1,128)}, u32[]{:S(2)}) copy-start(s32[1,9]{1,0:T(1,128)} %param.10) | copy-start | bytes 112
  23.9 101.7 %all-gather.6.cloned.1.call-start = ((), (), s32[]{:S(2)}) async-start(), calls=%async_computation.9 | async-start | bytes 4718592 | tf_op jit(solution)/shard_map/all_gather | solution.py:601
  91.8 63.4 %all-gather.10.cloned.1.call-start = ((), (), s32[]{:S(2)}) async-start(), calls=%async_computation.11 | async-start | bytes 1310720 | tf_op jit(solution)/shard_map/all_gather | solution.py:596
  92.5 128.2 %reduce-scatter.8.cloned.1.call-start = ((), (), s32[]{:S(2)}) async-start(), calls=%async_computation.12 | async-start | bytes 4718592 | tf_op jit(solution)/shard_map/reduce_scatter | solution.py:611
  94.7 31.0 %copy-start.24 = (bf16[8,256,384]{2,1,0:T(8,128)(2,1)}, bf16[8,256,384]{2,1,0:T(8,128)(2,1)S(1)}, u32[]{:S(2)}) copy-start(bf16[8,256,384]{2,1,0:T(8,128)(2,1)S(1)} %copy.72) | copy-start | bytes 4718596
  139.4 20.3 %copy-start.2 = (bf16[1024,256]{1,0:T(8,128)(2,1)}, bf16[1024,256]{1,0:T(8,128)(2,1)S(1)}, u32[]{:S(2)}) copy-start(bf16[1024,256]{1,0:T(8,128)(2,1)S(1)} %get-tuple-element.19.o_ref) | copy-start | bytes 1572868
  165.6 4.3 copy-start.21
  165.6 51.7 %all-to-all-start.1 = ((bf16[64,2,32,256]{3,1,0,2:T(2,128)(2,1)}), bf16[64,2,32,256]{3,1,0,2:T(2,128)(2,1)}, u32[]{:S(2)}, u32[]{:S(2)}) async-start(bf16[64,2,32,256]{3,1,0,2:T(2,128)(2,1)} %copy.75), calls=%async_computation.2 | async-start | bytes 4194304 | tf_op jit(solution)/shard_map/all_to_all | solution.py:597
  169.8 414.2 %all-gather.12.cloned.1.call-start = ((), (), s32[]{:S(2)}) async-start(), calls=%async_computation.13 | async-start | bytes 4718592 | tf_op jit(solution)/shard_map/all_gather | solution.py:627
  544.2 2.1 copy-start.15
  544.2 2.1 copy-start.17
  544.2 2.2 copy-start.19
  548.7 39.2 %copy-start.1 = (bf16[1024,256]{1,0:T(8,128)(2,1)S(1)}, bf16[1024,256]{1,0:T(8,128)(2,1)}, u32[]{:S(2)}) copy-start(bf16[1024,256]{1,0:T(8,128)(2,1)} %copy-done) | copy-start | bytes 1572868
  548.7 39.2 %copy-start.3 = (bf16[1024,256]{1,0:T(8,128)(2,1)S(1)}, bf16[1024,256]{1,0:T(8,128)(2,1)}, u32[]{:S(2)}) copy-start(bf16[1024,256]{1,0:T(8,128)(2,1)} %copy-done.2) | copy-start | bytes 1572868
  548.7 39.2 %copy-start.5 = (bf16[1024,64]{1,0:T(8,128)(2,1)S(1)}, bf16[1024,64]{1,0:T(8,128)(2,1)}, u32[]{:S(2)}) copy-start(bf16[1024,64]{1,0:T(8,128)(2,1)} %copy-done.4) | copy-start | bytes 393220
  548.8 39.2 %copy-start.7 = (f32[1024,4]{1,0:T(8,128)S(1)}, f32[1024,4]{1,0:T(8,128)}, u32[]{:S(2)}) copy-start(f32[1024,4]{1,0:T(8,128)} %copy-done.6) | copy-start | bytes 49156
  548.8 122.0 %reduce-scatter.10.cloned.1.call-start = ((), (), s32[]{:S(2)}) async-start(), calls=%async_computation.14 | async-start | bytes 4718592 | tf_op jit(solution)/shard_map/reduce_scatter | solution.py:633
  587.9 11.4 %copy-start.25 = (bf16[8,256,384]{2,1,0:T(8,128)(2,1)S(1)}, bf16[8,256,384]{2,1,0:T(8,128)(2,1)}, u32[]{:S(2)}) copy-start(bf16[8,256,384]{2,1,0:T(8,128)(2,1)} %copy-done.24) | copy-start | bytes 4718596
  603.9 130.4 %reduce-scatter.12.cloned.1.call-start = ((), (), s32[]{:S(2)}) async-start(), calls=%async_computation.15 | async-start | bytes 3932160 | tf_op jit(solution)/shard_map/reduce_scatter | solution.py:635
  615.4 55.4 %copy-start.16 = (bf16[1,128,2048]{2,1,0:T(8,128)(2,1)S(1)}, bf16[1,128,2048]{2,1,0:T(8,128)(2,1)}, u32[]{:S(2)}) copy-start(bf16[1,128,2048]{2,1,0:T(8,128)(2,1)} %param.9) | copy-start | bytes 1572868
  615.4 90.0 %all-to-all-start.3 = ((bf16[2048,2,1,256]{3,1,2,0:T(2,128)(2,1)}), bf16[2048,2,1,256]{3,1,2,0:T(2,128)(2,1)}, u32[]{:S(2)}, u32[]{:S(2)}) async-start(bf16[2048,2,1,256]{3,1,2,0:T(2,128)(2,1)} %bitcast.102), calls=%async_computation.7 | async-start | bytes 4194304 | tf_op jit(solution)/shard_map/all_to_all | solution.py:622
  620.2 251.8 %reduce-scatter.16.cloned.1.call-start = ((), (), s32[]{:S(2)}) async-start(), calls=%async_computation.17 | async-start | bytes 1081344
  673.7 242.1 %reduce-scatter.14.cloned.1.call-start = ((), (), s32[]{:S(2)}) async-start(), calls=%async_computation.16 | async-start | bytes 2621440 | tf_op jit(solution)/shard_map/reduce_scatter | solution.py:628
  713.1 24.9 %copy-start.18 = (bf16[128,2048]{1,0:T(8,128)(2,1)S(1)}, bf16[128,2048]{1,0:T(8,128)(2,1)}, u32[]{:S(2)}) copy-start(bf16[128,2048]{1,0:T(8,128)(2,1)} %reduce-scatter.8.cloned.1.call-done) | copy-start | bytes 1572868
  713.1 24.9 %copy-start.22 = (bf16[1,128,2048]{2,1,0:T(8,128)(2,1)S(1)}, bf16[1,128,2048]{2,1,0:T(8,128)(2,1)}, u32[]{:S(2)}) copy-start(bf16[1,128,2048]{2,1,0:T(8,128)(2,1)} %param.11) | copy-start | bytes 1572868
  718.1 19.9 %copy-start.20 = (f32[128,2048]{1,0:T(8,128)S(1)}, f32[128,2048]{1,0:T(8,128)}, u32[]{:S(2)}) copy-start(f32[128,2048]{1,0:T(8,128)} %get-tuple-element.21) | copy-start | bytes 3145732
  734.3 139.9 %all-to-all-start.2 = ((f32[8,64,384]{2,1,0:T(8,128)}), f32[8,64,384]{2,1,0:T(8,128)S(1)}, u32[]{:S(2)}, u32[]{:S(2)}) async-start(f32[8,64,384]{2,1,0:T(8,128)} %reduce-scatter.12.cloned.1.call-done), calls=%async_computation.5 | async-start | bytes 1572864 | tf_op jit(solution)/shard_map/all_to_all | solution.py:636
  875.2 40.5 %copy-start.23 = (f32[256,2048]{1,0:T(8,128)S(1)}, f32[256,2048]{1,0:T(8,128)}, u32[]{:S(2)}) copy-start(f32[256,2048]{1,0:T(8,128)} %get-tuple-element.59) | copy-start | bytes 6291460
  (10 other events, 8.9 us)
Sparse Core Ops, SparseCore 0:
  24.1 36.6 all-gather.7
  91.9 33.7 all-gather.5
  127.3 27.9 all-gather.9
  159.9 60.8 reduce-scatter.7
  548.8 35.2 all-gather.11
  604.0 66.7 reduce-scatter.9
  673.1 61.1 reduce-scatter.11
  736.5 135.4 reduce-scatter.15
  875.0 40.6 reduce-scatter.13

commit v3 on v2

--- a/solution.py
+++ b/solution.py
@@ -528,26 +528,523 @@
     )(normed, d_mlp, gate_up, down)
 
 
-def mlp_lax(normed_two, d_mlp, gate_up_mine, w_down):
-    ff_part = w_down.shape[0]
-    d_mlp = lax.all_gather(d_mlp, EVERY, axis=0, tiled=True)
-    normed_two = lax.all_gather(normed_two, EVERY, axis=0, tiled=True)
-    gate_up = dot(normed_two, gate_up_mine, ((1,), (0,)))
-    gate, up = gate_up[:, :ff_part], gate_up[:, ff_part:]
-    sigma = jax.nn.sigmoid(gate)
-    active = gate * sigma
-    hidden = (active * up).astype(jnp.bfloat16)
-    down_term = dot(hidden, w_down, ((1,), (0,))).astype(jnp.bfloat16)
-    d_hidden = dot(d_mlp, w_down, ((1,), (1,)))
-    d_gate = d_hidden * up * sigma * (1.0 + gate * (1.0 - sigma))
-    d_up = d_hidden * active
-    d_gate_up = jnp.concatenate([d_gate, d_up], axis=1).astype(jnp.bfloat16)
-    normed_term = dot(d_gate_up, gate_up_mine, ((1,), (1,))).astype(jnp.bfloat16)
-    grad_down = dot(hidden, d_mlp, ((0,), (0,)))
-    gate_up_grad = dot(normed_two, d_gate_up, ((0,), (0,))).astype(jnp.bfloat16)
-    mlp_proj = lax.psum_scatter(down_term, EVERY, scatter_dimension=0, tiled=True).astype(jnp.float32)
-    d_normed_two = lax.psum_scatter(normed_term, EVERY, scatter_dimension=0, tiled=True).astype(jnp.float32)
-    return (mlp_proj, d_normed_two, gate_up_grad, grad_down)
+class Place:
+    def __init__(self, line):
+        self.line = line
+        self.c, self.z = lax.axis_index("ctx"), lax.axis_index("shard")
+        self.q, self.core = self.c // 2, self.c % 2
+        self.me = self.c * line + self.z
+        self.every = 8 * line
+        self.cx, self.cy = (self.c + 2 - 4 * (self.q % 2), self.z), (self.c + 4 - 8 * (self.q // 2), self.z)
+        self.sibling = (self.c + 1 - 2 * self.core, self.z)
+        self.qx, self.qy, self.qd = self.q + 1 - 2 * (self.q % 2), self.q + 2 - 4 * (self.q // 2), 3 - self.q
+
+    def peer(self, i):
+        other = lax.rem(self.me + i, self.every)
+        return other, (other // self.line, other % self.line)
+
+    def greet_all(self):
+        barrier = pltpu.get_barrier_semaphore()
+
+        @pl.loop(1, self.every)
+        def _(i):
+            pl.semaphore_signal(barrier, inc=1, device_id=self.peer(i)[1], device_id_type=pl.DeviceIdType.MESH)
+
+        pl.semaphore_wait(barrier, self.every - 1)
+
+    def push_all(self, source, target, send_sems, recv_sems):
+        @pl.loop(1, self.every)
+        def _(i):
+            other, device = self.peer(i)
+            remote(source(other), target(self.me), send_sems.at[other], recv_sems.at[self.me], device).start()
+
+    def wait_all(self, source, target, send_sems, recv_sems, sent=True):
+        @pl.loop(1, self.every)
+        def _(i):
+            other, device = self.peer(i)
+            copy = remote(source(other), target(other), send_sems.at[other], recv_sems.at[other], device)
+            if sent:
+                copy.wait_send()
+            else:
+                copy.wait_recv()
+
+
+def plane_gather(at, buf, blk, sems):
+    p_send, p_recv, f_send, f_recv, s_send, s_recv = sems
+    half = blk // 2
+
+    def rows(chip, core, first=0, count=half):
+        return buf.at[pl.ds(pl.multiple_of((2 * chip + core) * blk + first, half), count), :]
+
+    def same(ref, send, recv, device):
+        return remote(ref, ref, send, recv, device)
+
+    way = ((at.cx, at.qx, 0), (at.cy, at.qy, half), (at.cx, at.qx, half), (at.cy, at.qy, 0))
+
+    def sent(i):
+        return same(rows(at.q, at.core, way[i][2]), p_send.at[i], p_recv.at[i], way[i][0])
+
+    def arriving(i):
+        return same(rows(way[i][1], at.core, way[i][2]), p_send.at[i], p_recv.at[i], way[i][0])
+
+    def onward(i):
+        chip, first, device = ((at.qx, 0, at.cy), (at.qy, half, at.cx))[i]
+        return same(rows(chip, at.core, first), f_send.at[i], f_recv.at[i], device)
+
+    def passed(i):
+        first, device = ((0, at.cy), (half, at.cx))[i]
+        return same(rows(at.qd, at.core, first), f_send.at[i], f_recv.at[i], device)
+
+    def across(i, core):
+        if i == 0:
+            ref = rows(at.q, core, 0, blk)
+        elif i < 5:
+            ref = rows(way[i - 1][1], core, way[i - 1][2])
+        else:
+            ref = rows(at.qd, core, (i - 5) * half)
+        return same(ref, s_send.at[i], s_recv.at[i], at.sibling)
+
+    def start():
+        for i in range(4):
+            sent(i).start()
+        across(0, at.core).start()
+
+    def finish():
+        for i in (0, 1):
+            arriving(i).wait_recv()
+            onward(i).start()
+            across(i + 1, at.core).start()
+        for i in (2, 3):
+            arriving(i).wait_recv()
+            across(i + 1, at.core).start()
+        for i in (0, 1):
+            passed(i).wait_recv()
+            across(i + 5, at.core).start()
+        for i in range(7):
+            across(i, 1 - at.core).wait_recv()
+
+    def end():
+        for i in range(4):
+            sent(i).wait_send()
+        for i in (0, 1):
+            onward(i).wait_send()
+        for i in range(7):
+            across(i, at.core).wait_send()
+
+    return start, finish, end
+
+
+GATHER_SEMS = (4, 4, 2, 2, 7, 7)
+REDUCE_SEMS = (4, 4, 2, 2, 4, 4)
+
+
+def plane_reduce(at, term, core_land, land, blk, sems):
+    s_send, s_recv, r2_send, r2_recv, r3_send, r3_recv = sems
+    half = blk // 2
+    chips = (at.qd, at.qx, at.qy, at.q)
+
+    def rows(chip, core, first=0, count=half):
+        return term.at[pl.ds(pl.multiple_of((2 * chip + core) * blk + first, half), count), :]
+
+    def landed(first, count):
+        return land.at[pl.ds(first, count), :]
+
+    def across(i):
+        return remote(rows(chips[i], 1 - at.core, 0, blk), core_land.at[i], s_send.at[i], s_recv.at[i], at.sibling)
+
+    def second(i):
+        first, device = ((0, at.cy), (half, at.cx))[i]
+        return remote(rows(at.qd, at.core, first), landed(2 * blk + first, half), r2_send.at[i], r2_recv.at[i], device)
+
+    def third(i):
+        device, chip, first, lands = (
+            (at.cx, at.qx, 0, 0), (at.cy, at.qy, half, blk + half), (at.cx, at.qx, half, half), (at.cy, at.qy, 0, blk)
+        )[i]
+        return remote(rows(chip, at.core, first), landed(lands, half), r3_send.at[i], r3_recv.at[i], device)
+
+    def add_core(i):
+        across(i).wait_recv()
+        add_rows(rows(chips[i], at.core, 0, blk), [core_land.at[i]], blk)
+
+    def give(i):
+        across(i).start()
+
+    def take(result):
+        add_core(0)
+        second(0).start()
+        second(1).start()
+        add_core(1)
+        third(2).start()
+        add_core(2)
+        third(3).start()
+        for i, (chip, first) in enumerate(((at.qx, 0), (at.qy, half))):
+            second(i).wait_recv()
+            add_rows(rows(chip, at.core, first), [landed(2 * blk + first, half)], half)
+            third(i).start()
+        add_core(3)
+        for i in range(4):
+            third(i).wait_recv()
+        add_rows(rows(at.q, at.core, 0, blk), [landed(0, blk), landed(blk, blk)], blk, result)
+
+    def end():
+        for i in range(4):
+            across(i).wait_send()
+            third(i).wait_send()
+        for i in (0, 1):
+            second(i).wait_send()
+
+    return give, take, end
+
+
+def front_kernel(
+    line, blk, q_part, kv_part,
+    tokens_ref, gains_ref, w_qkv_ref, w_out_ref, q_seg_ref, k_seg_ref,
+    mid_ref, normed_two_ref, qkv_ref, attn_ref, lse_ref, tops_ref, gain_ref, normed_ref, w_qkv_all_ref, w_out_all_ref,
+    buf, term, core_land, land, w_qkv, w_out, gain_land, top_land, proj,
+    *sems,
+):
+    at = Place(line)
+    gather = plane_gather(at, buf, blk, sems[:6])
+    reduce = plane_reduce(at, term, core_land, land, blk, sems[6:12])
+    qkv_send, qkv_recv, gain_send, gain_recv, top_send, top_recv, out_send, out_recv, own_sem, write_sem = sems[12:]
+    w_rows, width = w_out_ref.shape
+    size = 8 * blk
+    mine = pl.ds(pl.multiple_of(at.c * blk, blk), blk)
+
+    own = [
+        pltpu.make_async_copy(tokens_ref, buf.at[mine, :], own_sem.at[0]),
+        pltpu.make_async_copy(gains_ref, gain_land.at[at.me], own_sem.at[1]),
+        pltpu.make_async_copy(w_qkv_ref.at[at.c], w_qkv.at[at.me], own_sem.at[2]),
+        pltpu.make_async_copy(w_out_ref, w_out.at[at.z], own_sem.at[3]),
+    ]
+    for copy in own:
+        copy.start()
+    at.greet_all()
+    qkv_push = (lambda other: w_qkv_ref.at[other // line], lambda slot: w_qkv.at[slot], qkv_send, qkv_recv)
+    gain_push = (lambda other: gains_ref, lambda slot: gain_land.at[slot], gain_send, gain_recv)
+    top_push = (lambda other: top_land.at[at.me], lambda slot: top_land.at[slot], top_send, top_recv)
+    at.push_all(*gain_push)
+    own[0].wait()
+    gather[0]()
+    at.push_all(*qkv_push)
+
+    def out_copy(i, slot):
+        z = lax.rem(at.z + i, line)
+        return z, remote(w_out_ref, w_out.at[slot(z)], out_send.at[z], out_recv.at[slot(z)], (at.c, z))
+
+    for i in range(1, line):
+        out_copy(i, lambda z: at.z)[1].start()
+    gather[1]()
+    for copy in own[1:]:
+        copy.wait()
+    at.wait_all(*gain_push, sent=False)
+    for i in range(at.every // 2):
+        pair = gain_land[2 * i].astype(jnp.float32) + gain_land[2 * i + 1].astype(jnp.float32)
+        gain_ref[:, i * 128 : (i + 1) * 128] = pair[:8, :]
+    gather[2]()
+    at.wait_all(*gain_push)
+
+    @pl.loop(0, size // 32)
+    def _(i):
+        part = pl.ds(pl.multiple_of(i * 32, 32), 32)
+        rows = buf[part, :].astype(jnp.float32)
+        buf[part, :] = (rows * rms_scale(rows) * gain_ref[0:1, :]).astype(jnp.bfloat16)
+
+    writes = [
+        pltpu.make_async_copy(buf, normed_ref, write_sem.at[0]),
+        pltpu.make_async_copy(w_qkv, w_qkv_all_ref, write_sem.at[1]),
+        pltpu.make_async_copy(w_out, w_out_all_ref, write_sem.at[2]),
+    ]
+    writes[0].start()
+    at.wait_all(*qkv_push, sent=False)
+    writes[1].start()
+
+    @pl.loop(0, size // 256)
+    def _(i):
+        part = pl.ds(pl.multiple_of(i * 256, 256), 256)
+        qkv_ref[part, :] = dot(buf[part, :], w_qkv[...].reshape(width, q_part + 2 * kv_part), ((1,), (0,))).astype(jnp.bfloat16)
+
+    heads = q_part // HEAD_DIM
+    block = math.gcd(size, 256)
+    tops = [jnp.full((1, 1), NEGATIVE, jnp.float32)] * heads
+    for i in range(size // block):
+        rows, cols = pl.ds(i * block, block), (i + 1) * block
+        live = seen_mask(i * block, block, cols, q_seg_ref[rows, :], k_seg_ref[:, :cols])
+        keys, values = qkv_ref[:cols, q_part : q_part + kv_part], qkv_ref[:cols, q_part + kv_part :]
+        for h in range(heads):
+            span = slice(h * HEAD_DIM, (h + 1) * HEAD_DIM)
+            scores = dot(qkv_ref[rows, span], keys, ((1,), (1,))) * SCALE
+            scores = jnp.where(live, scores, NEGATIVE)
+            peak = jnp.max(scores, axis=-1, keepdims=True)
+            weights = jnp.exp(scores - peak)
+            total = jnp.sum(weights, axis=-1, keepdims=True)
+            out = dot(weights.astype(jnp.bfloat16), values, ((1,), (0,)))
+            attn_ref[rows, span] = (out / total).astype(jnp.bfloat16)
+            lse_ref[rows, h : h + 1] = peak + jnp.log(total)
+            tops[h] = jnp.maximum(tops[h], jnp.max(peak, axis=0, keepdims=True))
+    lanes = lax.broadcasted_iota(jnp.int32, (8, 128), 1)
+    tile = jnp.full((8, 128), NEGATIVE, jnp.float32)
+    for h in range(heads):
+        tile = jnp.where(lanes == h, tops[h], tile)
+    top_land[at.me] = tile
+    at.push_all(*top_push)
+
+    for i in range(1, line):
+        out_copy(i, lambda z: z)[1].wait_recv()
+    writes[2].start()
+    for i, chip in enumerate((at.qd, at.qx, at.qy, at.q)):
+        for core in (1 - at.core, at.core):
+            part = pl.ds(pl.multiple_of((2 * chip + core) * blk, blk), blk)
+
+            @pl.loop(0, width // 512)
+            def _(j):
+                span = pl.ds(pl.multiple_of(j * 512, 512), 512)
+                matrix = w_out[:, :, span].reshape(line * w_rows, 512)
+                term[part, span] = dot(attn_ref[part, :], matrix, ((1,), (0,))).astype(jnp.bfloat16)
+
+        reduce[0](i)
+    reduce[1](proj)
+
+    own_again = pltpu.make_async_copy(tokens_ref, land.at[pl.ds(0, blk), :], own_sem.at[0])
+    own_again.start()
+    own_again.wait()
+
+    @pl.loop(0, blk // 32)
+    def _(i):
+        part = pl.ds(pl.multiple_of(i * 32, 32), 32)
+        rows = land[part, :].astype(jnp.float32) + BRANCH * proj[part, :]
+        mid_ref[part, :] = rows
+        normed_two_ref[part, :] = (rows * rms_scale(rows) * gain_ref[1:2, :]).astype(jnp.bfloat16)
+
+    at.wait_all(*top_push, sent=False)
+    tops_ref[...] = top_land[...]
+    reduce[2]()
+    at.wait_all(*qkv_push)
+    at.wait_all(*top_push)
+    for i in range(1, line):
+        out_copy(i, lambda z: at.z)[1].wait_send()
+    for copy in writes:
+        copy.wait()
+
+
+def front(line, tokens, gains, w_qkv, w_out, q_seg, k_seg):
+    blk, width = tokens.shape
+    w_rows, cols = w_out.shape[0], w_qkv.shape[2]
+    size, every = 8 * blk, 8 * line
+    q_part = HEADS * HEAD_DIM // 8
+    kv_part = (cols - q_part) // 2
+    heads = q_part // HEAD_DIM
+    any_spec, vmem_spec = pl.BlockSpec(memory_space=pl.ANY), pl.BlockSpec(memory_space=pltpu.VMEM)
+    bf16, f32, dma, out = jnp.bfloat16, jnp.float32, pltpu.SemaphoreType.DMA, jax.ShapeDtypeStruct
+    return pl.pallas_call(
+        functools.partial(front_kernel, line, blk, q_part, kv_part),
+        out_shape=(
+            out((blk, width), f32),
+            out((blk, width), bf16),
+            out((size, cols), bf16),
+            out((size, q_part), bf16),
+            out((size, heads), f32),
+            out((every, 8, 128), f32),
+            out((8, width), f32),
+            out((size, width), bf16),
+            out((every, w_rows, cols), bf16),
+            out((line, w_rows, width), bf16),
+        ),
+        in_specs=[any_spec] * 4 + [vmem_spec] * 2,
+        out_specs=(vmem_spec,) * 7 + (any_spec,) * 3,
+        scratch_shapes=[
+            pltpu.VMEM((size, width), bf16),
+            pltpu.VMEM((size, width), bf16),
+            pltpu.VMEM((4, blk, width), bf16),
+            pltpu.VMEM((3 * blk, width), bf16),
+            pltpu.VMEM((every, w_rows, cols), bf16),
+            pltpu.VMEM((line, w_rows, width), bf16),
+            pltpu.VMEM((every, 16, 128), bf16),
+            pltpu.VMEM((every, 8, 128), f32),
+            pltpu.VMEM((blk, width), f32),
+            *[dma((n,)) for n in GATHER_SEMS + REDUCE_SEMS + (every,) * 6 + (line, line, 4, 3)],
+        ],
+        compiler_params=pltpu.CompilerParams(collective_id=1, has_side_effects=True, vmem_limit_bytes=60 * MIB),
+    )(tokens, gains, w_qkv, w_out, q_seg, k_seg)
+
+
+def back_kernel(
+    line, blk, q_part, kv_part,
+    d_attn_ref, tokens_ref, d_mid_ref, qkv_ref, attn_ref, lse_ref, gain_ref, gain_term_ref, q_seg_ref, k_seg_ref, normed_ref, w_qkv_ref, w_out_ref,
+    grad_tokens_ref, grad_qkv_ref, grad_out_ref, gain_sum_ref,
+    buf, term, core_land, land, w_qkv, w_out, normed, d_heads, d_qkv, dk_sum, dv_sum, stage_qkv, stage_out, qkv_land, out_land, gain_stage, gain_land, d_normed,
+    *sems,
+):
+    at = Place(line)
+    gather = plane_gather(at, buf, blk, sems[:6])
+    reduce = plane_reduce(at, term, core_land, land, blk, sems[6:12])
+    qkv_send, qkv_recv, gain_send, gain_recv, out_send, out_recv, own_sem = sems[12:]
+    width = buf.shape[1]
+    w_rows = w_out.shape[1]
+    size = 8 * blk
+    mine = pl.ds(pl.multiple_of(at.c * blk, blk), blk)
+    own = [
+        pltpu.make_async_copy(d_attn_ref, buf.at[mine, :], own_sem.at[0]),
+        pltpu.make_async_copy(w_out_ref, w_out, own_sem.at[1]),
+        pltpu.make_async_copy(w_qkv_ref, w_qkv, own_sem.at[2]),
+        pltpu.make_async_copy(normed_ref, normed, own_sem.at[3]),
+    ]
+    for copy in own:
+        copy.start()
+    at.greet_all()
+    own[0].wait()
+    gather[0]()
+    gather[1]()
+    for copy in own[1:]:
+        copy.wait()
+
+    @pl.loop(0, size // 256)
+    def _(i):
+        part = pl.ds(pl.multiple_of(i * 256, 256), 256)
+        d_heads[part, :] = dot(buf[part, :], w_out[...].reshape(line * w_rows, width), ((1,), (1,))).astype(jnp.bfloat16)
+
+    @pl.loop(0, width // 256)
+    def _(i):
+        span = pl.ds(pl.multiple_of(i * 256, 256), 256)
+        stage_out[:, :, span] = dot(attn_ref[...], buf[:, span], ((0,), (0,))).astype(jnp.bfloat16).reshape(line, w_rows, 256)
+
+    def out_copy(i):
+        z = lax.rem(at.z + i, line)
+        return remote(stage_out.at[z], out_land.at[at.z], out_send.at[z], out_recv.at[at.z], (at.c, z))
+
+    def out_arrival(i):
+        z = lax.rem(at.z + i, line)
+        return remote(stage_out.at[z], out_land.at[z], out_send.at[z], out_recv.at[z], (at.c, z))
+
+    for i in range(1, line):
+        out_copy(i).start()
+
+    heads = q_part // HEAD_DIM
+    block = math.gcd(size, 256)
+    dk_sum[...] = jnp.zeros_like(dk_sum)
+    dv_sum[...] = jnp.zeros_like(dv_sum)
+    for i in range(size // block):
+        rows, cols = pl.ds(i * block, block), (i + 1) * block
+        live = seen_mask(i * block, block, cols, q_seg_ref[rows, :], k_seg_ref[:, :cols])
+        keys, values = qkv_ref[:cols, q_part : q_part + kv_part], qkv_ref[:cols, q_part + kv_part :]
+        for h in range(heads):
+            span = slice(h * HEAD_DIM, (h + 1) * HEAD_DIM)
+            queries, d_out = qkv_ref[rows, span], d_heads[rows, span]
+            delta = jnp.sum(d_out.astype(jnp.float32) * attn_ref[rows, span].astype(jnp.float32), axis=-1, keepdims=True)
+            scores = dot(queries, keys, ((1,), (1,))) * SCALE
+            probs = jnp.where(live, jnp.exp(scores - lse_ref[rows, h : h + 1]), 0.0)
+            d_probs = dot(d_out, values, ((1,), (1,)))
+            d_scores = (probs * (d_probs - delta)).astype(jnp.bfloat16)
+            d_qkv[rows, span] = (dot(d_scores, keys, ((1,), (0,))) * SCALE).astype(jnp.bfloat16)
+            dk_sum[:cols, :] += dot(d_scores, queries, ((0,), (0,)))
+            dv_sum[:cols, :] += dot(probs.astype(jnp.bfloat16), d_out, ((0,), (0,)))
+    d_qkv[:, q_part : q_part + kv_part] = (dk_sum[...] * SCALE).astype(jnp.bfloat16)
+    d_qkv[:, q_part + kv_part :] = dv_sum[...].astype(jnp.bfloat16)
+
+    for i, chip in enumerate((at.qd, at.qx, at.qy, at.q)):
+        for core in (1 - at.core, at.core):
+            part = pl.ds(pl.multiple_of((2 * chip + core) * blk, blk), blk)
+
+            @pl.loop(0, width // 512)
+            def _(j):
+                span = pl.ds(pl.multiple_of(j * 512, 512), 512)
+                matrix = w_qkv[pl.ds(pl.multiple_of(j * (512 // w_rows), 512 // w_rows), 512 // w_rows)].reshape(512, q_part + 2 * kv_part)
+                term[part, span] = dot(d_qkv[part, :], matrix, ((1,), (1,))).astype(jnp.bfloat16)
+
+        reduce[0](i)
+
+    @pl.loop(0, width // 256)
+    def _(i):
+        span = pl.ds(pl.multiple_of(i * 256, 256), 256)
+        blocks = pl.ds(pl.multiple_of(i * (256 // w_rows), 256 // w_rows), 256 // w_rows)
+        grads = dot(normed[:, span], d_qkv[...], ((0,), (0,))).astype(jnp.bfloat16)
+        stage_qkv[blocks] = grads.reshape(256 // w_rows, w_rows, q_part + 2 * kv_part)
+
+    qkv_push = (lambda other: stage_qkv.at[other], lambda slot: qkv_land.at[slot], qkv_send, qkv_recv)
+    at.push_all(*qkv_push)
+    qkv_land[at.me] = stage_qkv[at.me]
+    out_land[at.z] = stage_out[at.z]
+    reduce[1](d_normed)
+
+    gain_stage[...] = jnp.zeros_like(gain_stage)
+    gain_stage[1:2, :] = gain_term_ref[...]
+
+    @pl.loop(0, blk // 32)
+    def _(i):
+        part = pl.ds(pl.multiple_of(i * 32, 32), 32)
+        rows = tokens_ref[part, :].astype(jnp.float32)
+        d_rows, gain_term = norm_backward(d_normed[part, :], rows, rms_scale(rows), gain_ref[0:1, :])
+        grad_tokens_ref[part, :] = d_mid_ref[part, :] + d_rows
+        gain_stage[0:1, :] += gain_term.reshape(1, width)
+
+    def gain_tile(other):
+        return gain_stage.at[:, pl.ds(pl.multiple_of((other // 2) * 128, 128), 128)]
+
+    gain_push = (gain_tile, lambda slot: gain_land.at[slot], gain_send, gain_recv)
+    at.push_all(*gain_push)
+    gain_land[at.me] = gain_stage[:, pl.ds(pl.multiple_of((at.me // 2) * 128, 128), 128)]
+
+    for i in range(1, line):
+        out_arrival(i).wait_recv()
+    total = out_land[0].astype(jnp.float32)
+    for i in range(1, line):
+        total = total + out_land[i].astype(jnp.float32)
+    grad_out_ref[...] = total
+    at.wait_all(*qkv_push, sent=False)
+
+    @pl.loop(0, 8)
+    def _(i):
+        total = qkv_land[i * line].astype(jnp.float32)
+        for j in range(1, line):
+            total = total + qkv_land[i * line + j].astype(jnp.float32)
+        grad_qkv_ref[i] = total
+
+    at.wait_all(*gain_push, sent=False)
+    gain_sum_ref[...] = jnp.sum(gain_land[...], axis=0)
+    gather[2]()
+    reduce[2]()
+    at.wait_all(*qkv_push)
+    at.wait_all(*gain_push)
+    for i in range(1, line):
+        out_copy(i).wait_send()
+
+
+def back(line, d_attn, tokens, d_mid, qkv, attn_out, lse, gain, gain_term, q_seg, k_seg, normed, w_qkv, w_out):
+    blk, width = tokens.shape
+    w_rows, cols = w_out.shape[1], w_qkv.shape[2]
+    size, every = 8 * blk, 8 * line
+    q_part = HEADS * HEAD_DIM // 8
+    kv_part = (cols - q_part) // 2
+    any_spec, vmem_spec = pl.BlockSpec(memory_space=pl.ANY), pl.BlockSpec(memory_space=pltpu.VMEM)
+    bf16, f32, dma, out = jnp.bfloat16, jnp.float32, pltpu.SemaphoreType.DMA, jax.ShapeDtypeStruct
+    return pl.pallas_call(
+        functools.partial(back_kernel, line, blk, q_part, kv_part),
+        out_shape=(out((blk, width), f32), out((8, w_rows, cols), f32), out((w_rows, width), f32), out((8, 128), f32)),
+        in_specs=[any_spec] + [vmem_spec] * 9 + [any_spec] * 3,
+        out_specs=(vmem_spec,) * 4,
+        scratch_shapes=[
+            pltpu.VMEM((size, width), bf16),
+            pltpu.VMEM((size, width), bf16),
+            pltpu.VMEM((4, blk, width), bf16),
+            pltpu.VMEM((3 * blk, width), bf16),
+            pltpu.VMEM((every, w_rows, cols), bf16),
+            pltpu.VMEM((line, w_rows, width), bf16),
+            pltpu.VMEM((size, width), bf16),
+            pltpu.VMEM((size, q_part), bf16),
+            pltpu.VMEM((size, cols), bf16),
+            pltpu.VMEM((size, kv_part), f32),
+            pltpu.VMEM((size, kv_part), f32),
+            pltpu.VMEM((every, w_rows, cols), bf16),
+            pltpu.VMEM((line, w_rows, width), bf16),
+            pltpu.VMEM((every, w_rows, cols), bf16),
+            pltpu.VMEM((line, w_rows, width), bf16),
+            pltpu.VMEM((8, width), f32),
+            pltpu.VMEM((every, 8, 128), f32),
+            pltpu.VMEM((blk, width), f32),
+            *[dma((n,)) for n in GATHER_SEMS + REDUCE_SEMS + (every,) * 4 + (line, line, 4)],
+        ],
+        compiler_params=pltpu.CompilerParams(collective_id=2, has_side_effects=True, vmem_limit_bytes=60 * MIB),
+    )(d_attn, tokens, d_mid, qkv, attn_out, lse, gain, gain_term, q_seg, k_seg, normed, w_qkv, w_out)
 
 
 def split_heads(w, parts):
@@ -614,11 +1111,24 @@
     clip = CLIP_TARGET / jnp.maximum(head_top, CLIP_TARGET)
 
     scale_two = rms_scale(mid)
-    d_mlp = (BRANCH * grad_rows).astype(jnp.bfloat16)
-    normed_two = (mid * scale_two * gain_two).astype(jnp.bfloat16)
-    mlp = functools.partial(mlp_exchange, n_shard) if n_ctx == 8 else mlp_lax
-    mlp_proj, d_normed_two, gate_up_grad, grad_down = mlp(normed_two, d_mlp, gate_up_mine, w_down)
-    mixed = (mid + BRANCH * mlp_proj).astype(jnp.bfloat16).reshape(1, count, width)
+    d_mlp = lax.all_gather((BRANCH * grad_rows).astype(jnp.bfloat16), EVERY, axis=0, tiled=True)
+    normed_two = lax.all_gather((mid * scale_two * gain_two).astype(jnp.bfloat16), EVERY, axis=0, tiled=True)
+    gate_up = dot(normed_two, gate_up_mine, ((1,), (0,)))
+    gate, up = gate_up[:, :ff_part], gate_up[:, ff_part:]
+    sigma = jax.nn.sigmoid(gate)
+    active = gate * sigma
+    hidden = (active * up).astype(jnp.bfloat16)
+    down_term = dot(hidden, w_down, ((1,), (0,))).astype(jnp.bfloat16)
+    d_hidden = dot(d_mlp, w_down, ((1,), (1,)))
+    d_gate = d_hidden * up * sigma * (1.0 + gate * (1.0 - sigma))
+    d_up = d_hidden * active
+    d_gate_up = jnp.concatenate([d_gate, d_up], axis=1).astype(jnp.bfloat16)
+    normed_term = dot(d_gate_up, gate_up_mine, ((1,), (1,))).astype(jnp.bfloat16)
+    grad_down = dot(hidden, d_mlp, ((0,), (0,)))
+    gate_up_grad = dot(normed_two, d_gate_up, ((0,), (0,))).astype(jnp.bfloat16)
+    mlp_proj = lax.psum_scatter(down_term, EVERY, scatter_dimension=0, tiled=True)
+    mixed = (mid + BRANCH * mlp_proj.astype(jnp.float32)).astype(jnp.bfloat16).reshape(1, count, width)
+    d_normed_two = lax.psum_scatter(normed_term, EVERY, scatter_dimension=0, tiled=True).astype(jnp.float32)
     grad_gate_up = lax.all_to_all(gate_up_grad.reshape(n * w_rows, 2, 1, ff_part), EVERY, split_axis=0, concat_axis=2, tiled=True)
     grad_gate_up = grad_gate_up.reshape(w_rows, 2 * n * ff_part).astype(jnp.float32)
     d_mid_norm, gain_two_term = norm_backward(d_normed_two, mid, scale_two, gain_two)
@@ -641,10 +1151,54 @@
     return (mixed, grad_tokens, grad_qkv, grad_out, grad_gate_up, grad_down, gain_terms[0], gain_terms[1], clip)
 
 
+def on_planes(n_shard, tokens, lengths, cotangent, w_qkv, w_out, w_gate_up, w_down, gain_attn, gain_mlp):
+    count, width = tokens.shape[1:]
+    n = 8 * n_shard
+    w_rows = w_qkv.shape[0]
+    ff_part = w_down.shape[0]
+    rows = tokens.reshape(count, width)
+    grad_rows = cotangent.reshape(count, width).astype(jnp.float32)
+    size = count * 8
+    seg = segment_ids(jnp.arange(size, dtype=jnp.int32), lengths[0])
+    q_seg, k_seg = seg.reshape(size, 1), seg.reshape(1, size)
+    side = lax.rem(lax.axis_index("ctx") * n_shard + lax.axis_index("shard"), 2)
+
+    gains = jnp.stack([gain_attn, gain_mlp])
+    none = jnp.zeros_like(gains)
+    gains = jnp.where(side == 0, jnp.concatenate([gains, none], axis=1), jnp.concatenate([none, gains], axis=1))
+    gains = jnp.pad(gains, ((0, 14), (0, 0)))
+    mid, normed_two, qkv, attn_out, lse, tops, gain, normed_one, qkv_mine, out_mine = front(
+        n_shard, rows, gains, split_heads(w_qkv, 8).transpose(1, 0, 2), w_out, q_seg, k_seg
+    )
+    heads = HEADS // 8
+    head_top = jnp.max(tops[:, 0, :heads].reshape(8, n_shard, heads), axis=1).reshape(HEADS)
+    clip = CLIP_TARGET / jnp.maximum(head_top, CLIP_TARGET)
+
+    gate_up_mine = lax.all_to_all(w_gate_up.reshape(w_rows, 2, n, ff_part), EVERY, split_axis=2, concat_axis=0, tiled=True)
+    gate_up_mine = gate_up_mine.reshape(width, 2 * ff_part)
+    d_mlp = (BRANCH * grad_rows).astype(jnp.bfloat16)
+    mlp_proj, d_normed_two, gate_up_grad, grad_down = mlp_exchange(n_shard, normed_two, d_mlp, gate_up_mine, w_down)
+    mixed = (mid + BRANCH * mlp_proj).astype(jnp.bfloat16).reshape(1, count, width)
+    grad_gate_up = lax.all_to_all(gate_up_grad.reshape(n * w_rows, 2, 1, ff_part), EVERY, split_axis=0, concat_axis=2, tiled=True)
+    grad_gate_up = grad_gate_up.reshape(w_rows, 2 * n * ff_part).astype(jnp.float32)
+    d_mid_norm, gain_two_term = norm_backward(d_normed_two, mid, rms_scale(mid), gain[1:2])
+    d_mid = grad_rows + d_mid_norm
+
+    d_attn = (BRANCH * d_mid).astype(jnp.bfloat16)
+    grad_tokens, qkv_grad, grad_out, gain_sum = back(
+        n_shard, d_attn, rows, d_mid, qkv, attn_out, lse, gain, gain_two_term.reshape(1, width), q_seg, k_seg, normed_one, qkv_mine, out_mine
+    )
+    grad_qkv = join_heads(qkv_grad.transpose(1, 0, 2), 8)
+    gain_grads = jnp.where(side == 0, gain_sum[:2, :w_rows], gain_sum[:2, w_rows : 2 * w_rows])
+    return (mixed, grad_tokens.reshape(1, count, width), grad_qkv, grad_out, grad_gate_up, grad_down, gain_grads[0], gain_grads[1], clip)
+
+
 def solution(mesh):
     by_token, by_row = P("shard", "ctx", None), P(EVERY, None)
+    n_ctx, n_shard = mesh.shape["ctx"], mesh.shape["shard"]
+    program = functools.partial(on_planes, n_shard) if n_ctx == 8 else functools.partial(per_device, n_ctx, n_shard)
     return jax.shard_map(
-        functools.partial(per_device, mesh.shape["ctx"], mesh.shape["shard"]),
+        program,
         mesh=mesh,
         in_specs=(by_token, P("shard", None), by_token, by_row, by_row, by_row, by_row, P(EVERY), P(EVERY)),
         out_specs=(by_token, by_token, by_row, by_row, by_row, by_row, P(EVERY), P(EVERY), P()),

time: 935 us -> 612 us (0.65)
  waiting for transfers between devices: 365 us -> 0.01 us
  Pallas kernels: 337 us -> 551 us
  blocking collectives: 104 us -> 0 us
  matrix products: 28.4 us -> 0 us
  between operations: 15.4 us -> 1.13 us
  other arithmetic: 20 us -> 9.09 us
  local copies, waits for them, and re-layouts: 40.9 us -> 30.9 us
    pallas_call x2, Pallas kernels: 17.2 us -> 248 us  [the longest x1 136 us: front(): pl.pallas_call(functools.partial(front_kernel, line, blk, q_part, kv_part...]
    unnamed x10 -> x0, waiting for transfers between devices: 131 us -> none
    reduce_scatter x4 -> x0, waiting for transfers between devices: 105 us -> none  [the longest x1 50.5 us: per_device(): lax.psum_scatter(qkv_term, 'ctx', scatter_dimension=0, tiled=True)]
    all_gather x4 -> x0, waiting for transfers between devices: 82.1 us -> none  [the longest x1 35.3 us: per_device(): lax.all_gather((BRANCH * d_mid).astype(jnp.bfloat16), 'ctx', axis=0, tile...]
    all_gather x1 -> x0, blocking collectives: 66.4 us -> none  [per_device(): lax.all_gather(jnp.stack([gain_attn, gain_mlp]), EVERY, axis=1, tiled=True)]
    all_to_all x3 -> x2, waiting for transfers between devices: 46.6 us -> 0.01 us  [the longest x1 0.01 us: on_planes(): lax.all_to_all(w_gate_up.reshape(w_rows, 2, n, ff_part), EVERY, split_axi...]
    dot_general x6 -> x0, matrix products: 28.4 us -> none  [dot(): lax.dot_general(left, right, ((dims[0], dims[1]), ((), ())), preferred_el...]
    pallas_call x1, Pallas kernels: 320 us -> 303 us  [mlp_exchange(): pl.pallas_call(functools.partial(mlp_kernel, line, blk, part), out_shape=...]
  transfers between devices with their start and end apart: 12 -> 2, of which waited for: 8 -> 0; matrix products, arithmetic and copies ran while one was open for 6% -> 2% of each run, Pallas kernels for 1% -> 41%
where the time goes in v3:
time: 612 us; the launch traced here: 608 us
  Pallas kernels  551 us (90%)
  local copies, waits for them, and re-layouts  30.9 us (5%)
  starting transfers between devices  16 us (3%)
  other arithmetic  9.09 us (1%)
    pallas_call x1, Pallas kernels, mlp_exchange(): pl.pallas_call(functools.partial(mlp_kernel, line, blk, part), out_shape=...  303 us
    pallas_call x1, Pallas kernels, front(): pl.pallas_call(functools.partial(front_kernel, line, blk, q_part, kv_part...  136 us
    pallas_call x1, Pallas kernels, back(): pl.pallas_call(functools.partial(back_kernel, line, blk, q_part, kv_part)...  113 us
  transfers between devices with their start and end apart: 2, of which 0 were waited for; matrix products, arithmetic and copies ran while one was open for 2% of the time, Pallas kernels for 41%

profile of v3, /device:TPU:0, one launch (start us, length us, event | category | flops | bytes accessed | tf_op | source)
XLA Modules:
  0.0 608.3 jit_solution(6821193918236572684)
XLA Ops:
  0.6 2.1 copy.62
  2.8 3.5 copy.49
  6.3 7.5 %all-to-all-start = ((bf16[64,2,32,256]{3,1,0,2:T(2,128)(2,1)}), bf16[64,2,32,256]{3,1,0,2:T(2,128)(2,1)S(1)}, u32[]{:S(2)}, u32[]{:S(2)}) async-start(bf16[64,2,32,256]{3,1,0,2:T(2,128)(2,1)} %copy.49), calls=%async_computation | async-start | bytes 4194304 | tf_op jit(solution)/shard_map/all_to_all | solution.py:1177
  13.8 0.2 reduce-window.4
  14.5 1.0 copy.48.q_seg_ref
  15.6 0.6 pad.6.gains_ref
  16.2 0.9 maximum_bitcast_fusion.w_qkv_ref
  17.1 135.6 %shard_map.160 = (f32[128,2048]{1,0:T(8,128)}, bf16[128,2048]{1,0:T(8,128)(2,1)}, bf16[1024,384]{1,0:T(8,128)(2,1)}, bf16[1024,256]{1,0:T(8,128)(2,1)}, f32[1024...) custom-call(bf16[128,2048]{1,0:T(8,128)(2,1)} %bitcast.57, ...), custom_call_target="tpu_custom_call" | custom-call | tf_op jit(solution)/shard_map/pallas_call | solution.py:839
  152.7 0.9 fusion.d_mlp_ref
  153.6 1.8 copy.63
  155.4 302.9 %shard_map.161 = (f32[128,2048]{1,0:T(8,128)}, f32[128,2048]{1,0:T(8,128)}, bf16[2048,512]{1,0:T(8,128)(2,1)}, f32[256,2048]{1,0:T(8,128)}) custom-call(bf16[128,2048]{1,0:T(8,128)(2,1)} %get-tuple-element.28.normed_ref, bf16[128,2048]{1,0:T(8,128)(2,1)} %fusion.d_mlp_ref, bf16[2048,512]{1,0:T(8,128)(2,1)} %bitcast.55, bf16[256,2048]{1,0:T(8,128)(2,1)} %down_ref.1), custom_call_target="tpu_custom_call" | custom-call | tf_op jit(solution)/shard_map/pallas_call | solution.py:486
  458.3 4.0 reshape.113
  462.3 8.5 %all-to-all-start.1 = ((bf16[2048,2,1,256]{3,1,2,0:T(2,128)(2,1)}), bf16[2048,2,1,256]{3,1,2,0:T(2,128)(2,1)S(1)}, u32[]{:S(2)}, u32[]{:S(2)}) async-start(bf16[2048,2,1,256]{3,1,2,0:T(2,128)(2,1)} %bitcast.54), calls=%async_computation.1 | async-start | bytes 4194304 | tf_op jit(solution)/shard_map/all_to_all | solution.py:1182
  470.8 0.8 slice.44
  471.6 0.9 slice.52
  472.6 0.6 div.15
  473.2 0.2 multiply_reduce_fusion.2
  473.3 2.3 multiply_reduce_fusion
  475.7 1.7 multiply_convert_fusion
  477.4 112.6 %shard_map.162 = (f32[128,2048]{1,0:T(8,128)}, f32[8,64,384]{2,1,0:T(8,128)}, f32[64,2048]{1,0:T(8,128)}, f32[8,128]{1,0:T(8,128)}) custom-call(bf16[128,2048]{1,0:T(8,128)(2,1)} %get-tuple-element.47.d_attn_ref, bf16[128,2048]{1,0:T(8,128)(2,1)} %bitcast.58, f32[128,2048]{1,0:T(8,128)} %get-tuple-element.48.d_mid_ref, ...), custom_call_target="tpu_custom_call" | custom-call | tf_op jit(solution)/shard_map/pallas_call | solution.py:1020
  590.1 1.2 fusion.2
  591.3 0.2 copy.52
  591.7 0.2 copy.53
  592.1 0.5 slice_bitcast_fusion.1
  592.6 0.9 pad_maximum_fusion
  593.5 1.8 convert_bitcast_fusion
  595.3 4.4 copy.55
  599.7 5.1 reshape.115
  604.7 1.0 copy.70
  605.7 0.8 copy.71
  606.5 0.2 copy-done.4
  606.7 1.3 copy.72
  (52 shorter events, 1.0 us)
Async XLA Ops:
  6.3 7.6 %copy-start.12 = (s32[1,9]{1,0:T(1,128)S(1)}, s32[1,9]{1,0:T(1,128)}, u32[]{:S(2)}) copy-start(s32[1,9]{1,0:T(1,128)} %param.10) | copy-start | bytes 112
  6.3 7.8 %copy-start.8 = (bf16[64,3072]{1,0:T(8,128)(2,1)S(1)}, bf16[64,3072]{1,0:T(8,128)(2,1)}, u32[]{:S(2)}) copy-start(bf16[64,3072]{1,0:T(8,128)(2,1)} %param.12) | copy-start | bytes 1179652
  6.3 8.1 %slice-start = ((bf16[64,3072]{1,0:T(8,128)(2,1)}), bf16[64,2048]{1,0:T(8,128)(2,1)S(1)}, s32[]{:S(2)}) async-start(bf16[64,3072]{1,0:T(8,128)(2,1)} %param.12), calls=%async_computation.2 | async-start | bytes 524288 | tf_op jit(solution)/shard_map/slice | solution.py:1054
  6.3 147.4 %all-to-all-start = ((bf16[64,2,32,256]{3,1,0,2:T(2,128)(2,1)}), bf16[64,2,32,256]{3,1,0,2:T(2,128)(2,1)S(1)}, u32[]{:S(2)}, u32[]{:S(2)}) async-start(bf16[64,2,32,256]{3,1,0,2:T(2,128)(2,1)} %copy.49), calls=%async_computation | async-start | bytes 4194304 | tf_op jit(solution)/shard_map/all_to_all | solution.py:1177
  13.8 1.7 copy-start.13
  13.8 1.7 copy-start.14
  14.2 138.5 %copy-start.2 = (bf16[1,128,2048]{2,1,0:T(8,128)(2,1)S(1)}, bf16[1,128,2048]{2,1,0:T(8,128)(2,1)}, u32[]{:S(2)}) copy-start(bf16[1,128,2048]{2,1,0:T(8,128)(2,1)} %param.11) | copy-start | bytes 1572868
  14.5 2.6 copy-start.10
  462.3 10.9 %copy-start = (f32[128,2048]{1,0:T(8,128)S(1)}, f32[128,2048]{1,0:T(8,128)}, u32[]{:S(2)}) copy-start(f32[128,2048]{1,0:T(8,128)} %get-tuple-element.27) | copy-start | bytes 3145732
  462.3 131.2 %all-to-all-start.1 = ((bf16[2048,2,1,256]{3,1,2,0:T(2,128)(2,1)}), bf16[2048,2,1,256]{3,1,2,0:T(2,128)(2,1)S(1)}, u32[]{:S(2)}, u32[]{:S(2)}) async-start(bf16[2048,2,1,256]{3,1,2,0:T(2,128)(2,1)} %bitcast.54), calls=%async_computation.1 | async-start | bytes 4194304 | tf_op jit(solution)/shard_map/all_to_all | solution.py:1182
  473.2 2.5 copy-start.1
  473.2 2.5 copy-start.3
  473.2 2.5 copy-start.6
  590.1 1.5 copy-start.5
  591.3 0.7 copy-start.11
  599.7 5.1 copy-start.7
  599.7 6.0 copy-start.9
  604.7 2.0 copy-start.4

commit v4 on v3

--- a/solution.py
+++ b/solution.py
@@ -156,150 +156,305 @@
             keep[part, :] = total
 
 
-def mlp_kernel(
-    line, blk, part, normed_ref, d_mlp_ref, gate_up_ref, down_ref,
-    mlp_ref, d_normed_ref, gate_up_grad_ref, down_grad_ref,
-    act, land, line_land, w_gu, w_down, acc_gu, acc_down, hid, d_gu, sib_gu, sib_down,
-    z_send, z_recv, p_send, p_recv, f_send, f_recv, r2_send, r2_recv, r3_send, r3_recv, r4_send, r4_recv,
-    w_send, w_recv, g_send, g_recv, own_sem, out_sem,
-):
-    c, z = lax.axis_index("ctx"), lax.axis_index("shard")
-    q, core = c // 2, c % 2
-    half = blk // 2
-    width = w_down.shape[1]
-    slot_rows = 4 * blk
-    cx, cy, sibling = (c + 2 - 4 * (q % 2), z), (c + 4 - 8 * (q // 2), z), (c + 1 - 2 * core, z)
-    qx, qy = q + 1 - 2 * (q % 2), q + 2 - 4 * (q // 2)
-    qd = 3 - q
-    up, down = (c, z + 1), (c, z - 1)
-    has_up, has_down = z < line - 1, z > 0
-
-    def source(k):
-        if line == 1:
-            return z * 0
-        mirrored = z >= line // 2
-        near = jnp.where(mirrored, line - 1 - z, z)
+class Place:
+    def __init__(self, line):
+        self.line = line
+        self.c, self.z = lax.axis_index("ctx"), lax.axis_index("shard")
+        self.q, self.core = self.c // 2, self.c % 2
+        self.me = self.c * line + self.z
+        self.every = 8 * line
+        self.cx, self.cy = (self.c + 2 - 4 * (self.q % 2), self.z), (self.c + 4 - 8 * (self.q // 2), self.z)
+        self.sibling = (self.c + 1 - 2 * self.core, self.z)
+        self.qx, self.qy, self.qd = self.q + 1 - 2 * (self.q % 2), self.q + 2 - 4 * (self.q // 2), 3 - self.q
+
+    def source(self, k):
+        if self.line == 1:
+            return self.z * 0
+        mirrored = self.z >= self.line // 2
+        near = jnp.where(mirrored, self.line - 1 - self.z, self.z)
         turn = (k + 1) // 2
         both = near - turn if k % 2 == 1 else near + turn
         at = jnp.where(k <= 2 * near, both, k)
-        return jnp.where(mirrored, line - 1 - at, at)
-
-    def block(at, chip):
-        return pl.multiple_of((at * 4 + chip) * blk, blk)
-
-    def rows(tensor, at, chip, first=0, count=blk):
-        return act.at[tensor, pl.ds(pl.multiple_of(block(at, chip) + first, half), count), :]
-
-    greet([cx, cy, sibling], [(has_up, up), (has_down, down)])
-
-    own = [
-        pltpu.make_async_copy(normed_ref, rows(0, z, q), own_sem.at[0]),
-        pltpu.make_async_copy(d_mlp_ref, rows(1, z, q), own_sem.at[1]),
-    ]
-    mine = [pl.ds(pl.multiple_of(core * part + extra, part), part) for extra in (0, 2 * part)]
-    own_weights = [
-        pltpu.make_async_copy(gate_up_ref.at[:, :part], w_gu.at[:, mine[0]], own_sem.at[2]),
-        pltpu.make_async_copy(gate_up_ref.at[:, part:], w_gu.at[:, mine[1]], own_sem.at[3]),
-        pltpu.make_async_copy(down_ref, w_down.at[mine[0], :], own_sem.at[4]),
-    ]
-    to_sibling = [
-        remote(gate_up_ref.at[:, :part], w_gu.at[:, mine[0]], w_send.at[0], w_recv.at[0], sibling),
-        remote(gate_up_ref.at[:, part:], w_gu.at[:, mine[1]], w_send.at[1], w_recv.at[1], sibling),
-        remote(down_ref, w_down.at[mine[0], :], w_send.at[2], w_recv.at[2], sibling),
-    ]
-    theirs = [pl.ds(pl.multiple_of((1 - core) * part + extra, part), part) for extra in (0, 2 * part)]
-    from_sibling = [
-        remote(gate_up_ref.at[:, :part], w_gu.at[:, theirs[0]], w_send.at[0], w_recv.at[0], sibling),
-        remote(gate_up_ref.at[:, part:], w_gu.at[:, theirs[1]], w_send.at[1], w_recv.at[1], sibling),
-        remote(down_ref, w_down.at[theirs[0], :], w_send.at[2], w_recv.at[2], sibling),
-    ]
-
-    def line_copy(tensor, at, way):
-        ref = rows(tensor, at, q)
-        return remote(ref, ref, z_send.at[tensor, at, way], z_recv.at[tensor, at], (up, down)[way])
-
-    def plane_copies(tensor, at):
-        copies = []
-        for i, (device, first) in enumerate(((cx, 0), (cy, half), (cx, half), (cy, 0))):
-            ref = rows(tensor, at, q, first, half)
-            copies.append(remote(ref, ref, p_send.at[tensor, at, i], p_recv.at[tensor, at, i], device))
-        return copies
-
-    def plane_arrivals(tensor, at):
-        arrivals = []
-        for i, (device, chip, first) in enumerate(((cx, qx, 0), (cy, qy, half), (cx, qx, half), (cy, qy, 0))):
-            ref = rows(tensor, at, chip, first, half)
-            arrivals.append(remote(ref, ref, p_send.at[tensor, at, i], p_recv.at[tensor, at, i], device))
-        return arrivals
-
-    def onward_copies(tensor, at):
-        first, second = rows(tensor, at, qx, 0, half), rows(tensor, at, qy, half, half)
-        return [
-            remote(first, first, f_send.at[tensor, at, 0], f_recv.at[tensor, at, 0], cy),
-            remote(second, second, f_send.at[tensor, at, 1], f_recv.at[tensor, at, 1], cx),
-        ]
-
-    def onward_arrivals(tensor, at):
-        first, second = rows(tensor, at, qd, 0, half), rows(tensor, at, qd, half, half)
-        return [
-            remote(first, first, f_send.at[tensor, at, 0], f_recv.at[tensor, at, 0], cy),
-            remote(second, second, f_send.at[tensor, at, 1], f_recv.at[tensor, at, 1], cx),
-        ]
-
-    def send_line(tensor, at, condition, way):
-        @pl.when(condition)
-        def _():
-            line_copy(tensor, at, way).start()
-
-    def wait_line(tensor, at, condition, way):
-        @pl.when(condition)
-        def _():
-            line_copy(tensor, at, way).wait_send()
-
-    def step_a(k):
-        at = source(k)
-        for tensor in (0, 1):
-            if k > 0:
-                line_copy(tensor, at, 0).wait_recv()
-                send_line(tensor, at, (at < z) & has_up, 0)
-                send_line(tensor, at, (at > z) & has_down, 1)
-            for copy in plane_copies(tensor, at):
-                copy.start()
-
-    def step_b(k):
-        at = source(k)
-        for tensor in (0, 1):
-            arrivals = plane_arrivals(tensor, at)
-            onward = onward_copies(tensor, at)
-            for i in (0, 1):
-                arrivals[i].wait_recv()
-                onward[i].start()
-
-    def step_c(k):
-        at = source(k)
-        for tensor in (0, 1):
-            for copy in plane_arrivals(tensor, at)[2:] + onward_arrivals(tensor, at):
+        return jnp.where(mirrored, self.line - 1 - at, at)
+
+    def line_spread(self, copy, k):
+        at = self.source(k)
+        if k > 0:
+            copy(at, 0).wait_recv()
+        for way, condition in enumerate(self.line_ways(at)):
+
+            @pl.when(condition)
+            def _():
+                copy(at, way).start()
+
+    def line_sent(self, copy, k):
+        at = self.source(k)
+        for way, condition in enumerate(self.line_ways(at)):
+
+            @pl.when(condition)
+            def _():
+                copy(at, way).wait_send()
+
+    def line_ways(self, at):
+        return ((at <= self.z) & (self.z < self.line - 1), (at >= self.z) & (self.z > 0))
+
+    def peer(self, i):
+        other = lax.rem(self.me + i, self.every)
+        return other, (other // self.line, other % self.line)
+
+    def greet_all(self):
+        barrier = pltpu.get_barrier_semaphore()
+
+        @pl.loop(1, self.every)
+        def _(i):
+            pl.semaphore_signal(barrier, inc=1, device_id=self.peer(i)[1], device_id_type=pl.DeviceIdType.MESH)
+
+        pl.semaphore_wait(barrier, self.every - 1)
+
+    def push_all(self, source, target, send_sems, recv_sems):
+        @pl.loop(1, self.every)
+        def _(i):
+            other, device = self.peer(i)
+            remote(source(other), target(self.me), send_sems.at[other], recv_sems.at[self.me], device).start()
+
+    def wait_all(self, source, target, send_sems, recv_sems, sent=True):
+        @pl.loop(1, self.every)
+        def _(i):
+            other, device = self.peer(i)
+            copy = remote(source(other), target(other), send_sems.at[other], recv_sems.at[other], device)
+            if sent:
+                copy.wait_send()
+            else:
                 copy.wait_recv()
-            for copy in plane_copies(tensor, at) + onward_copies(tensor, at):
-                copy.wait_send()
-            wait_line(tensor, at, (at <= z) & has_up, 0)
-            wait_line(tensor, at, (at >= z) & has_down, 1)
+
+
+class SliceGather:
+    def __init__(self, place, rows, blk, sems):
+        self.place, self.rows, self.half = place, rows, blk // 2
+        self.z_send, self.z_recv, self.p_send, self.p_recv, self.f_send, self.f_recv = sems
+        p, half = place, blk // 2
+        self.ways = ((p.cx, p.qx, 0), (p.cy, p.qy, half), (p.cx, p.qx, half), (p.cy, p.qy, 0))
+        self.turns = ((p.qx, 0, p.cy), (p.qy, half, p.cx))
+
+    def line_copy(self, at, way):
+        ref = self.rows(at, self.place.q, 0, 2 * self.half)
+        return remote(ref, ref, self.z_send.at[at, way], self.z_recv.at[at], (self.place.c, self.place.z + 1 - 2 * way))
+
+    def plane_copy(self, at, i, arriving=False):
+        device, chip, first = self.ways[i]
+        ref = self.rows(at, chip if arriving else self.place.q, first, self.half)
+        return remote(ref, ref, self.p_send.at[at, i], self.p_recv.at[at, i], device)
+
+    def onward_copy(self, at, i, arriving=False):
+        chip, first, device = self.turns[i]
+        ref = self.rows(at, self.place.qd if arriving else chip, first, self.half)
+        return remote(ref, ref, self.f_send.at[at, i], self.f_recv.at[at, i], device)
+
+    def a(self, k):
+        self.place.line_spread(self.line_copy, k)
+        for i in range(4):
+            self.plane_copy(self.place.source(k), i).start()
+
+    def b(self, k):
+        at = self.place.source(k)
+        for i in (0, 1):
+            self.plane_copy(at, i, True).wait_recv()
+            self.onward_copy(at, i).start()
+
+    def c(self, k):
+        at = self.place.source(k)
+        for i in (2, 3):
+            self.plane_copy(at, i, True).wait_recv()
+        for i in (0, 1):
+            self.onward_copy(at, i, True).wait_recv()
+        for i in range(4):
+            self.plane_copy(at, i).wait_send()
+        for i in (0, 1):
+            self.onward_copy(at, i).wait_send()
+        self.place.line_sent(self.line_copy, k)
+
+
+def slice_gather_sems(line):
+    return [pltpu.SemaphoreType.DMA(shape) for shape in ((line, 2), (line,), (line, 4), (line, 4), (line, 2), (line, 2))]
+
+
+class SliceReduce:
+    def __init__(self, place, rows, blk, land, line_land, result, sems):
+        self.place, self.rows, self.blk, self.half = place, rows, blk, blk // 2
+        self.land, self.line_land, self.result = land, line_land, result
+        self.r2_send, self.r2_recv, self.r3_send, self.r3_recv, self.r4_send, self.r4_recv = sems
+        p, half = place, blk // 2
+        self.seconds = ((0, p.cy), (half, p.cx))
+        self.thirds = ((p.cx, p.qx, 0, 0), (p.cy, p.qy, half, blk + half), (p.cx, p.qx, half, half), (p.cy, p.qy, 0, blk))
+
+    def landing(self, at, first, count):
+        return self.land.at[at, pl.ds(first, count), :]
+
+    def second(self, at, i):
+        first, device = self.seconds[i]
+        return remote(
+            self.rows(at, self.place.qd, first, self.half), self.landing(at, 2 * self.blk + first, self.half), self.r2_send.at[at, i], self.r2_recv.at[at, i], device
+        )
+
+    def third(self, at, i):
+        device, chip, first, lands = self.thirds[i]
+        return remote(
+            self.rows(at, chip, first, self.half), self.landing(at, lands, self.half), self.r3_send.at[at, i], self.r3_recv.at[at, i], device
+        )
+
+    def line_copy(self, at, way):
+        p = self.place
+        slot = jnp.where((way == 1) & (at == p.z - 1), p.line, at)
+        return remote(
+            self.rows(at, p.q, 0, self.blk), self.line_land.at[slot], self.r4_send.at[at], self.r4_recv.at[slot], (p.c, p.z + 1 - 2 * way)
+        )
+
+    def line_arrival(self, at, slot):
+        return remote(self.rows(at, self.place.q, 0, self.blk), self.line_land.at[slot], self.r4_send.at[at], self.r4_recv.at[slot], self.place.sibling)
+
+    def a(self, k):
+        at = self.place.source(k)
+        for i in (0, 1):
+            self.second(at, i).start()
+        for i in (2, 3):
+            self.third(at, i).start()
+
+    def b(self, k):
+        at = self.place.source(k)
+        for i in (0, 1):
+            chip, first = self.thirds[i][1:3]
+            self.second(at, i).wait_recv()
+            add_rows(self.rows(at, chip, first, self.half), [self.landing(at, 2 * self.blk + first, self.half)], self.half)
+            self.third(at, i).start()
+
+    def c(self, k):
+        p, blk = self.place, self.blk
+        at = p.source(k)
+        has_up, has_down = p.z < p.line - 1, p.z > 0
+        for i in range(4):
+            self.third(at, i).wait_recv()
+        mine = self.rows(at, p.q, 0, blk)
+        plane = [self.landing(at, 0, blk), self.landing(at, blk, blk)]
+        if k > 0:
+            joined = ((at > p.z) & has_down) | ((at < p.z) & has_up)
+
+            @pl.when(joined)
+            def _():
+                self.line_arrival(at, at).wait_recv()
+                add_rows(mine, plane + [self.line_land.at[at]], blk)
+
+            @pl.when(jnp.logical_not(joined))
+            def _():
+                add_rows(mine, plane, blk)
+
+            for way, condition in enumerate((at > p.z, at < p.z)):
+
+                @pl.when(condition)
+                def _():
+                    self.line_copy(at, way).start()
+
+        else:
+            add_rows(mine, plane, blk, self.result)
+            for condition, slot in ((has_down, at), (has_up, p.line)):
+
+                @pl.when(condition)
+                def _():
+                    self.line_arrival(at, slot).wait_recv()
+                    add_rows(self.result, [self.line_land.at[slot]], blk, self.result)
+
+    def end(self, k):
+        at = self.place.source(k)
+        for i in (0, 1):
+            self.second(at, i).wait_send()
+        for i in range(4):
+            self.third(at, i).wait_send()
+        if k > 0:
+            self.line_copy(at, 0).wait_send()
+
+
+def slice_reduce_sems(line):
+    return [pltpu.SemaphoreType.DMA(shape) for shape in ((line, 2), (line, 2), (line, 4), (line, 4), (line,), (line + 1,))]
+
+
+def slice_rows(ref, blk):
+    def rows(at, chip, first, count):
+        return ref.at[pl.ds(pl.multiple_of((at * 4 + chip) * blk + first, blk // 2), count), :]
+
+    return rows
+
+
+def mlp_kernel(
+    line, blk, part, normed_ref, d_mlp_ref, w_gate_up_ref, down_ref,
+    mlp_term_ref, d_normed_ref, gate_up_grad_ref, down_grad_ref,
+    act, land, line_land, w_gu, w_down, acc_gu, acc_down, hid, d_gu, sib_gu, sib_down, grad_land,
+    w_send, w_recv, g_send, g_recv, c_send, c_recv, d_send, d_recv, own_sem, out_sem, *sems,
+):
+    place = Place(line)
+    core, me, sibling = place.core, place.me, place.sibling
+    width = w_down.shape[1]
+    w_rows = w_gate_up_ref.shape[0]
+    slot_rows = 4 * blk
+    rows = slice_rows(act.at[0], blk)
+    gather = SliceGather(place, rows, blk, sems[:6])
+    reduce = SliceReduce(place, rows, blk, land, line_land, d_normed_ref, sems[6:])
+
+    def slot_of(k):
+        return pl.ds(pl.multiple_of(place.source(k) * slot_rows, slot_rows), slot_rows)
+
+    own = pltpu.make_async_copy(normed_ref, rows(place.z, place.q, 0, blk), own_sem.at[0])
+    d_mlp_in = pltpu.make_async_copy(d_mlp_ref, act.at[1], own_sem.at[1])
+    mine = pl.ds(pl.multiple_of(core * 2 * part, 2 * part), 2 * part)
+    theirs = pl.ds(pl.multiple_of((1 - core) * 2 * part, 2 * part), 2 * part)
+    mine_rows = pl.ds(pl.multiple_of(core * part, part), part)
+    their_rows = pl.ds(pl.multiple_of((1 - core) * part, part), part)
+
+    def columns(other, i):
+        return w_gate_up_ref.at[:, pl.ds(pl.multiple_of((i * place.every + other) * part, part), part)]
+
+    def column_place(other, slot, i):
+        first = ((other // line) % 2) * 2 * part + i * part
+        return w_gu.at[pl.ds(pl.multiple_of(slot * w_rows, w_rows), w_rows), pl.ds(pl.multiple_of(first, part), part)]
+
+    def send_columns():
+        @pl.loop(1, place.every)
+        def _(i):
+            other, device = place.peer(i)
+            for j in (0, 1):
+                remote(columns(other, j), column_place(other, me, j), c_send.at[j, other], c_recv.at[j, me], device).start()
+
+    def wait_columns(sent):
+        @pl.loop(1, place.every)
+        def _(i):
+            other, device = place.peer(i)
+            for j in (0, 1):
+                copy = remote(columns(other, j), column_place(me, other, j), c_send.at[j, other], c_recv.at[j, other], device)
+                if sent:
+                    copy.wait_send()
+                else:
+                    copy.wait_recv()
+
+    own_weights = [pltpu.make_async_copy(columns(me, j), column_place(me, me, j), own_sem.at[2 + j]) for j in (0, 1)]
+    own_weights.append(pltpu.make_async_copy(down_ref, w_down.at[mine_rows, :], own_sem.at[4]))
+    down_to = remote(down_ref, w_down.at[mine_rows, :], w_send.at[0], w_recv.at[0], sibling)
+    down_from = remote(down_ref, w_down.at[their_rows, :], w_send.at[0], w_recv.at[0], sibling)
+    columns_to = remote(w_gu.at[:, mine], w_gu.at[:, mine], w_send.at[1], w_recv.at[1], sibling)
+    columns_from = remote(w_gu.at[:, theirs], w_gu.at[:, theirs], w_send.at[1], w_recv.at[1], sibling)
 
     def compute(k):
-        slot = pl.ds(pl.multiple_of(source(k) * slot_rows, slot_rows), slot_rows)
-        tile = 256 if part % 256 == 0 else part
-
-        @pl.loop(0, 2 * part // tile)
+        slot = slot_of(k)
+
+        @pl.loop(0, 2)
         def _(j):
-            span = pl.ds(pl.multiple_of(j * tile, tile), tile)
-            upper = pl.ds(pl.multiple_of(j * tile + 2 * part, tile), tile)
-            gate = dot(act[0, slot, :], w_gu[:, span], ((1,), (0,)))
+            span = pl.ds(pl.multiple_of(j * part, part), part)
+            lower = pl.ds(pl.multiple_of(j * 2 * part, part), part)
+            upper = pl.ds(pl.multiple_of(j * 2 * part + part, part), part)
+            gate = dot(act[0, slot, :], w_gu[:, lower], ((1,), (0,)))
             above = dot(act[0, slot, :], w_gu[:, upper], ((1,), (0,)))
             d_hidden = dot(act[1, slot, :], w_down[span, :], ((1,), (1,)))
             sigma = jax.nn.sigmoid(gate)
             active = gate * sigma
             hid[:, span] = (active * above).astype(jnp.bfloat16)
-            d_gu[:, span] = (d_hidden * above * sigma * (1.0 + gate * (1.0 - sigma))).astype(jnp.bfloat16)
+            d_gu[:, lower] = (d_hidden * above * sigma * (1.0 + gate * (1.0 - sigma))).astype(jnp.bfloat16)
             d_gu[:, upper] = (d_hidden * active).astype(jnp.bfloat16)
 
         @pl.loop(0, width // 256)
@@ -315,108 +470,32 @@
             act[1, slot, span] = dot(hid[...], w_down[:, span], ((1,), (0,))).astype(jnp.bfloat16)
             act[0, slot, span] = dot(d_gu[...], w_gu[span, :], ((1,), (1,))).astype(jnp.bfloat16)
 
-    def landing(tensor, at, first, count):
-        return land.at[tensor, at, pl.ds(first, count), :]
-
-    def second_copies(tensor, at):
-        return [
-            remote(rows(tensor, at, qd, 0, half), landing(tensor, at, 2 * blk, half), r2_send.at[tensor, at, 0], r2_recv.at[tensor, at, 0], cy),
-            remote(rows(tensor, at, qd, half, half), landing(tensor, at, 2 * blk + half, half), r2_send.at[tensor, at, 1], r2_recv.at[tensor, at, 1], cx),
-        ]
-
-    def third_copies(tensor, at):
-        copies = []
-        for i, (device, chip, first, lands) in enumerate(((cx, qx, 0, 0), (cy, qy, half, blk + half), (cx, qx, half, half), (cy, qy, 0, blk))):
-            copies.append(
-                remote(rows(tensor, at, chip, first, half), landing(tensor, at, lands, half), r3_send.at[tensor, at, i], r3_recv.at[tensor, at, i], device)
-            )
-        return copies
-
-    def reduce_a(k):
-        at = source(k)
-        for tensor in (1, 0):
-            for copy in second_copies(tensor, at) + third_copies(tensor, at)[2:]:
-                copy.start()
-
-    def reduce_b(k):
-        at = source(k)
-        for tensor in (1, 0):
-            for i, (chip, first) in enumerate(((qx, 0), (qy, half))):
-                second_copies(tensor, at)[i].wait_recv()
-                add_rows(rows(tensor, at, chip, first, half), [landing(tensor, at, 2 * blk + first, half)], half)
-                third_copies(tensor, at)[i].start()
-
-    def sum_copy(tensor, at, way):
-        place = jnp.where((way == 1) & (at == z - 1), line, at)
-        return remote(rows(tensor, at, q), line_land.at[tensor, place], r4_send.at[tensor, at], r4_recv.at[tensor, place], (up, down)[way])
-
-    def reduce_c(k):
-        at = source(k)
-        results = (d_normed_ref, mlp_ref)
-        for tensor in (1, 0):
-            for copy in third_copies(tensor, at):
-                copy.wait_recv()
-            mine_rows = rows(tensor, at, q)
-            plane = [landing(tensor, at, 0, blk), landing(tensor, at, blk, blk)]
-            if k > 0:
-                joined = ((at > z) & has_down) | ((at < z) & has_up)
-
-                @pl.when(joined)
-                def _():
-                    arrival = remote(mine_rows, line_land.at[tensor, at], r4_send.at[tensor, at], r4_recv.at[tensor, at], sibling)
-                    arrival.wait_recv()
-                    add_rows(mine_rows, plane + [line_land.at[tensor, at]], blk)
-
-                @pl.when(jnp.logical_not(joined))
-                def _():
-                    add_rows(mine_rows, plane, blk)
-
-                @pl.when(at > z)
-                def _():
-                    sum_copy(tensor, at, 0).start()
-
-                @pl.when(at < z)
-                def _():
-                    sum_copy(tensor, at, 1).start()
-
-            else:
-                add_rows(mine_rows, plane, blk, results[tensor])
-                for condition, place in ((has_down, at), (has_up, line)):
-
-                    @pl.when(condition)
-                    def _():
-                        remote(mine_rows, line_land.at[tensor, place], r4_send.at[tensor, at], r4_recv.at[tensor, place], sibling).wait_recv()
-                        add_rows(results[tensor], [line_land.at[tensor, place]], blk, results[tensor])
-
-    def reduce_end(k):
-        at = source(k)
-        for tensor in (1, 0):
-            for copy in second_copies(tensor, at) + third_copies(tensor, at):
-                copy.wait_send()
-            if k > 0:
-                sum_copy(tensor, at, 0).wait_send()
+    def term_out(k):
+        return pltpu.make_async_copy(act.at[1, slot_of(k), :], mlp_term_ref.at[slot_of(k), :], out_sem.at[2 + k])
+
+    half_gu, whole_gu = pl.ds(0, 2 * part), pl.ds(2 * part, 2 * part)
+    grad_copies = [
+        remote(w_gu.at[:, half_gu], sib_gu, g_send.at[0], g_recv.at[0], sibling),
+        remote(w_down.at[:part, :], sib_down, g_send.at[1], g_recv.at[1], sibling),
+    ]
+    down_out = pltpu.make_async_copy(acc_down.at[mine_rows, :], down_grad_ref, out_sem.at[0])
 
     def exchange_grads():
-        gate_half, up_half = theirs[0], theirs[1]
-
         @pl.loop(0, width // 256)
         def _(j):
             span = pl.ds(pl.multiple_of(j * 256, 256), 256)
-            w_gu[span, :part] = acc_gu[span, gate_half].astype(jnp.bfloat16)
-            w_gu[span, part : 2 * part] = acc_gu[span, up_half].astype(jnp.bfloat16)
-
-        w_down[:part, :] = acc_down[theirs[0], :].astype(jnp.bfloat16)
+            w_gu[span, half_gu] = acc_gu[span, theirs].astype(jnp.bfloat16)
+
+        w_down[:part, :] = acc_down[their_rows, :].astype(jnp.bfloat16)
         for copy in grad_copies:
             copy.start()
 
-    grad_copies = [
-        remote(w_gu.at[:, : 2 * part], sib_gu, g_send.at[0], g_recv.at[0], sibling),
-        remote(w_down.at[:part, :], sib_down, g_send.at[1], g_recv.at[1], sibling),
-    ]
-    grad_outs = [
-        pltpu.make_async_copy(w_gu.at[:, 2 * part :], gate_up_grad_ref, out_sem.at[0]),
-        pltpu.make_async_copy(acc_down.at[mine[0], :], down_grad_ref, out_sem.at[1]),
-    ]
+    grad_push = (
+        lambda other: w_gu.at[pl.ds(pl.multiple_of(other * w_rows, w_rows), w_rows), whole_gu],
+        lambda slot: grad_land.at[slot],
+        d_send,
+        d_recv,
+    )
 
     def finish_grads():
         for copy in grad_copies:
@@ -425,57 +504,66 @@
         @pl.loop(0, width // 256)
         def _(j):
             span = pl.ds(pl.multiple_of(j * 256, 256), 256)
+            w_gu[span, whole_gu] = (acc_gu[span, mine] + sib_gu[span, :].astype(jnp.float32)).astype(jnp.bfloat16)
+
+        place.push_all(*grad_push)
+        grad_land[me] = w_gu[pl.ds(pl.multiple_of(me * w_rows, w_rows), w_rows), whole_gu]
+        acc_down[mine_rows, :] = acc_down[mine_rows, :] + sib_down[...].astype(jnp.float32)
+        down_out.start()
+
+    def write_grads():
+        place.wait_all(*grad_push, sent=False)
+
+        @pl.loop(0, place.every)
+        def _(j):
+            span = pl.ds(pl.multiple_of(j * w_rows, w_rows), w_rows)
+            acc_gu[span, half_gu] = grad_land[j].astype(jnp.float32)
             for i in (0, 1):
-                cols = slice(i * part, (i + 1) * part)
-                w_gu[span, 2 * part + i * part : 2 * part + (i + 1) * part] = (
-                    acc_gu[span, mine[i]] + sib_gu[span, cols].astype(jnp.float32)
-                ).astype(jnp.bfloat16)
-
-        acc_down[mine[0], :] = acc_down[mine[0], :] + sib_down[...].astype(jnp.float32)
-        for copy in grad_outs:
-            copy.start()
-
-    for copy in own:
+                target = gate_up_grad_ref.at[:, pl.ds(pl.multiple_of((i * place.every + j) * part, part), part)]
+                pltpu.make_async_copy(acc_gu.at[span, pl.ds(i * part, part)], target, out_sem.at[1]).start()
+
+    for copy in [own, d_mlp_in] + own_weights:
         copy.start()
-    for copy in own:
+    place.greet_all()
+    own.wait()
+    gather.a(0)
+    down_to.start()
+    send_columns()
+    for k in range(1, line):
+        gather.a(k)
+        gather.b(k - 1)
+    for copy in [d_mlp_in] + own_weights:
         copy.wait()
-    for tensor in (0, 1):
-        send_line(tensor, z, has_up, 0)
-        send_line(tensor, z, has_down, 1)
-    step_a(0)
-    for copy in to_sibling + own_weights:
-        copy.start()
+    wait_columns(False)
+    columns_to.start()
+    down_from.wait_recv()
+    columns_from.wait_recv()
+    down_to.wait_send()
+    columns_to.wait_send()
+    wait_columns(True)
     for k in range(line):
-        if k + 1 < line:
-            step_a(k + 1)
-        step_b(k)
+        gather.c(k)
+        compute(k)
+        reduce.a(k)
+        term_out(k).start()
         if k == 0:
-            for copy in own_weights:
-                copy.wait()
-            for copy in from_sibling:
-                copy.wait_recv()
-            for copy in to_sibling:
-                copy.wait_send()
-        else:
-            step_c(k - 1)
-            compute(k - 1)
-            reduce_a(k - 1)
-    step_c(line - 1)
-    compute(line - 1)
-    reduce_a(line - 1)
+            gather.b(line - 1)
     exchange_grads()
     backwards = range(line - 1, -1, -1)
     for k in backwards:
-        reduce_b(k)
+        reduce.b(k)
     finish_grads()
     for k in backwards:
-        reduce_c(k)
+        reduce.c(k)
+    write_grads()
     for k in backwards:
-        reduce_end(k)
+        reduce.end(k)
+        term_out(k).wait()
     for copy in grad_copies:
         copy.wait_send()
-    for copy in grad_outs:
-        copy.wait()
+    place.wait_all(*grad_push)
+    down_out.wait()
+    pltpu.make_async_copy(gate_up_grad_ref, gate_up_grad_ref, out_sem.at[1]).wait()
 
 
 def mlp_exchange(line, normed, d_mlp, gate_up, down):
@@ -486,17 +574,17 @@
     return pl.pallas_call(
         functools.partial(mlp_kernel, line, blk, part),
         out_shape=(
+            jax.ShapeDtypeStruct(d_mlp.shape, bf16),
             jax.ShapeDtypeStruct((blk, width), f32),
-            jax.ShapeDtypeStruct((blk, width), f32),
-            jax.ShapeDtypeStruct((width, 2 * part), bf16),
+            jax.ShapeDtypeStruct(gate_up.shape, f32),
             jax.ShapeDtypeStruct((part, width), f32),
         ),
         in_specs=[any_spec] * 4,
-        out_specs=(vmem_spec, vmem_spec, any_spec, any_spec),
+        out_specs=(any_spec, vmem_spec, any_spec, any_spec),
         scratch_shapes=[
             pltpu.VMEM((2, line * 4 * blk, width), bf16),
-            pltpu.VMEM((2, line, 3 * blk, width), bf16),
-            pltpu.VMEM((2, line + 1, blk, width), bf16),
+            pltpu.VMEM((line, 3 * blk, width), bf16),
+            pltpu.VMEM((line + 1, blk, width), bf16),
             pltpu.VMEM((width, 4 * part), bf16),
             pltpu.VMEM((2 * part, width), bf16),
             pltpu.VMEM((width, 4 * part), f32),
@@ -505,68 +593,22 @@
             pltpu.VMEM((4 * blk, 4 * part), bf16),
             pltpu.VMEM((width, 2 * part), bf16),
             pltpu.VMEM((part, width), bf16),
-            dma((2, line, 2)),
-            dma((2, line)),
-            dma((2, line, 4)),
-            dma((2, line, 4)),
-            dma((2, line, 2)),
-            dma((2, line, 2)),
-            dma((2, line, 2)),
-            dma((2, line, 2)),
-            dma((2, line, 4)),
-            dma((2, line, 4)),
-            dma((2, line)),
-            dma((2, line + 1)),
-            dma((3,)),
-            dma((3,)),
+            pltpu.VMEM((8 * line, gate_up.shape[0], 2 * part), bf16),
             dma((2,)),
             dma((2,)),
+            dma((2,)),
+            dma((2,)),
+            dma((2, 8 * line)),
+            dma((2, 8 * line)),
+            dma((8 * line,)),
+            dma((8 * line,)),
             dma((5,)),
-            dma((2,)),
+            dma((2 + line,)),
+            *slice_gather_sems(line),
+            *slice_reduce_sems(line),
         ],
         compiler_params=pltpu.CompilerParams(collective_id=0, has_side_effects=True, vmem_limit_bytes=63 * MIB),
     )(normed, d_mlp, gate_up, down)
-
-
-class Place:
-    def __init__(self, line):
-        self.line = line
-        self.c, self.z = lax.axis_index("ctx"), lax.axis_index("shard")
-        self.q, self.core = self.c // 2, self.c % 2
-        self.me = self.c * line + self.z
-        self.every = 8 * line
-        self.cx, self.cy = (self.c + 2 - 4 * (self.q % 2), self.z), (self.c + 4 - 8 * (self.q // 2), self.z)
-        self.sibling = (self.c + 1 - 2 * self.core, self.z)
-        self.qx, self.qy, self.qd = self.q + 1 - 2 * (self.q % 2), self.q + 2 - 4 * (self.q // 2), 3 - self.q
-
-    def peer(self, i):
-        other = lax.rem(self.me + i, self.every)
-        return other, (other // self.line, other % self.line)
-
-    def greet_all(self):
-        barrier = pltpu.get_barrier_semaphore()
-
-        @pl.loop(1, self.every)
-        def _(i):
-            pl.semaphore_signal(barrier, inc=1, device_id=self.peer(i)[1], device_id_type=pl.DeviceIdType.MESH)
-
-        pl.semaphore_wait(barrier, self.every - 1)
-
-    def push_all(self, source, target, send_sems, recv_sems):
-        @pl.loop(1, self.every)
-        def _(i):
-            other, device = self.peer(i)
-            remote(source(other), target(self.me), send_sems.at[other], recv_sems.at[self.me], device).start()
-
-    def wait_all(self, source, target, send_sems, recv_sems, sent=True):
-        @pl.loop(1, self.every)
-        def _(i):
-            other, device = self.peer(i)
-            copy = remote(source(other), target(other), send_sems.at[other], recv_sems.at[other], device)
-            if sent:
-                copy.wait_send()
-            else:
-                copy.wait_recv()
 
 
 def plane_gather(at, buf, blk, sems):
@@ -609,17 +651,21 @@
             sent(i).start()
         across(0, at.core).start()
 
-    def finish():
+    def turn():
         for i in (0, 1):
             arriving(i).wait_recv()
             onward(i).start()
             across(i + 1, at.core).start()
+
+    def rest():
         for i in (2, 3):
             arriving(i).wait_recv()
             across(i + 1, at.core).start()
         for i in (0, 1):
             passed(i).wait_recv()
             across(i + 5, at.core).start()
+
+    def whole():
         for i in range(7):
             across(i, 1 - at.core).wait_recv()
 
@@ -631,7 +677,7 @@
         for i in range(7):
             across(i, at.core).wait_send()
 
-    return start, finish, end
+    return start, turn, rest, whole, end
 
 
 GATHER_SEMS = (4, 4, 2, 2, 7, 7)
@@ -698,15 +744,17 @@
 
 def front_kernel(
     line, blk, q_part, kv_part,
-    tokens_ref, gains_ref, w_qkv_ref, w_out_ref, q_seg_ref, k_seg_ref,
-    mid_ref, normed_two_ref, qkv_ref, attn_ref, lse_ref, tops_ref, gain_ref, normed_ref, w_qkv_all_ref, w_out_all_ref,
-    buf, term, core_land, land, w_qkv, w_out, gain_land, top_land, proj,
+    tokens_ref, d_mlp_ref, gains_ref, w_qkv_ref, w_out_ref, q_seg_ref, k_seg_ref,
+    mid_ref, normed_two_ref, qkv_ref, attn_ref, lse_ref, tops_ref, gain_ref, normed_ref, w_qkv_all_ref, w_out_all_ref, d_mlp_all_ref,
+    buf, term, core_land, land, w_qkv, w_line, w_out, gain_land, top_land, proj,
     *sems,
 ):
     at = Place(line)
     gather = plane_gather(at, buf, blk, sems[:6])
     reduce = plane_reduce(at, term, core_land, land, blk, sems[6:12])
-    qkv_send, qkv_recv, gain_send, gain_recv, top_send, top_recv, out_send, out_recv, own_sem, write_sem = sems[12:]
+    line_send, line_recv, qkv_send, qkv_recv, gain_send, gain_recv, top_send, top_recv, out_send, out_recv, own_sem, write_sem = sems[12:24]
+    d_mlp_rows = slice_rows(d_mlp_all_ref, blk)
+    beside = SliceGather(at, d_mlp_rows, blk, sems[24:])
     w_rows, width = w_out_ref.shape
     size = 8 * blk
     mine = pl.ds(pl.multiple_of(at.c * blk, blk), blk)
@@ -714,34 +762,56 @@
     own = [
         pltpu.make_async_copy(tokens_ref, buf.at[mine, :], own_sem.at[0]),
         pltpu.make_async_copy(gains_ref, gain_land.at[at.me], own_sem.at[1]),
-        pltpu.make_async_copy(w_qkv_ref.at[at.c], w_qkv.at[at.me], own_sem.at[2]),
+        pltpu.make_async_copy(w_qkv_ref, w_line.at[at.z], own_sem.at[2]),
         pltpu.make_async_copy(w_out_ref, w_out.at[at.z], own_sem.at[3]),
+        pltpu.make_async_copy(d_mlp_ref, d_mlp_rows(at.z, at.q, 0, blk), own_sem.at[4]),
     ]
     for copy in own:
         copy.start()
     at.greet_all()
-    qkv_push = (lambda other: w_qkv_ref.at[other // line], lambda slot: w_qkv.at[slot], qkv_send, qkv_recv)
     gain_push = (lambda other: gains_ref, lambda slot: gain_land.at[slot], gain_send, gain_recv)
     top_push = (lambda other: top_land.at[at.me], lambda slot: top_land.at[slot], top_send, top_recv)
+
+    def qkv_line(place, way):
+        return remote(w_line.at[place], w_line.at[place], line_send.at[place, way], line_recv.at[place], (at.c, at.z + 1 - 2 * way))
+
+    def out_line(place, way):
+        return remote(w_out.at[place], w_out.at[place], out_send.at[place, way], out_recv.at[place], (at.c, at.z + 1 - 2 * way))
+
+    def qkv_copy(i, place, arriving=False):
+        other = lax.rem(at.c + i, 8)
+        slot = (other if arriving else at.c) * line + place
+        return remote(w_line.at[place, other], w_qkv.at[slot], qkv_send.at[place, other], qkv_recv.at[slot], (other, at.z))
+
+    def qkv_step(k):
+        at.line_spread(qkv_line, k)
+
+        @pl.loop(1, 8)
+        def _(i):
+            qkv_copy(i, at.source(k)).start()
+
+        w_qkv[at.c * line + at.source(k)] = w_line[at.source(k), at.c]
+
+    start, turn, rest, whole, end = gather
+    own[0].wait()
+    start()
+    own[2].wait()
+    qkv_step(0)
     at.push_all(*gain_push)
-    own[0].wait()
-    gather[0]()
-    at.push_all(*qkv_push)
-
-    def out_copy(i, slot):
-        z = lax.rem(at.z + i, line)
-        return z, remote(w_out_ref, w_out.at[slot(z)], out_send.at[z], out_recv.at[slot(z)], (at.c, z))
-
-    for i in range(1, line):
-        out_copy(i, lambda z: at.z)[1].start()
-    gather[1]()
-    for copy in own[1:]:
-        copy.wait()
+    turn()
+    qkv_step(1)
+    rest()
+    for k in range(2, line - 1):
+        qkv_step(k)
+    own[1].wait()
     at.wait_all(*gain_push, sent=False)
     for i in range(at.every // 2):
         pair = gain_land[2 * i].astype(jnp.float32) + gain_land[2 * i + 1].astype(jnp.float32)
         gain_ref[:, i * 128 : (i + 1) * 128] = pair[:8, :]
-    gather[2]()
+    own[4].wait()
+    beside.a(0)
+    whole()
+    end()
     at.wait_all(*gain_push)
 
     @pl.loop(0, size // 32)
@@ -756,7 +826,16 @@
         pltpu.make_async_copy(w_out, w_out_all_ref, write_sem.at[2]),
     ]
     writes[0].start()
-    at.wait_all(*qkv_push, sent=False)
+    qkv_step(line - 1)
+    own[3].wait()
+    at.line_spread(out_line, 0)
+    beside.b(0)
+    for k in range(line):
+
+        @pl.loop(1, 8)
+        def _(i):
+            qkv_copy(i, at.source(k), True).wait_recv()
+
     writes[1].start()
 
     @pl.loop(0, size // 256)
@@ -764,10 +843,14 @@
         part = pl.ds(pl.multiple_of(i * 256, 256), 256)
         qkv_ref[part, :] = dot(buf[part, :], w_qkv[...].reshape(width, q_part + 2 * kv_part), ((1,), (0,))).astype(jnp.bfloat16)
 
+    at.line_spread(out_line, 1)
+    beside.a(1)
     heads = q_part // HEAD_DIM
     block = math.gcd(size, 256)
     tops = [jnp.full((1, 1), NEGATIVE, jnp.float32)] * heads
     for i in range(size // block):
+        if i > 0 and i + 1 < line:
+            at.line_spread(out_line, i + 1)
         rows, cols = pl.ds(i * block, block), (i + 1) * block
         live = seen_mask(i * block, block, cols, q_seg_ref[rows, :], k_seg_ref[:, :cols])
         keys, values = qkv_ref[:cols, q_part : q_part + kv_part], qkv_ref[:cols, q_part + kv_part :]
@@ -789,8 +872,10 @@
     top_land[at.me] = tile
     at.push_all(*top_push)
 
-    for i in range(1, line):
-        out_copy(i, lambda z: z)[1].wait_recv()
+    for k in range(size // block + 1, line):
+        at.line_spread(out_line, k)
+    beside.b(1)
+    beside.a(2)
     writes[2].start()
     for i, chip in enumerate((at.qd, at.qx, at.qy, at.q)):
         for core in (1 - at.core, at.core):
@@ -804,6 +889,10 @@
 
         reduce[0](i)
     reduce[1](proj)
+    beside.b(2)
+    for k in range(3, line):
+        beside.a(k)
+        beside.b(k)
 
     own_again = pltpu.make_async_copy(tokens_ref, land.at[pl.ds(0, blk), :], own_sem.at[0])
     own_again.start()
@@ -819,15 +908,22 @@
     at.wait_all(*top_push, sent=False)
     tops_ref[...] = top_land[...]
     reduce[2]()
-    at.wait_all(*qkv_push)
     at.wait_all(*top_push)
-    for i in range(1, line):
-        out_copy(i, lambda z: at.z)[1].wait_send()
+    for k in range(line):
+        at.line_sent(qkv_line, k)
+        at.line_sent(out_line, k)
+
+        @pl.loop(1, 8)
+        def _(i):
+            qkv_copy(i, at.source(k)).wait_send()
+
+    for k in range(line):
+        beside.c(k)
     for copy in writes:
         copy.wait()
 
 
-def front(line, tokens, gains, w_qkv, w_out, q_seg, k_seg):
+def front(line, tokens, d_mlp, gains, w_qkv, w_out, q_seg, k_seg):
     blk, width = tokens.shape
     w_rows, cols = w_out.shape[0], w_qkv.shape[2]
     size, every = 8 * blk, 8 * line
@@ -849,36 +945,48 @@
             out((size, width), bf16),
             out((every, w_rows, cols), bf16),
             out((line, w_rows, width), bf16),
+            out((line * 4 * blk, width), bf16),
         ),
-        in_specs=[any_spec] * 4 + [vmem_spec] * 2,
-        out_specs=(vmem_spec,) * 7 + (any_spec,) * 3,
+        in_specs=[any_spec] * 5 + [vmem_spec] * 2,
+        out_specs=(vmem_spec,) * 7 + (any_spec,) * 4,
         scratch_shapes=[
             pltpu.VMEM((size, width), bf16),
             pltpu.VMEM((size, width), bf16),
             pltpu.VMEM((4, blk, width), bf16),
             pltpu.VMEM((3 * blk, width), bf16),
             pltpu.VMEM((every, w_rows, cols), bf16),
+            pltpu.VMEM((line, 8, w_rows, cols), bf16),
             pltpu.VMEM((line, w_rows, width), bf16),
             pltpu.VMEM((every, 16, 128), bf16),
             pltpu.VMEM((every, 8, 128), f32),
             pltpu.VMEM((blk, width), f32),
-            *[dma((n,)) for n in GATHER_SEMS + REDUCE_SEMS + (every,) * 6 + (line, line, 4, 3)],
+            *[dma((n,)) for n in GATHER_SEMS + REDUCE_SEMS],
+            dma((line, 2)),
+            dma((line,)),
+            dma((line, 8)),
+            *[dma((every,))] * 5,
+            dma((line, 2)),
+            dma((line,)),
+            dma((5,)),
+            dma((3,)),
+            *slice_gather_sems(line),
         ],
         compiler_params=pltpu.CompilerParams(collective_id=1, has_side_effects=True, vmem_limit_bytes=60 * MIB),
-    )(tokens, gains, w_qkv, w_out, q_seg, k_seg)
+    )(tokens, d_mlp, gains, w_qkv, w_out, q_seg, k_seg)
 
 
 def back_kernel(
     line, blk, q_part, kv_part,
-    d_attn_ref, tokens_ref, d_mid_ref, qkv_ref, attn_ref, lse_ref, gain_ref, gain_term_ref, q_seg_ref, k_seg_ref, normed_ref, w_qkv_ref, w_out_ref,
-    grad_tokens_ref, grad_qkv_ref, grad_out_ref, gain_sum_ref,
-    buf, term, core_land, land, w_qkv, w_out, normed, d_heads, d_qkv, dk_sum, dv_sum, stage_qkv, stage_out, qkv_land, out_land, gain_stage, gain_land, d_normed,
+    d_attn_ref, tokens_ref, mid_ref, d_mid_ref, qkv_ref, attn_ref, lse_ref, gain_ref, gain_term_ref, q_seg_ref, k_seg_ref, normed_ref, w_qkv_ref, w_out_ref, mlp_term_ref,
+    mixed_ref, grad_tokens_ref, grad_qkv_ref, grad_out_ref, gain_sum_ref,
+    buf, term, core_land, land, w_qkv, w_out, normed, d_heads, d_qkv, dk_sum, dv_sum, stage_qkv, stage_out, qkv_land, out_land, gain_stage, gain_land, d_normed, mlp_term, mlp_land, mlp_line_land, mlp_sum,
     *sems,
 ):
     at = Place(line)
     gather = plane_gather(at, buf, blk, sems[:6])
     reduce = plane_reduce(at, term, core_land, land, blk, sems[6:12])
-    qkv_send, qkv_recv, gain_send, gain_recv, out_send, out_recv, own_sem = sems[12:]
+    qkv_send, qkv_recv, gain_send, gain_recv, out_send, out_recv, own_sem = sems[12:19]
+    beside = SliceReduce(at, slice_rows(mlp_term, blk), blk, mlp_land, mlp_line_land, mlp_sum, sems[19:])
     width = buf.shape[1]
     w_rows = w_out.shape[1]
     size = 8 * blk
@@ -888,20 +996,28 @@
         pltpu.make_async_copy(w_out_ref, w_out, own_sem.at[1]),
         pltpu.make_async_copy(w_qkv_ref, w_qkv, own_sem.at[2]),
         pltpu.make_async_copy(normed_ref, normed, own_sem.at[3]),
+        pltpu.make_async_copy(mlp_term_ref, mlp_term, own_sem.at[4]),
     ]
     for copy in own:
         copy.start()
     at.greet_all()
     own[0].wait()
-    gather[0]()
-    gather[1]()
+    start, turn, rest, whole, end = gather
+    start()
+    turn()
+    rest()
     for copy in own[1:]:
         copy.wait()
+    beside.a(line - 1)
+    whole()
 
     @pl.loop(0, size // 256)
     def _(i):
         part = pl.ds(pl.multiple_of(i * 256, 256), 256)
         d_heads[part, :] = dot(buf[part, :], w_out[...].reshape(line * w_rows, width), ((1,), (1,))).astype(jnp.bfloat16)
+
+    if line > 1:
+        beside.a(line - 2)
 
     @pl.loop(0, width // 256)
     def _(i):
@@ -940,6 +1056,9 @@
             dv_sum[:cols, :] += dot(probs.astype(jnp.bfloat16), d_out, ((0,), (0,)))
     d_qkv[:, q_part : q_part + kv_part] = (dk_sum[...] * SCALE).astype(jnp.bfloat16)
     d_qkv[:, q_part + kv_part :] = dv_sum[...].astype(jnp.bfloat16)
+    beside.b(line - 1)
+    for k in range(line - 3, 0, -1):
+        beside.a(k)
 
     for i, chip in enumerate((at.qd, at.qx, at.qy, at.q)):
         for core in (1 - at.core, at.core):
@@ -965,6 +1084,10 @@
     qkv_land[at.me] = stage_qkv[at.me]
     out_land[at.z] = stage_out[at.z]
     reduce[1](d_normed)
+    if line > 2:
+        beside.a(0)
+    for k in range(line - 2, -1, -1):
+        beside.b(k)
 
     gain_stage[...] = jnp.zeros_like(gain_stage)
     gain_stage[1:2, :] = gain_term_ref[...]
@@ -984,6 +1107,9 @@
     at.push_all(*gain_push)
     gain_land[at.me] = gain_stage[:, pl.ds(pl.multiple_of((at.me // 2) * 128, 128), 128)]
 
+    for k in range(line - 1, -1, -1):
+        beside.c(k)
+    mixed_ref[...] = (mid_ref[...] + BRANCH * mlp_sum[...]).astype(jnp.bfloat16)
     for i in range(1, line):
         out_arrival(i).wait_recv()
     total = out_land[0].astype(jnp.float32)
@@ -1001,15 +1127,17 @@
 
     at.wait_all(*gain_push, sent=False)
     gain_sum_ref[...] = jnp.sum(gain_land[...], axis=0)
-    gather[2]()
+    end()
     reduce[2]()
+    for k in range(line):
+        beside.end(k)
     at.wait_all(*qkv_push)
     at.wait_all(*gain_push)
     for i in range(1, line):
         out_copy(i).wait_send()
 
 
-def back(line, d_attn, tokens, d_mid, qkv, attn_out, lse, gain, gain_term, q_seg, k_seg, normed, w_qkv, w_out):
+def back(line, d_attn, tokens, mid, d_mid, qkv, attn_out, lse, gain, gain_term, q_seg, k_seg, normed, w_qkv, w_out, mlp_term):
     blk, width = tokens.shape
     w_rows, cols = w_out.shape[1], w_qkv.shape[2]
     size, every = 8 * blk, 8 * line
@@ -1019,9 +1147,9 @@
     bf16, f32, dma, out = jnp.bfloat16, jnp.float32, pltpu.SemaphoreType.DMA, jax.ShapeDtypeStruct
     return pl.pallas_call(
         functools.partial(back_kernel, line, blk, q_part, kv_part),
-        out_shape=(out((blk, width), f32), out((8, w_rows, cols), f32), out((w_rows, width), f32), out((8, 128), f32)),
-        in_specs=[any_spec] + [vmem_spec] * 9 + [any_spec] * 3,
-        out_specs=(vmem_spec,) * 4,
+        out_shape=(out((blk, width), bf16), out((blk, width), f32), out((8, w_rows, cols), f32), out((w_rows, width), f32), out((8, 128), f32)),
+        in_specs=[any_spec] + [vmem_spec] * 10 + [any_spec] * 4,
+        out_specs=(vmem_spec,) * 5,
         scratch_shapes=[
             pltpu.VMEM((size, width), bf16),
             pltpu.VMEM((size, width), bf16),
@@ -1041,10 +1169,15 @@
             pltpu.VMEM((8, width), f32),
             pltpu.VMEM((every, 8, 128), f32),
             pltpu.VMEM((blk, width), f32),
-            *[dma((n,)) for n in GATHER_SEMS + REDUCE_SEMS + (every,) * 4 + (line, line, 4)],
+            pltpu.VMEM((line * 4 * blk, width), bf16),
+            pltpu.VMEM((line, 3 * blk, width), bf16),
+            pltpu.VMEM((line + 1, blk, width), bf16),
+            pltpu.VMEM((blk, width), f32),
+            *[dma((n,)) for n in GATHER_SEMS + REDUCE_SEMS + (every,) * 4 + (line, line, 5)],
+            *slice_reduce_sems(line),
         ],
         compiler_params=pltpu.CompilerParams(collective_id=2, has_side_effects=True, vmem_limit_bytes=60 * MIB),
-    )(d_attn, tokens, d_mid, qkv, attn_out, lse, gain, gain_term, q_seg, k_seg, normed, w_qkv, w_out)
+    )(d_attn, tokens, mid, d_mid, qkv, attn_out, lse, gain, gain_term, q_seg, k_seg, normed, w_qkv, w_out, mlp_term)
 
 
 def split_heads(w, parts):
@@ -1153,9 +1286,7 @@
 
 def on_planes(n_shard, tokens, lengths, cotangent, w_qkv, w_out, w_gate_up, w_down, gain_attn, gain_mlp):
     count, width = tokens.shape[1:]
-    n = 8 * n_shard
     w_rows = w_qkv.shape[0]
-    ff_part = w_down.shape[0]
     rows = tokens.reshape(count, width)
     grad_rows = cotangent.reshape(count, width).astype(jnp.float32)
     size = count * 8
@@ -1167,30 +1298,24 @@
     none = jnp.zeros_like(gains)
     gains = jnp.where(side == 0, jnp.concatenate([gains, none], axis=1), jnp.concatenate([none, gains], axis=1))
     gains = jnp.pad(gains, ((0, 14), (0, 0)))
-    mid, normed_two, qkv, attn_out, lse, tops, gain, normed_one, qkv_mine, out_mine = front(
-        n_shard, rows, gains, split_heads(w_qkv, 8).transpose(1, 0, 2), w_out, q_seg, k_seg
+    mid, normed_two, qkv, attn_out, lse, tops, gain, normed_one, qkv_mine, out_mine, d_mlp = front(
+        n_shard, rows, (BRANCH * grad_rows).astype(jnp.bfloat16), gains, split_heads(w_qkv, 8).transpose(1, 0, 2), w_out, q_seg, k_seg
     )
     heads = HEADS // 8
     head_top = jnp.max(tops[:, 0, :heads].reshape(8, n_shard, heads), axis=1).reshape(HEADS)
     clip = CLIP_TARGET / jnp.maximum(head_top, CLIP_TARGET)
 
-    gate_up_mine = lax.all_to_all(w_gate_up.reshape(w_rows, 2, n, ff_part), EVERY, split_axis=2, concat_axis=0, tiled=True)
-    gate_up_mine = gate_up_mine.reshape(width, 2 * ff_part)
-    d_mlp = (BRANCH * grad_rows).astype(jnp.bfloat16)
-    mlp_proj, d_normed_two, gate_up_grad, grad_down = mlp_exchange(n_shard, normed_two, d_mlp, gate_up_mine, w_down)
-    mixed = (mid + BRANCH * mlp_proj).astype(jnp.bfloat16).reshape(1, count, width)
-    grad_gate_up = lax.all_to_all(gate_up_grad.reshape(n * w_rows, 2, 1, ff_part), EVERY, split_axis=0, concat_axis=2, tiled=True)
-    grad_gate_up = grad_gate_up.reshape(w_rows, 2 * n * ff_part).astype(jnp.float32)
+    mlp_term, d_normed_two, grad_gate_up, grad_down = mlp_exchange(n_shard, normed_two, d_mlp, w_gate_up, w_down)
     d_mid_norm, gain_two_term = norm_backward(d_normed_two, mid, rms_scale(mid), gain[1:2])
     d_mid = grad_rows + d_mid_norm
 
     d_attn = (BRANCH * d_mid).astype(jnp.bfloat16)
-    grad_tokens, qkv_grad, grad_out, gain_sum = back(
-        n_shard, d_attn, rows, d_mid, qkv, attn_out, lse, gain, gain_two_term.reshape(1, width), q_seg, k_seg, normed_one, qkv_mine, out_mine
+    mixed, grad_tokens, qkv_grad, grad_out, gain_sum = back(
+        n_shard, d_attn, rows, mid, d_mid, qkv, attn_out, lse, gain, gain_two_term.reshape(1, width), q_seg, k_seg, normed_one, qkv_mine, out_mine, mlp_term
     )
     grad_qkv = join_heads(qkv_grad.transpose(1, 0, 2), 8)
     gain_grads = jnp.where(side == 0, gain_sum[:2, :w_rows], gain_sum[:2, w_rows : 2 * w_rows])
-    return (mixed, grad_tokens.reshape(1, count, width), grad_qkv, grad_out, grad_gate_up, grad_down, gain_grads[0], gain_grads[1], clip)
+    return (mixed.reshape(1, count, width), grad_tokens.reshape(1, count, width), grad_qkv, grad_out, grad_gate_up, grad_down, gain_grads[0], gain_grads[1], clip)
 
 
 def solution(mesh):

time: 612 us -> 577 us (0.943)
  starting transfers between devices: 16 us -> 0 us
  Pallas kernels: 551 us -> 536 us
  local copies, waits for them, and re-layouts: 30.9 us -> 16.6 us
    pallas_call x1, Pallas kernels: 303 us -> 237 us  [mlp_exchange(): pl.pallas_call(functools.partial(mlp_kernel, line, blk, part), out_shape=...]
    pallas_call x1, Pallas kernels: 113 us -> 151 us  [back(): pl.pallas_call(functools.partial(back_kernel, line, blk, q_part, kv_part)...]
    all_to_all x2 -> x0, starting transfers between devices: 16 us -> none  [the longest x1 8.47 us: on_planes(): lax.all_to_all(gate_up_grad.reshape(n * w_rows, 2, 1, ff_part), EVERY, sp...]
    pallas_call x1, Pallas kernels: 136 us -> 148 us  [front(): pl.pallas_call(functools.partial(front_kernel, line, blk, q_part, kv_part...]
    convert_element_type x2 -> x0, local copies, waits for them, and re-layouts: 9.44 us -> none  [on_planes(): grad_gate_up.reshape(w_rows, 2 * n * ff_part).astype(jnp.float32)]
    reshape x2 -> x0, local copies, waits for them, and re-layouts: 7.44 us -> none  [the longest x1 3.96 us: on_planes(): gate_up_grad.reshape(n * w_rows, 2, 1, ff_part)]
  transfers between devices with their start and end apart: 2 -> 0, of which waited for: 0 -> 0; matrix products, arithmetic and copies ran while one was open for 2% -> 0% of each run, Pallas kernels for 41% -> 0%
where the time goes in v4:
time: 577 us; the launch traced here: 567 us
  Pallas kernels  536 us (93%)
  local copies, waits for them, and re-layouts  16.6 us (3%)
  other arithmetic  13.2 us (2%)
    pallas_call x1, Pallas kernels, mlp_exchange(): pl.pallas_call(functools.partial(mlp_kernel, line, blk, part), out_shape=...  237 us
    pallas_call x1, Pallas kernels, back(): pl.pallas_call(functools.partial(back_kernel, line, blk, q_part, kv_part)...  151 us
    pallas_call x1, Pallas kernels, front(): pl.pallas_call(functools.partial(front_kernel, line, blk, q_part, kv_part...  148 us

profile of v4, /device:TPU:0, one launch (start us, length us, event | category | flops | bytes accessed | tf_op | source)
XLA Modules:
  0.0 567.2 jit_solution(13151290818888327172)
XLA Ops:
  0.6 0.8 reduce-window.4
  1.5 0.7 pad_maximum_fusion.1
  2.3 0.6 pad.6.gains_ref
  2.9 0.9 fusion.2
  3.8 0.1 reshape_reshape.6
  4.0 0.1 reshape_reshape.7
  4.1 1.0 slice.40
  5.1 0.9 maximum_bitcast_fusion.w_qkv_ref
  6.0 1.0 copy.41.q_seg_ref
  7.0 1.9 fusion.d_mlp_ref
  9.0 148.4 %shard_map.160 = (f32[128,2048]{1,0:T(8,128)}, bf16[128,2048]{1,0:T(8,128)(2,1)}, bf16[1024,384]{1,0:T(8,128)(2,1)}, bf16[1024,256]{1,0:T(8,128)(2,1)}, f32[1024...) custom-call(bf16[128,2048]{1,0:T(8,128)(2,1)} %bitcast.33, ...), custom_call_target="tpu_custom_call" | custom-call | tf_op jit(solution)/shard_map/pallas_call | solution.py:935
  157.4 1.4 multiply_reduce_fusion.2
  158.8 0.9 slice.44
  159.6 0.9 slice.52
  160.6 0.6 div.15
  161.2 237.2 %shard_map.161 = (bf16[2048,2048]{1,0:T(8,128)(2,1)}, f32[128,2048]{1,0:T(8,128)}, f32[64,16384]{1,0:T(8,128)}, f32[256,2048]{1,0:T(8,128)}) custom-call(bf16[128,2048]{1,0:T(8,128)(2,1)} %get-tuple-element.30.normed_ref, bf16[2048,2048]{1,0:T(8,128)(2,1)} %get-tuple-element.31.d_mlp_ref, bf16[64,16384]{1,0:T(8,128)(2,1)} %w_gate_up_ref.1, ...), custom_call_target="tpu_custom_call" | custom-call | tf_op jit(solution)/shard_map/pallas_call | solution.py:574
  398.4 2.5 multiply_reduce_fusion
  400.8 3.0 multiply_convert_fusion
  403.9 150.8 %shard_map.162 = (bf16[128,2048]{1,0:T(8,128)(2,1)}, f32[128,2048]{1,0:T(8,128)}, f32[8,64,384]{2,1,0:T(8,128)}, f32[64,2048]{1,0:T(8,128)}, f32[8,128]{1,0:T(8,128)}) custom-call(bf16[128,2048]{1,0:T(8,128)(2,1)} %get-tuple-element.51.d_attn_ref, bf16[128,2048]{1,0:T(8,128)(2,1)} %bitcast.34, f32[128,2048]{1,0:T(8,128)} %get-tuple-element.29.mid_ref, ...), custom_call_target="tpu_custom_call" | custom-call | tf_op jit(solution)/shard_map/pallas_call | solution.py:1148
  554.7 0.9 slice_select_fusion
  555.6 0.5 slice_bitcast_fusion.1
  556.1 1.1 slice_bitcast_fusion
  557.2 1.2 fusion.1
  558.4 0.2 copy.44
  558.7 0.2 copy.45
  559.0 0.9 pad_maximum_fusion
  560.0 0.8 copy.60
  560.8 1.0 copy.61
  561.7 0.8 copy.62
  562.5 2.1 copy.63
  564.7 1.0 copy-done.2
  565.6 1.3 copy.64
  (26 shorter events, 0.6 us)
Async XLA Ops:
  2.3 6.6 %copy-start.6 = (s32[1024]{0:T(1024)}, s32[1024]{0:T(1024)S(1)}, u32[]{:S(2)}) copy-start(s32[1024]{0:T(1024)S(1)} %convert_reduce_fusion) | copy-start | bytes 12292
  161.2 239.6 %copy-start.1 = (bf16[1,128,2048]{2,1,0:T(8,128)(2,1)S(1)}, bf16[1,128,2048]{2,1,0:T(8,128)(2,1)}, u32[]{:S(2)}) copy-start(bf16[1,128,2048]{2,1,0:T(8,128)(2,1)} %param.11) | copy-start | bytes 1572868
  554.7 5.3 copy-start.5
  554.7 6.1 %copy-start.3 = (f32[128,2048]{1,0:T(8,128)S(1)}, f32[128,2048]{1,0:T(8,128)}, u32[]{:S(2)}) copy-start(f32[128,2048]{1,0:T(8,128)} %get-tuple-element.42) | copy-start | bytes 3145732
  557.2 4.6 copy-start.4
  559.0 3.5 copy-start
  562.5 3.1 copy-start.2

commit v5 on v4

--- a/solution.py
+++ b/solution.py
@@ -383,20 +383,50 @@
     return rows
 
 
+class ColumnSpread:
+    def __init__(self, place, source, target, part, send_sems, recv_sems):
+        self.place, self.source, self.target, self.part = place, source, target, part
+        self.send_sems, self.recv_sems = send_sems, recv_sems
+
+    def copies(self, other, slot):
+        rows = self.source.shape[0]
+        for j in (0, 1):
+            columns = self.source.at[:, pl.ds(pl.multiple_of((j * self.place.every + other) * self.part, self.part), self.part)]
+            yield j, columns, self.target.at[pl.ds(pl.multiple_of(slot * rows, rows), rows), pl.ds(j * self.part, self.part)]
+
+    def start(self):
+        @pl.loop(1, self.place.every)
+        def _(i):
+            other, device = self.place.peer(i)
+            for j, source, target in self.copies(other, self.place.me):
+                remote(source, target, self.send_sems.at[j, other], self.recv_sems.at[j, self.place.me], device).start()
+
+    def own(self, sems):
+        return [pltpu.make_async_copy(source, target, sems[j]) for j, source, target in self.copies(self.place.me, self.place.me)]
+
+    def wait(self):
+        @pl.loop(1, self.place.every)
+        def _(i):
+            other, device = self.place.peer(i)
+            for j, source, target in self.copies(other, other):
+                copy = remote(source, target, self.send_sems.at[j, other], self.recv_sems.at[j, other], device)
+                copy.wait_recv()
+                copy.wait_send()
+
+
 def mlp_kernel(
-    line, blk, part, normed_ref, d_mlp_ref, w_gate_up_ref, down_ref,
-    mlp_term_ref, d_normed_ref, gate_up_grad_ref, down_grad_ref,
-    act, land, line_land, w_gu, w_down, acc_gu, acc_down, hid, d_gu, sib_gu, sib_down, grad_land,
-    w_send, w_recv, g_send, g_recv, c_send, c_recv, d_send, d_recv, own_sem, out_sem, *sems,
+    line, blk, part, normed_ref, d_mlp_ref, gate_up_ref, down_ref, mid_ref, grad_ref, gain_ref,
+    mlp_term_ref, d_mid_ref, d_attn_ref, gain_term_ref, gate_up_grad_ref, down_grad_ref,
+    act, land, line_land, w_gu, w_down, acc_gu, acc_down, hid, d_gu, sib_gu, sib_down, d_normed,
+    w_send, w_recv, g_send, g_recv, own_sem, out_sem, *sems,
 ):
     place = Place(line)
-    core, me, sibling = place.core, place.me, place.sibling
+    core, sibling = place.core, place.sibling
     width = w_down.shape[1]
-    w_rows = w_gate_up_ref.shape[0]
     slot_rows = 4 * blk
     rows = slice_rows(act.at[0], blk)
     gather = SliceGather(place, rows, blk, sems[:6])
-    reduce = SliceReduce(place, rows, blk, land, line_land, d_normed_ref, sems[6:])
+    reduce = SliceReduce(place, rows, blk, land, line_land, d_normed, sems[6:])
 
     def slot_of(k):
         return pl.ds(pl.multiple_of(place.source(k) * slot_rows, slot_rows), slot_rows)
@@ -408,37 +438,18 @@
     mine_rows = pl.ds(pl.multiple_of(core * part, part), part)
     their_rows = pl.ds(pl.multiple_of((1 - core) * part, part), part)
 
-    def columns(other, i):
-        return w_gate_up_ref.at[:, pl.ds(pl.multiple_of((i * place.every + other) * part, part), part)]
-
-    def column_place(other, slot, i):
-        first = ((other // line) % 2) * 2 * part + i * part
-        return w_gu.at[pl.ds(pl.multiple_of(slot * w_rows, w_rows), w_rows), pl.ds(pl.multiple_of(first, part), part)]
-
-    def send_columns():
-        @pl.loop(1, place.every)
-        def _(i):
-            other, device = place.peer(i)
-            for j in (0, 1):
-                remote(columns(other, j), column_place(other, me, j), c_send.at[j, other], c_recv.at[j, me], device).start()
-
-    def wait_columns(sent):
-        @pl.loop(1, place.every)
-        def _(i):
-            other, device = place.peer(i)
-            for j in (0, 1):
-                copy = remote(columns(other, j), column_place(me, other, j), c_send.at[j, other], c_recv.at[j, other], device)
-                if sent:
-                    copy.wait_send()
-                else:
-                    copy.wait_recv()
-
-    own_weights = [pltpu.make_async_copy(columns(me, j), column_place(me, me, j), own_sem.at[2 + j]) for j in (0, 1)]
-    own_weights.append(pltpu.make_async_copy(down_ref, w_down.at[mine_rows, :], own_sem.at[4]))
-    down_to = remote(down_ref, w_down.at[mine_rows, :], w_send.at[0], w_recv.at[0], sibling)
-    down_from = remote(down_ref, w_down.at[their_rows, :], w_send.at[0], w_recv.at[0], sibling)
-    columns_to = remote(w_gu.at[:, mine], w_gu.at[:, mine], w_send.at[1], w_recv.at[1], sibling)
-    columns_from = remote(w_gu.at[:, theirs], w_gu.at[:, theirs], w_send.at[1], w_recv.at[1], sibling)
+    own_weights = [
+        pltpu.make_async_copy(gate_up_ref, w_gu.at[:, mine], own_sem.at[2]),
+        pltpu.make_async_copy(down_ref, w_down.at[mine_rows, :], own_sem.at[3]),
+    ]
+    weights_to = [
+        remote(gate_up_ref, w_gu.at[:, mine], w_send.at[0], w_recv.at[0], sibling),
+        remote(down_ref, w_down.at[mine_rows, :], w_send.at[1], w_recv.at[1], sibling),
+    ]
+    weights_from = [
+        remote(gate_up_ref, w_gu.at[:, theirs], w_send.at[0], w_recv.at[0], sibling),
+        remote(down_ref, w_down.at[their_rows, :], w_send.at[1], w_recv.at[1], sibling),
+    ]
 
     def compute(k):
         slot = slot_of(k)
@@ -490,12 +501,7 @@
         for copy in grad_copies:
             copy.start()
 
-    grad_push = (
-        lambda other: w_gu.at[pl.ds(pl.multiple_of(other * w_rows, w_rows), w_rows), whole_gu],
-        lambda slot: grad_land.at[slot],
-        d_send,
-        d_recv,
-    )
+    columns_out = pltpu.make_async_copy(w_gu.at[:, whole_gu], gate_up_grad_ref, out_sem.at[1])
 
     def finish_grads():
         for copy in grad_copies:
@@ -506,67 +512,80 @@
             span = pl.ds(pl.multiple_of(j * 256, 256), 256)
             w_gu[span, whole_gu] = (acc_gu[span, mine] + sib_gu[span, :].astype(jnp.float32)).astype(jnp.bfloat16)
 
-        place.push_all(*grad_push)
-        grad_land[me] = w_gu[pl.ds(pl.multiple_of(me * w_rows, w_rows), w_rows), whole_gu]
+        columns_out.start()
         acc_down[mine_rows, :] = acc_down[mine_rows, :] + sib_down[...].astype(jnp.float32)
         down_out.start()
-
-    def write_grads():
-        place.wait_all(*grad_push, sent=False)
-
-        @pl.loop(0, place.every)
-        def _(j):
-            span = pl.ds(pl.multiple_of(j * w_rows, w_rows), w_rows)
-            acc_gu[span, half_gu] = grad_land[j].astype(jnp.float32)
-            for i in (0, 1):
-                target = gate_up_grad_ref.at[:, pl.ds(pl.multiple_of((i * place.every + j) * part, part), part)]
-                pltpu.make_async_copy(acc_gu.at[span, pl.ds(i * part, part)], target, out_sem.at[1]).start()
 
     for copy in [own, d_mlp_in] + own_weights:
         copy.start()
     place.greet_all()
     own.wait()
     gather.a(0)
-    down_to.start()
-    send_columns()
-    for k in range(1, line):
-        gather.a(k)
-        gather.b(k - 1)
+    for copy in weights_to:
+        copy.start()
+    gather.a(1)
+    gather.b(0)
+    gather.a(2)
+    gather.b(1)
     for copy in [d_mlp_in] + own_weights:
         copy.wait()
-    wait_columns(False)
-    columns_to.start()
-    down_from.wait_recv()
-    columns_from.wait_recv()
-    down_to.wait_send()
-    columns_to.wait_send()
-    wait_columns(True)
-    for k in range(line):
-        gather.c(k)
-        compute(k)
-        reduce.a(k)
-        term_out(k).start()
-        if k == 0:
-            gather.b(line - 1)
+    for copy in weights_from:
+        copy.wait_recv()
+    for copy in weights_to:
+        copy.wait_send()
+    gather.a(3)
+    gather.b(2)
+    gather.c(0)
+    compute(0)
+    term_out(0).start()
+    gather.b(3)
+    gather.c(1)
+    compute(1)
+    term_out(1).start()
+    reduce.a(1)
+    gather.c(2)
+    compute(2)
+    term_out(2).start()
+    reduce.a(2)
+    gather.c(3)
+    compute(3)
+    term_out(3).start()
+    reduce.a(3)
     exchange_grads()
+    reduce.b(3)
+    reduce.b(2)
+    finish_grads()
+    reduce.a(0)
+    reduce.c(3)
+    reduce.b(1)
+    reduce.c(2)
+    reduce.b(0)
+    reduce.c(1)
+    reduce.c(0)
     backwards = range(line - 1, -1, -1)
-    for k in backwards:
-        reduce.b(k)
-    finish_grads()
-    for k in backwards:
-        reduce.c(k)
-    write_grads()
+
+    gain_term_ref[...] = jnp.zeros_like(gain_term_ref)
+
+    @pl.loop(0, blk // 32)
+    def _(i):
+        part = pl.ds(pl.multiple_of(i * 32, 32), 32)
+        mid = mid_ref[part, :]
+        d_rows, gain_term = norm_backward(d_normed[part, :], mid, rms_scale(mid), gain_ref[1:2, :])
+        d_mid = grad_ref[part, :].astype(jnp.float32) + d_rows
+        d_mid_ref[part, :] = d_mid
+        d_attn_ref[part, :] = (BRANCH * d_mid).astype(jnp.bfloat16)
+        gain_term_ref[0:1, :] += gain_term.reshape(1, width)
+
     for k in backwards:
         reduce.end(k)
         term_out(k).wait()
     for copy in grad_copies:
         copy.wait_send()
-    place.wait_all(*grad_push)
     down_out.wait()
-    pltpu.make_async_copy(gate_up_grad_ref, gate_up_grad_ref, out_sem.at[1]).wait()
-
-
-def mlp_exchange(line, normed, d_mlp, gate_up, down):
+    columns_out.wait()
+
+
+def mlp_exchange(line, normed, d_mlp, gate_up, down, mid, grad, gain):
     blk, width = normed.shape
     part = down.shape[0]
     any_spec, vmem_spec = pl.BlockSpec(memory_space=pl.ANY), pl.BlockSpec(memory_space=pltpu.VMEM)
@@ -576,11 +595,13 @@
         out_shape=(
             jax.ShapeDtypeStruct(d_mlp.shape, bf16),
             jax.ShapeDtypeStruct((blk, width), f32),
-            jax.ShapeDtypeStruct(gate_up.shape, f32),
+            jax.ShapeDtypeStruct((blk, width), bf16),
+            jax.ShapeDtypeStruct((8, width), f32),
+            jax.ShapeDtypeStruct(gate_up.shape, bf16),
             jax.ShapeDtypeStruct((part, width), f32),
         ),
-        in_specs=[any_spec] * 4,
-        out_specs=(any_spec, vmem_spec, any_spec, any_spec),
+        in_specs=[any_spec] * 4 + [vmem_spec] * 3,
+        out_specs=(any_spec, vmem_spec, vmem_spec, vmem_spec, any_spec, any_spec),
         scratch_shapes=[
             pltpu.VMEM((2, line * 4 * blk, width), bf16),
             pltpu.VMEM((line, 3 * blk, width), bf16),
@@ -593,22 +614,18 @@
             pltpu.VMEM((4 * blk, 4 * part), bf16),
             pltpu.VMEM((width, 2 * part), bf16),
             pltpu.VMEM((part, width), bf16),
-            pltpu.VMEM((8 * line, gate_up.shape[0], 2 * part), bf16),
+            pltpu.VMEM((blk, width), f32),
             dma((2,)),
             dma((2,)),
             dma((2,)),
             dma((2,)),
-            dma((2, 8 * line)),
-            dma((2, 8 * line)),
-            dma((8 * line,)),
-            dma((8 * line,)),
             dma((5,)),
             dma((2 + line,)),
             *slice_gather_sems(line),
             *slice_reduce_sems(line),
         ],
         compiler_params=pltpu.CompilerParams(collective_id=0, has_side_effects=True, vmem_limit_bytes=63 * MIB),
-    )(normed, d_mlp, gate_up, down)
+    )(normed, d_mlp, gate_up, down, mid, grad, gain)
 
 
 def plane_gather(at, buf, blk, sems):
@@ -744,9 +761,9 @@
 
 def front_kernel(
     line, blk, q_part, kv_part,
-    tokens_ref, d_mlp_ref, gains_ref, w_qkv_ref, w_out_ref, q_seg_ref, k_seg_ref,
-    mid_ref, normed_two_ref, qkv_ref, attn_ref, lse_ref, tops_ref, gain_ref, normed_ref, w_qkv_all_ref, w_out_all_ref, d_mlp_all_ref,
-    buf, term, core_land, land, w_qkv, w_line, w_out, gain_land, top_land, proj,
+    tokens_ref, grad_ref, w_gate_up_ref, gains_ref, w_qkv_ref, w_out_ref, q_seg_ref, k_seg_ref,
+    mid_ref, normed_two_ref, qkv_ref, attn_ref, lse_ref, tops_ref, gain_ref, normed_ref, w_qkv_all_ref, w_out_all_ref, d_mlp_all_ref, gate_up_ref,
+    buf, term, core_land, land, w_qkv, w_line, w_out, gain_land, top_land, proj, d_mlp,
     *sems,
 ):
     at = Place(line)
@@ -754,7 +771,8 @@
     reduce = plane_reduce(at, term, core_land, land, blk, sems[6:12])
     line_send, line_recv, qkv_send, qkv_recv, gain_send, gain_recv, top_send, top_recv, out_send, out_recv, own_sem, write_sem = sems[12:24]
     d_mlp_rows = slice_rows(d_mlp_all_ref, blk)
-    beside = SliceGather(at, d_mlp_rows, blk, sems[24:])
+    beside = SliceGather(at, d_mlp_rows, blk, sems[24:30])
+    spread = ColumnSpread(at, w_gate_up_ref, gate_up_ref, gate_up_ref.shape[1] // 2, *sems[30:])
     w_rows, width = w_out_ref.shape
     size = 8 * blk
     mine = pl.ds(pl.multiple_of(at.c * blk, blk), blk)
@@ -764,10 +782,13 @@
         pltpu.make_async_copy(gains_ref, gain_land.at[at.me], own_sem.at[1]),
         pltpu.make_async_copy(w_qkv_ref, w_line.at[at.z], own_sem.at[2]),
         pltpu.make_async_copy(w_out_ref, w_out.at[at.z], own_sem.at[3]),
-        pltpu.make_async_copy(d_mlp_ref, d_mlp_rows(at.z, at.q, 0, blk), own_sem.at[4]),
+        pltpu.make_async_copy(d_mlp, d_mlp_rows(at.z, at.q, 0, blk), own_sem.at[4]),
+        *spread.own([own_sem.at[5], own_sem.at[6]]),
     ]
-    for copy in own:
+    for copy in own[:4] + own[5:]:
         copy.start()
+    d_mlp[...] = (BRANCH * grad_ref[...].astype(jnp.float32)).astype(jnp.bfloat16)
+    own[4].start()
     at.greet_all()
     gain_push = (lambda other: gains_ref, lambda slot: gain_land.at[slot], gain_send, gain_recv)
     top_push = (lambda other: top_land.at[at.me], lambda slot: top_land.at[slot], top_send, top_recv)
@@ -800,6 +821,7 @@
     at.push_all(*gain_push)
     turn()
     qkv_step(1)
+    spread.start()
     rest()
     for k in range(2, line - 1):
         qkv_step(k)
@@ -919,11 +941,14 @@
 
     for k in range(line):
         beside.c(k)
+    spread.wait()
+    for copy in own[5:]:
+        copy.wait()
     for copy in writes:
         copy.wait()
 
 
-def front(line, tokens, d_mlp, gains, w_qkv, w_out, q_seg, k_seg):
+def front(line, tokens, grad, w_gate_up, gains, w_qkv, w_out, q_seg, k_seg):
     blk, width = tokens.shape
     w_rows, cols = w_out.shape[0], w_qkv.shape[2]
     size, every = 8 * blk, 8 * line
@@ -946,9 +971,10 @@
             out((every, w_rows, cols), bf16),
             out((line, w_rows, width), bf16),
             out((line * 4 * blk, width), bf16),
+            out((width, w_gate_up.shape[1] // every), bf16),
         ),
-        in_specs=[any_spec] * 5 + [vmem_spec] * 2,
-        out_specs=(vmem_spec,) * 7 + (any_spec,) * 4,
+        in_specs=[any_spec, vmem_spec] + [any_spec] * 4 + [vmem_spec] * 2,
+        out_specs=(vmem_spec,) * 7 + (any_spec,) * 5,
         scratch_shapes=[
             pltpu.VMEM((size, width), bf16),
             pltpu.VMEM((size, width), bf16),
@@ -960,6 +986,7 @@
             pltpu.VMEM((every, 16, 128), bf16),
             pltpu.VMEM((every, 8, 128), f32),
             pltpu.VMEM((blk, width), f32),
+            pltpu.VMEM((blk, width), bf16),
             *[dma((n,)) for n in GATHER_SEMS + REDUCE_SEMS],
             dma((line, 2)),
             dma((line,)),
@@ -967,26 +994,36 @@
             *[dma((every,))] * 5,
             dma((line, 2)),
             dma((line,)),
-            dma((5,)),
+            dma((7,)),
             dma((3,)),
             *slice_gather_sems(line),
+            dma((2, every)),
+            dma((2, every)),
         ],
         compiler_params=pltpu.CompilerParams(collective_id=1, has_side_effects=True, vmem_limit_bytes=60 * MIB),
-    )(tokens, d_mlp, gains, w_qkv, w_out, q_seg, k_seg)
+    )(tokens, grad, w_gate_up, gains, w_qkv, w_out, q_seg, k_seg)
 
 
 def back_kernel(
     line, blk, q_part, kv_part,
-    d_attn_ref, tokens_ref, mid_ref, d_mid_ref, qkv_ref, attn_ref, lse_ref, gain_ref, gain_term_ref, q_seg_ref, k_seg_ref, normed_ref, w_qkv_ref, w_out_ref, mlp_term_ref,
-    mixed_ref, grad_tokens_ref, grad_qkv_ref, grad_out_ref, gain_sum_ref,
-    buf, term, core_land, land, w_qkv, w_out, normed, d_heads, d_qkv, dk_sum, dv_sum, stage_qkv, stage_out, qkv_land, out_land, gain_stage, gain_land, d_normed, mlp_term, mlp_land, mlp_line_land, mlp_sum,
+    d_attn_ref, tokens_ref, mid_ref, d_mid_ref, qkv_ref, attn_ref, lse_ref, gain_ref, gain_term_ref, q_seg_ref, k_seg_ref, normed_ref, w_qkv_ref, w_out_ref, mlp_term_ref, columns_ref,
+    mixed_ref, grad_tokens_ref, grad_qkv_ref, grad_out_ref, gain_sum_ref, grad_gate_up_ref,
+    buf, term, core_land, land, w_qkv, w_out, normed, d_heads, d_qkv, dk_sum, dv_sum, stage_qkv, stage_out, qkv_land, out_land, gain_stage, gain_land, d_normed, mlp_term, mlp_land, mlp_line_land, mlp_sum, row_land, row_stage,
     *sems,
 ):
     at = Place(line)
     gather = plane_gather(at, buf, blk, sems[:6])
     reduce = plane_reduce(at, term, core_land, land, blk, sems[6:12])
     qkv_send, qkv_recv, gain_send, gain_recv, out_send, out_recv, own_sem = sems[12:19]
-    beside = SliceReduce(at, slice_rows(mlp_term, blk), blk, mlp_land, mlp_line_land, mlp_sum, sems[19:])
+    beside = SliceReduce(at, slice_rows(mlp_term, blk), blk, mlp_land, mlp_line_land, mlp_sum, sems[19:25])
+    row_send, row_recv, row_sem = sems[25:]
+    w_cols = w_qkv.shape[1]
+    part_ff = columns_ref.shape[1] // 2
+
+    def column_rows(other):
+        return columns_ref.at[pl.ds(pl.multiple_of(other * w_cols, w_cols), w_cols), :]
+
+    row_push = (column_rows, lambda slot: row_land.at[slot], row_send, row_recv)
     width = buf.shape[1]
     w_rows = w_out.shape[1]
     size = 8 * blk
@@ -997,6 +1034,7 @@
         pltpu.make_async_copy(w_qkv_ref, w_qkv, own_sem.at[2]),
         pltpu.make_async_copy(normed_ref, normed, own_sem.at[3]),
         pltpu.make_async_copy(mlp_term_ref, mlp_term, own_sem.at[4]),
+        pltpu.make_async_copy(column_rows(at.me), row_land.at[at.me], own_sem.at[5]),
     ]
     for copy in own:
         copy.start()
@@ -1006,6 +1044,7 @@
     start()
     turn()
     rest()
+    at.push_all(*row_push)
     for copy in own[1:]:
         copy.wait()
     beside.a(line - 1)
@@ -1090,7 +1129,7 @@
         beside.b(k)
 
     gain_stage[...] = jnp.zeros_like(gain_stage)
-    gain_stage[1:2, :] = gain_term_ref[...]
+    gain_stage[1:2, :] = gain_term_ref[0:1, :]
 
     @pl.loop(0, blk // 32)
     def _(i):
@@ -1106,6 +1145,16 @@
     gain_push = (gain_tile, lambda slot: gain_land.at[slot], gain_send, gain_recv)
     at.push_all(*gain_push)
     gain_land[at.me] = gain_stage[:, pl.ds(pl.multiple_of((at.me // 2) * 128, 128), 128)]
+
+    at.wait_all(*row_push, sent=False)
+
+    @pl.loop(0, at.every)
+    def _(j):
+        span = pl.ds(pl.multiple_of(j * w_cols, w_cols), w_cols)
+        row_stage[span, :] = row_land[j].astype(jnp.float32)
+        for i in (0, 1):
+            target = grad_gate_up_ref.at[:, pl.ds(pl.multiple_of((i * at.every + j) * part_ff, part_ff), part_ff)]
+            pltpu.make_async_copy(row_stage.at[span, pl.ds(i * part_ff, part_ff)], target, row_sem.at[0]).start()
 
     for k in range(line - 1, -1, -1):
         beside.c(k)
@@ -1131,13 +1180,15 @@
     reduce[2]()
     for k in range(line):
         beside.end(k)
+    at.wait_all(*row_push)
+    pltpu.make_async_copy(grad_gate_up_ref, grad_gate_up_ref, row_sem.at[0]).wait()
     at.wait_all(*qkv_push)
     at.wait_all(*gain_push)
     for i in range(1, line):
         out_copy(i).wait_send()
 
 
-def back(line, d_attn, tokens, mid, d_mid, qkv, attn_out, lse, gain, gain_term, q_seg, k_seg, normed, w_qkv, w_out, mlp_term):
+def back(line, d_attn, tokens, mid, d_mid, qkv, attn_out, lse, gain, gain_term, q_seg, k_seg, normed, w_qkv, w_out, mlp_term, columns):
     blk, width = tokens.shape
     w_rows, cols = w_out.shape[1], w_qkv.shape[2]
     size, every = 8 * blk, 8 * line
@@ -1147,9 +1198,9 @@
     bf16, f32, dma, out = jnp.bfloat16, jnp.float32, pltpu.SemaphoreType.DMA, jax.ShapeDtypeStruct
     return pl.pallas_call(
         functools.partial(back_kernel, line, blk, q_part, kv_part),
-        out_shape=(out((blk, width), bf16), out((blk, width), f32), out((8, w_rows, cols), f32), out((w_rows, width), f32), out((8, 128), f32)),
-        in_specs=[any_spec] + [vmem_spec] * 10 + [any_spec] * 4,
-        out_specs=(vmem_spec,) * 5,
+        out_shape=(out((blk, width), bf16), out((blk, width), f32), out((8, w_rows, cols), f32), out((w_rows, width), f32), out((8, 128), f32), out((w_rows, every * columns.shape[1]), f32)),
+        in_specs=[any_spec] + [vmem_spec] * 10 + [any_spec] * 5,
+        out_specs=(vmem_spec,) * 5 + (any_spec,),
         scratch_shapes=[
             pltpu.VMEM((size, width), bf16),
             pltpu.VMEM((size, width), bf16),
@@ -1173,11 +1224,16 @@
             pltpu.VMEM((line, 3 * blk, width), bf16),
             pltpu.VMEM((line + 1, blk, width), bf16),
             pltpu.VMEM((blk, width), f32),
-            *[dma((n,)) for n in GATHER_SEMS + REDUCE_SEMS + (every,) * 4 + (line, line, 5)],
+            pltpu.VMEM((every, w_rows, columns.shape[1]), bf16),
+            pltpu.VMEM(columns.shape, f32),
+            *[dma((n,)) for n in GATHER_SEMS + REDUCE_SEMS + (every,) * 4 + (line, line, 6)],
             *slice_reduce_sems(line),
+            dma((every,)),
+            dma((every,)),
+            dma((1,)),
         ],
-        compiler_params=pltpu.CompilerParams(collective_id=2, has_side_effects=True, vmem_limit_bytes=60 * MIB),
-    )(d_attn, tokens, mid, d_mid, qkv, attn_out, lse, gain, gain_term, q_seg, k_seg, normed, w_qkv, w_out, mlp_term)
+        compiler_params=pltpu.CompilerParams(collective_id=2, has_side_effects=True, vmem_limit_bytes=63 * MIB),
+    )(d_attn, tokens, mid, d_mid, qkv, attn_out, lse, gain, gain_term, q_seg, k_seg, normed, w_qkv, w_out, mlp_term, columns)
 
 
 def split_heads(w, parts):
@@ -1288,7 +1344,7 @@
     count, width = tokens.shape[1:]
     w_rows = w_qkv.shape[0]
     rows = tokens.reshape(count, width)
-    grad_rows = cotangent.reshape(count, width).astype(jnp.float32)
+    grad = cotangent.reshape(count, width)
     size = count * 8
     seg = segment_ids(jnp.arange(size, dtype=jnp.int32), lengths[0])
     q_seg, k_seg = seg.reshape(size, 1), seg.reshape(1, size)
@@ -1298,20 +1354,18 @@
     none = jnp.zeros_like(gains)
     gains = jnp.where(side == 0, jnp.concatenate([gains, none], axis=1), jnp.concatenate([none, gains], axis=1))
     gains = jnp.pad(gains, ((0, 14), (0, 0)))
-    mid, normed_two, qkv, attn_out, lse, tops, gain, normed_one, qkv_mine, out_mine, d_mlp = front(
-        n_shard, rows, (BRANCH * grad_rows).astype(jnp.bfloat16), gains, split_heads(w_qkv, 8).transpose(1, 0, 2), w_out, q_seg, k_seg
+    mid, normed_two, qkv, attn_out, lse, tops, gain, normed_one, qkv_mine, out_mine, d_mlp, gate_up_mine = front(
+        n_shard, rows, grad, w_gate_up, gains, split_heads(w_qkv, 8).transpose(1, 0, 2), w_out, q_seg, k_seg
     )
     heads = HEADS // 8
     head_top = jnp.max(tops[:, 0, :heads].reshape(8, n_shard, heads), axis=1).reshape(HEADS)
     clip = CLIP_TARGET / jnp.maximum(head_top, CLIP_TARGET)
 
-    mlp_term, d_normed_two, grad_gate_up, grad_down = mlp_exchange(n_shard, normed_two, d_mlp, w_gate_up, w_down)
-    d_mid_norm, gain_two_term = norm_backward(d_normed_two, mid, rms_scale(mid), gain[1:2])
-    d_mid = grad_rows + d_mid_norm
-
-    d_attn = (BRANCH * d_mid).astype(jnp.bfloat16)
-    mixed, grad_tokens, qkv_grad, grad_out, gain_sum = back(
-        n_shard, d_attn, rows, mid, d_mid, qkv, attn_out, lse, gain, gain_two_term.reshape(1, width), q_seg, k_seg, normed_one, qkv_mine, out_mine, mlp_term
+    mlp_term, d_mid, d_attn, gain_term, gate_up_grad, grad_down = mlp_exchange(
+        n_shard, normed_two, d_mlp, gate_up_mine, w_down, mid, grad, gain
+    )
+    mixed, grad_tokens, qkv_grad, grad_out, gain_sum, grad_gate_up = back(
+        n_shard, d_attn, rows, mid, d_mid, qkv, attn_out, lse, gain, gain_term, q_seg, k_seg, normed_one, qkv_mine, out_mine, mlp_term, gate_up_grad
     )
     grad_qkv = join_heads(qkv_grad.transpose(1, 0, 2), 8)
     gain_grads = jnp.where(side == 0, gain_sum[:2, :w_rows], gain_sum[:2, w_rows : 2 * w_rows])

time: 577 us -> 543 us (0.941)
  Pallas kernels: 536 us -> 513 us
  other arithmetic: 13.2 us -> 4.31 us
    pallas_call x1, Pallas kernels: 237 us -> 155 us  [mlp_exchange(): pl.pallas_call(functools.partial(mlp_kernel, line, blk, part), out_shape=...]
    pallas_call x1, Pallas kernels: 148 us -> 179 us  [front(): pl.pallas_call(functools.partial(front_kernel, line, blk, q_part, kv_part...]
    pallas_call x1, Pallas kernels: 151 us -> 178 us  [back(): pl.pallas_call(functools.partial(back_kernel, line, blk, q_part, kv_part)...]
where the time goes in v5:
time: 543 us; the launch traced here: 535 us
  Pallas kernels  513 us (94%)
  local copies, waits for them, and re-layouts  15.7 us (3%)
    pallas_call x1, Pallas kernels, front(): pl.pallas_call(functools.partial(front_kernel, line, blk, q_part, kv_part...  179 us
    pallas_call x1, Pallas kernels, back(): pl.pallas_call(functools.partial(back_kernel, line, blk, q_part, kv_part)...  178 us
    pallas_call x1, Pallas kernels, mlp_exchange(): pl.pallas_call(functools.partial(mlp_kernel, line, blk, part), out_shape=...  155 us

profile of v5, /device:TPU:0, one launch (start us, length us, event | category | flops | bytes accessed | tf_op | source)
XLA Modules:
  0.0 534.6 jit_solution(10033023168882379606)
XLA Ops:
  0.6 0.8 reduce-window.4
  1.5 0.7 pad_maximum_fusion.1
  2.2 0.1 broadcast_select_fusion
  2.2 0.1 convert_reduce_fusion
  2.3 0.0 copy-start.5
  2.3 0.6 pad.6.gains_ref
  2.9 0.9 fusion.1
  3.8 0.1 reshape_reshape.6
  4.0 0.1 reshape_reshape.7
  4.1 1.0 slice.37
  5.1 0.9 maximum_bitcast_fusion.w_qkv_ref
  6.0 1.0 copy.41.q_seg_ref
  7.0 179.4 %shard_map.160 = (f32[128,2048]{1,0:T(8,128)}, bf16[128,2048]{1,0:T(8,128)(2,1)}, bf16[1024,384]{1,0:T(8,128)(2,1)}, bf16[1024,256]{1,0:T(8,128)(2,1)}, f32[1024...) custom-call(bf16[128,2048]{1,0:T(8,128)(2,1)} %bitcast.26, ...), custom_call_target="tpu_custom_call" | custom-call | tf_op jit(solution)/shard_map/pallas_call | solution.py:960
  186.4 0.9 slice.48
  187.3 0.6 div.7
  187.9 155.5 %shard_map.161 = (bf16[2048,2048]{1,0:T(8,128)(2,1)}, f32[128,2048]{1,0:T(8,128)}, bf16[128,2048]{1,0:T(8,128)(2,1)}, f32[8,2048]{1,0:T(8,128)}, bf16[2048,512]{1,0:T(8,128)(2,1)}, /*index=5*/f32[256,2048]{1,0:T(8,128)}) custom-call(bf16[128,2048]{1,0:T(8,128)(2,1)} %get-tuple-element.33.normed_ref, bf16[2048,2048]{1,0:T(8,128)(2,1)} %get-tuple-element.34.d_mlp_ref, ...), custom_call_target="tpu_custom_call" | custom-call | tf_op jit(solution)/shard_map/pallas_call | solution.py:593
  343.4 178.5 %shard_map.162 = (bf16[128,2048]{1,0:T(8,128)(2,1)}, f32[128,2048]{1,0:T(8,128)}, f32[8,64,384]{2,1,0:T(8,128)}, f32[64,2048]{1,0:T(8,128)}, f32[8,128]{1,0:T(8,128)}, /*index=5*/f32[64,16384]{1,0:T(8,128)}) custom-call(bf16[128,2048]{1,0:T(8,128)(2,1)} %get-tuple-element.38.d_attn_ref, bf16[128,2048]{1,0:T(8,128)(2,1)} %bitcast.27, ...), custom_call_target="tpu_custom_call" | custom-call | tf_op jit(solution)/shard_map/pallas_call | solution.py:1199
  521.9 0.8 slice_select_fusion
  522.8 0.5 slice_bitcast_fusion.1
  523.3 1.1 slice_bitcast_fusion
  524.4 1.2 fusion
  525.6 0.2 copy.44
  525.8 0.1 reshape.78
  525.9 0.2 copy.45
  526.1 0.1 reshape.79
  526.2 0.9 pad_maximum_fusion
  527.2 0.8 copy.60
  528.0 1.0 copy.61
  528.9 0.8 copy.62
  529.7 2.1 copy.63
  531.9 1.0 copy-done.1
  532.8 1.3 copy.64
  (17 shorter events, 0.1 us)
Async XLA Ops:
  2.3 4.7 copy-start.5
  525.8 1.4 copy-start.4
  525.9 2.1 copy-start.2
  526.1 2.8 copy-start.3
  526.2 3.5 copy-start
  529.7 3.1 copy-start.1

commit v6 on v5

--- a/solution.py
+++ b/solution.py
@@ -202,6 +202,10 @@
         other = lax.rem(self.me + i, self.every)
         return other, (other // self.line, other % self.line)
 
+    def greet_near(self):
+        z, last = self.z, self.line - 1
+        greet([self.cx, self.cy, self.sibling], [(z < last, (self.c, z + 1)), (z > 0, (self.c, z - 1))])
+
     def greet_all(self):
         barrier = pltpu.get_barrier_semaphore()
 
@@ -211,8 +215,8 @@
 
         pl.semaphore_wait(barrier, self.every - 1)
 
-    def push_all(self, source, target, send_sems, recv_sems):
-        @pl.loop(1, self.every)
+    def push_all(self, source, target, send_sems, recv_sems, piece=0, pieces=1):
+        @pl.loop(max(1, piece * self.every // pieces), (piece + 1) * self.every // pieces)
         def _(i):
             other, device = self.peer(i)
             remote(source(other), target(self.me), send_sems.at[other], recv_sems.at[self.me], device).start()
@@ -302,15 +306,19 @@
             self.rows(at, chip, first, self.half), self.landing(at, lands, self.half), self.r3_send.at[at, i], self.r3_recv.at[at, i], device
         )
 
-    def line_copy(self, at, way):
+    def line_part(self, at, slot, part):
+        rows = pl.ds(part * self.half, self.half)
+        return self.rows(at, self.place.q, part * self.half, self.half), self.line_land.at[slot, rows, :]
+
+    def line_copy(self, at, way, part):
         p = self.place
         slot = jnp.where((way == 1) & (at == p.z - 1), p.line, at)
-        return remote(
-            self.rows(at, p.q, 0, self.blk), self.line_land.at[slot], self.r4_send.at[at], self.r4_recv.at[slot], (p.c, p.z + 1 - 2 * way)
-        )
-
-    def line_arrival(self, at, slot):
-        return remote(self.rows(at, self.place.q, 0, self.blk), self.line_land.at[slot], self.r4_send.at[at], self.r4_recv.at[slot], self.place.sibling)
+        source, target = self.line_part(at, slot, part)
+        return remote(source, target, self.r4_send.at[at, part], self.r4_recv.at[slot, part], (p.c, p.z + 1 - 2 * way))
+
+    def line_arrival(self, at, slot, part):
+        source, target = self.line_part(at, slot, part)
+        return remote(source, target, self.r4_send.at[at, part], self.r4_recv.at[slot, part], self.place.sibling)
 
     def a(self, k):
         at = self.place.source(k)
@@ -333,34 +341,37 @@
         has_up, has_down = p.z < p.line - 1, p.z > 0
         for i in range(4):
             self.third(at, i).wait_recv()
-        mine = self.rows(at, p.q, 0, blk)
-        plane = [self.landing(at, 0, blk), self.landing(at, blk, blk)]
-        if k > 0:
-            joined = ((at > p.z) & has_down) | ((at < p.z) & has_up)
-
-            @pl.when(joined)
-            def _():
-                self.line_arrival(at, at).wait_recv()
-                add_rows(mine, plane + [self.line_land.at[at]], blk)
-
-            @pl.when(jnp.logical_not(joined))
-            def _():
-                add_rows(mine, plane, blk)
-
-            for way, condition in enumerate((at > p.z, at < p.z)):
-
-                @pl.when(condition)
+        half = self.half
+        joined = ((at > p.z) & has_down) | ((at < p.z) & has_up)
+        for part in (0, 1):
+            mine = self.rows(at, p.q, part * half, half)
+            plane = [self.landing(at, part * half, half), self.landing(at, blk + part * half, half)]
+            if k > 0:
+
+                @pl.when(joined)
                 def _():
-                    self.line_copy(at, way).start()
-
-        else:
-            add_rows(mine, plane, blk, self.result)
-            for condition, slot in ((has_down, at), (has_up, p.line)):
-
-                @pl.when(condition)
+                    self.line_arrival(at, at, part).wait_recv()
+                    add_rows(mine, plane + [self.line_part(at, at, part)[1]], half)
+
+                @pl.when(jnp.logical_not(joined))
                 def _():
-                    self.line_arrival(at, slot).wait_recv()
-                    add_rows(self.result, [self.line_land.at[slot]], blk, self.result)
+                    add_rows(mine, plane, half)
+
+                for way, condition in enumerate((at > p.z, at < p.z)):
+
+                    @pl.when(condition)
+                    def _():
+                        self.line_copy(at, way, part).start()
+
+            else:
+                result = self.result.at[pl.ds(part * half, half), :]
+                add_rows(mine, plane, half, result)
+                for condition, slot in ((has_down, at), (has_up, p.line)):
+
+                    @pl.when(condition)
+                    def _():
+                        self.line_arrival(at, slot, part).wait_recv()
+                        add_rows(result, [self.line_part(at, slot, part)[1]], half, result)
 
     def end(self, k):
         at = self.place.source(k)
@@ -369,11 +380,60 @@
         for i in range(4):
             self.third(at, i).wait_send()
         if k > 0:
-            self.line_copy(at, 0).wait_send()
+            for part in (0, 1):
+                self.line_copy(at, 0, part).wait_send()
+
+
+class LineReduce:
+    def __init__(self, place, block, land, rows, sems):
+        self.place, self.block, self.land, self.rows = place, block, land, rows
+        self.send, self.recv = sems
+
+    def copy(self, at, way):
+        p = self.place
+        slot = jnp.where((way == 1) & (at == p.z - 1), p.line, at)
+        return remote(self.block(at), self.land.at[slot], self.send.at[at], self.recv.at[slot], (p.c, p.z + 1 - 2 * way))
+
+    def arrive(self, at, slot):
+        p = self.place
+        remote(self.block(at), self.land.at[slot], self.send.at[at], self.recv.at[slot], p.sibling).wait_recv()
+        add_rows(self.block(at), [self.land.at[slot]], self.rows)
+
+    def each(self, k, joined, after):
+        p = self.place
+        at = p.source(k)
+        for way, toward, behind in ((0, at > p.z, p.z > 0), (1, at < p.z, p.z < p.line - 1)):
+
+            @pl.when(toward & (behind if joined else jnp.logical_not(behind)))
+            def _():
+                after(at, way)
+
+    def first(self):
+        for k in range(self.place.line - 1, 0, -1):
+            self.each(k, False, lambda at, way: self.copy(at, way).start())
+
+    def join(self, k):
+        def step(at, way):
+            self.arrive(at, at)
+            self.copy(at, way).start()
+
+        self.each(k, True, step)
+
+    def last(self):
+        p = self.place
+        for condition, slot in ((p.z > 0, p.z), (p.z < p.line - 1, p.line)):
+
+            @pl.when(condition)
+            def _():
+                self.arrive(p.z, slot)
+
+    def end(self):
+        for k in range(1, self.place.line):
+            self.copy(self.place.source(k), 0).wait_send()
 
 
 def slice_reduce_sems(line):
-    return [pltpu.SemaphoreType.DMA(shape) for shape in ((line, 2), (line, 2), (line, 4), (line, 4), (line,), (line + 1,))]
+    return [pltpu.SemaphoreType.DMA(shape) for shape in ((line, 2), (line, 2), (line, 4), (line, 4), (line, 2), (line + 1, 2))]
 
 
 def slice_rows(ref, blk):
@@ -394,8 +454,10 @@
             columns = self.source.at[:, pl.ds(pl.multiple_of((j * self.place.every + other) * self.part, self.part), self.part)]
             yield j, columns, self.target.at[pl.ds(pl.multiple_of(slot * rows, rows), rows), pl.ds(j * self.part, self.part)]
 
-    def start(self):
-        @pl.loop(1, self.place.every)
+    def start(self, piece, pieces):
+        every = self.place.every
+
+        @pl.loop(max(1, piece * every // pieces), (piece + 1) * every // pieces)
         def _(i):
             other, device = self.place.peer(i)
             for j, source, target in self.copies(other, self.place.me):
@@ -518,7 +580,7 @@
 
     for copy in [own, d_mlp_in] + own_weights:
         copy.start()
-    place.greet_all()
+    place.greet_near()
     own.wait()
     gather.a(0)
     for copy in weights_to:
@@ -821,7 +883,8 @@
     at.push_all(*gain_push)
     turn()
     qkv_step(1)
-    spread.start()
+    own[4].wait()
+    beside.a(0)
     rest()
     for k in range(2, line - 1):
         qkv_step(k)
@@ -830,8 +893,7 @@
     for i in range(at.every // 2):
         pair = gain_land[2 * i].astype(jnp.float32) + gain_land[2 * i + 1].astype(jnp.float32)
         gain_ref[:, i * 128 : (i + 1) * 128] = pair[:8, :]
-    own[4].wait()
-    beside.a(0)
+    spread.start(0, 4)
     whole()
     end()
     at.wait_all(*gain_push)
@@ -852,6 +914,8 @@
     own[3].wait()
     at.line_spread(out_line, 0)
     beside.b(0)
+    beside.a(1)
+    spread.start(1, 4)
     for k in range(line):
 
         @pl.loop(1, 8)
@@ -866,13 +930,18 @@
         qkv_ref[part, :] = dot(buf[part, :], w_qkv[...].reshape(width, q_part + 2 * kv_part), ((1,), (0,))).astype(jnp.bfloat16)
 
     at.line_spread(out_line, 1)
-    beside.a(1)
+    beside.b(1)
+    beside.a(2)
+    spread.start(2, 4)
     heads = q_part // HEAD_DIM
     block = math.gcd(size, 256)
     tops = [jnp.full((1, 1), NEGATIVE, jnp.float32)] * heads
     for i in range(size // block):
         if i > 0 and i + 1 < line:
             at.line_spread(out_line, i + 1)
+        if i == 2:
+            beside.b(2)
+            beside.a(3)
         rows, cols = pl.ds(i * block, block), (i + 1) * block
         live = seen_mask(i * block, block, cols, q_seg_ref[rows, :], k_seg_ref[:, :cols])
         keys, values = qkv_ref[:cols, q_part : q_part + kv_part], qkv_ref[:cols, q_part + kv_part :]
@@ -896,8 +965,8 @@
 
     for k in range(size // block + 1, line):
         at.line_spread(out_line, k)
-    beside.b(1)
-    beside.a(2)
+    beside.b(3)
+    spread.start(3, 4)
     writes[2].start()
     for i, chip in enumerate((at.qd, at.qx, at.qy, at.q)):
         for core in (1 - at.core, at.core):
@@ -911,10 +980,6 @@
 
         reduce[0](i)
     reduce[1](proj)
-    beside.b(2)
-    for k in range(3, line):
-        beside.a(k)
-        beside.b(k)
 
     own_again = pltpu.make_async_copy(tokens_ref, land.at[pl.ds(0, blk), :], own_sem.at[0])
     own_again.start()
@@ -1008,7 +1073,7 @@
     line, blk, q_part, kv_part,
     d_attn_ref, tokens_ref, mid_ref, d_mid_ref, qkv_ref, attn_ref, lse_ref, gain_ref, gain_term_ref, q_seg_ref, k_seg_ref, normed_ref, w_qkv_ref, w_out_ref, mlp_term_ref, columns_ref,
     mixed_ref, grad_tokens_ref, grad_qkv_ref, grad_out_ref, gain_sum_ref, grad_gate_up_ref,
-    buf, term, core_land, land, w_qkv, w_out, normed, d_heads, d_qkv, dk_sum, dv_sum, stage_qkv, stage_out, qkv_land, out_land, gain_stage, gain_land, d_normed, mlp_term, mlp_land, mlp_line_land, mlp_sum, row_land, row_stage,
+    buf, term, core_land, land, w_qkv, w_out, normed, d_heads, d_qkv, dk_sum, dv_sum, stage_qkv, stage_out, qkv_land, out_land, gain_stage, gain_land, d_normed, mlp_term, mlp_land, mlp_line_land, mlp_sum, row_land, row_stage, qkv_line_land,
     *sems,
 ):
     at = Place(line)
@@ -1016,7 +1081,7 @@
     reduce = plane_reduce(at, term, core_land, land, blk, sems[6:12])
     qkv_send, qkv_recv, gain_send, gain_recv, out_send, out_recv, own_sem = sems[12:19]
     beside = SliceReduce(at, slice_rows(mlp_term, blk), blk, mlp_land, mlp_line_land, mlp_sum, sems[19:25])
-    row_send, row_recv, row_sem = sems[25:]
+    row_send, row_recv, row_sem = sems[25:28]
     w_cols = w_qkv.shape[1]
     part_ff = columns_ref.shape[1] // 2
 
@@ -1111,20 +1176,33 @@
 
         reduce[0](i)
 
-    @pl.loop(0, width // 256)
+    chunk = line * w_cols
+
+    @pl.loop(0, 8)
     def _(i):
-        span = pl.ds(pl.multiple_of(i * 256, 256), 256)
-        blocks = pl.ds(pl.multiple_of(i * (256 // w_rows), 256 // w_rows), 256 // w_rows)
-        grads = dot(normed[:, span], d_qkv[...], ((0,), (0,))).astype(jnp.bfloat16)
-        stage_qkv[blocks] = grads.reshape(256 // w_rows, w_rows, q_part + 2 * kv_part)
-
-    qkv_push = (lambda other: stage_qkv.at[other], lambda slot: qkv_land.at[slot], qkv_send, qkv_recv)
-    at.push_all(*qkv_push)
-    qkv_land[at.me] = stage_qkv[at.me]
+        grads = dot(normed[:, pl.ds(pl.multiple_of(i * chunk, chunk), chunk)], d_qkv[...], ((0,), (0,))).astype(jnp.bfloat16)
+        for place in range(line):
+            stage_qkv[pl.ds(pl.multiple_of((place * 8 + i) * w_cols, w_cols), w_cols), :] = grads[place * w_cols : (place + 1) * w_cols, :]
+
+    def qkv_block(place):
+        return stage_qkv.at[pl.ds(pl.multiple_of(place * 8 * w_cols, w_cols), 8 * w_cols), :]
+
+    def qkv_rows(i):
+        return stage_qkv.at[pl.ds(pl.multiple_of((at.z * 8 + i) * w_cols, w_cols), w_cols), :]
+
+    def qkv_copy(i, arriving=False):
+        other = lax.rem(at.c + i, 8)
+        slot = other if arriving else at.c
+        return remote(qkv_rows(other), qkv_land.at[slot], qkv_send.at[other], qkv_recv.at[slot], (other, at.z))
+
+    sum_qkv = LineReduce(at, qkv_block, qkv_line_land, 8 * w_cols, sems[28:])
+    sum_qkv.first()
     out_land[at.z] = stage_out[at.z]
     reduce[1](d_normed)
     if line > 2:
         beside.a(0)
+    for k in range(line - 1, 0, -1):
+        sum_qkv.join(k)
     for k in range(line - 2, -1, -1):
         beside.b(k)
 
@@ -1146,6 +1224,13 @@
     at.push_all(*gain_push)
     gain_land[at.me] = gain_stage[:, pl.ds(pl.multiple_of((at.me // 2) * 128, 128), 128)]
 
+    sum_qkv.last()
+
+    @pl.loop(1, 8)
+    def _(i):
+        qkv_copy(i).start()
+
+    qkv_land[at.c] = stage_qkv[pl.ds(pl.multiple_of((at.z * 8 + at.c) * w_cols, w_cols), w_cols), :]
     at.wait_all(*row_push, sent=False)
 
     @pl.loop(0, at.every)
@@ -1165,15 +1250,11 @@
     for i in range(1, line):
         total = total + out_land[i].astype(jnp.float32)
     grad_out_ref[...] = total
-    at.wait_all(*qkv_push, sent=False)
-
-    @pl.loop(0, 8)
+    @pl.loop(1, 8)
     def _(i):
-        total = qkv_land[i * line].astype(jnp.float32)
-        for j in range(1, line):
-            total = total + qkv_land[i * line + j].astype(jnp.float32)
-        grad_qkv_ref[i] = total
-
+        qkv_copy(i, True).wait_recv()
+
+    grad_qkv_ref[...] = qkv_land[...].astype(jnp.float32)
     at.wait_all(*gain_push, sent=False)
     gain_sum_ref[...] = jnp.sum(gain_land[...], axis=0)
     end()
@@ -1182,7 +1263,12 @@
         beside.end(k)
     at.wait_all(*row_push)
     pltpu.make_async_copy(grad_gate_up_ref, grad_gate_up_ref, row_sem.at[0]).wait()
-    at.wait_all(*qkv_push)
+    sum_qkv.end()
+
+    @pl.loop(1, 8)
+    def _(i):
+        qkv_copy(i).wait_send()
+
     at.wait_all(*gain_push)
     for i in range(1, line):
         out_copy(i).wait_send()
@@ -1213,9 +1299,9 @@
             pltpu.VMEM((size, cols), bf16),
             pltpu.VMEM((size, kv_part), f32),
             pltpu.VMEM((size, kv_part), f32),
-            pltpu.VMEM((every, w_rows, cols), bf16),
+            pltpu.VMEM((every * w_rows, cols), bf16),
             pltpu.VMEM((line, w_rows, width), bf16),
-            pltpu.VMEM((every, w_rows, cols), bf16),
+            pltpu.VMEM((8, w_rows, cols), bf16),
             pltpu.VMEM((line, w_rows, width), bf16),
             pltpu.VMEM((8, width), f32),
             pltpu.VMEM((every, 8, 128), f32),
@@ -1226,11 +1312,14 @@
             pltpu.VMEM((blk, width), f32),
             pltpu.VMEM((every, w_rows, columns.shape[1]), bf16),
             pltpu.VMEM(columns.shape, f32),
+            pltpu.VMEM((line + 1, 8 * w_rows, cols), bf16),
             *[dma((n,)) for n in GATHER_SEMS + REDUCE_SEMS + (every,) * 4 + (line, line, 6)],
             *slice_reduce_sems(line),
             dma((every,)),
             dma((every,)),
             dma((1,)),
+            dma((line,)),
+            dma((line + 1,)),
         ],
         compiler_params=pltpu.CompilerParams(collective_id=2, has_side_effects=True, vmem_limit_bytes=63 * MIB),
     )(d_attn, tokens, mid, d_mid, qkv, attn_out, lse, gain, gain_term, q_seg, k_seg, normed, w_qkv, w_out, mlp_term, columns)
@@ -1375,7 +1464,7 @@
 def solution(mesh):
     by_token, by_row = P("shard", "ctx", None), P(EVERY, None)
     n_ctx, n_shard = mesh.shape["ctx"], mesh.shape["shard"]
-    program = functools.partial(on_planes, n_shard) if n_ctx == 8 else functools.partial(per_device, n_ctx, n_shard)
+    program = functools.partial(on_planes, n_shard) if (n_ctx, n_shard) == (8, 4) else functools.partial(per_device, n_ctx, n_shard)
     return jax.shard_map(
         program,
         mesh=mesh,

time: 543 us -> 520 us (0.958)
  Pallas kernels: 513 us -> 491 us
    pallas_call x1, Pallas kernels: 178 us -> 167 us  [back(): pl.pallas_call(functools.partial(back_kernel, line, blk, q_part, kv_part)...]
    pallas_call x1, Pallas kernels: 179 us -> 173 us  [front(): pl.pallas_call(functools.partial(front_kernel, line, blk, q_part, kv_part...]
where the time goes in v6:
time: 520 us; the launch traced here: 512 us
  Pallas kernels  491 us (94%)
  local copies, waits for them, and re-layouts  15.7 us (3%)
    pallas_call x1, Pallas kernels, front(): pl.pallas_call(functools.partial(front_kernel, line, blk, q_part, kv_part...  173 us
    pallas_call x1, Pallas kernels, back(): pl.pallas_call(functools.partial(back_kernel, line, blk, q_part, kv_part)...  167 us
    pallas_call x1, Pallas kernels, mlp_exchange(): pl.pallas_call(functools.partial(mlp_kernel, line, blk, part), out_shape=...  150 us

profile of v6, /device:TPU:0, one launch (start us, length us, event | category | flops | bytes accessed | tf_op | source)
XLA Modules:
  0.0 512.3 jit_solution(12848346253744097705)
XLA Ops:
  0.6 0.8 reduce-window.4
  1.5 0.7 pad_maximum_fusion.1
  2.2 0.1 broadcast_select_fusion
  2.2 0.1 convert_reduce_fusion
  2.3 0.0 copy-start.5
  2.3 0.6 pad.6.gains_ref
  2.9 0.9 fusion.1
  3.8 0.1 reshape_reshape.6
  4.0 0.1 reshape_reshape.7
  4.1 1.0 slice.37
  5.1 0.9 maximum_bitcast_fusion.w_qkv_ref
  6.0 1.0 copy.41.q_seg_ref
  7.0 173.3 %shard_map.160 = (f32[128,2048]{1,0:T(8,128)}, bf16[128,2048]{1,0:T(8,128)(2,1)}, bf16[1024,384]{1,0:T(8,128)(2,1)}, bf16[1024,256]{1,0:T(8,128)(2,1)}, f32[1024...) custom-call(bf16[128,2048]{1,0:T(8,128)(2,1)} %bitcast.26, ...), custom_call_target="tpu_custom_call" | custom-call | tf_op jit(solution)/shard_map/pallas_call | solution.py:1025
  180.3 0.9 slice.48
  181.3 0.6 div.7
  181.9 150.4 %shard_map.161 = (bf16[2048,2048]{1,0:T(8,128)(2,1)}, f32[128,2048]{1,0:T(8,128)}, bf16[128,2048]{1,0:T(8,128)(2,1)}, f32[8,2048]{1,0:T(8,128)}, bf16[2048,512]{1,0:T(8,128)(2,1)}, /*index=5*/f32[256,2048]{1,0:T(8,128)}) custom-call(bf16[128,2048]{1,0:T(8,128)(2,1)} %get-tuple-element.33.normed_ref, bf16[2048,2048]{1,0:T(8,128)(2,1)} %get-tuple-element.34.d_mlp_ref, ...), custom_call_target="tpu_custom_call" | custom-call | tf_op jit(solution)/shard_map/pallas_call | solution.py:655
  332.2 167.4 %shard_map.162 = (bf16[128,2048]{1,0:T(8,128)(2,1)}, f32[128,2048]{1,0:T(8,128)}, f32[8,64,384]{2,1,0:T(8,128)}, f32[64,2048]{1,0:T(8,128)}, f32[8,128]{1,0:T(8,128)}, /*index=5*/f32[64,16384]{1,0:T(8,128)}) custom-call(bf16[128,2048]{1,0:T(8,128)(2,1)} %get-tuple-element.38.d_attn_ref, bf16[128,2048]{1,0:T(8,128)(2,1)} %bitcast.27, ...), custom_call_target="tpu_custom_call" | custom-call | tf_op jit(solution)/shard_map/pallas_call | solution.py:1285
  499.6 0.8 slice_select_fusion
  500.4 0.5 slice_bitcast_fusion.1
  501.0 1.1 slice_bitcast_fusion
  502.1 1.2 fusion
  503.3 0.2 copy.44
  503.5 0.1 reshape.78
  503.6 0.2 copy.45
  503.8 0.1 reshape.79
  503.9 0.9 pad_maximum_fusion
  504.9 0.8 copy.60
  505.7 1.0 copy.61
  506.6 0.8 copy.62
  507.4 2.1 copy.63
  509.6 1.0 copy-done.1
  510.5 1.3 copy.64
  (17 shorter events, 0.1 us)
Async XLA Ops:
  2.3 4.7 copy-start.5
  503.5 1.4 copy-start.4
  503.6 2.1 copy-start.2
  503.8 2.8 copy-start.3
  503.9 3.5 copy-start
  507.4 3.1 copy-start.1

commit v7 on v6

--- a/solution.py
+++ b/solution.py
@@ -41,6 +41,20 @@
 
 def dot(left, right, dims):
     return lax.dot_general(left, right, ((dims[0], dims[1]), ((), ())), preferred_element_type=jnp.float32)
+
+
+def segments(lengths_ref, positions):
+    bound = jnp.int32(0)
+    seg = jnp.zeros(positions.shape, jnp.int32)
+    for i in range(lengths_ref.shape[1] - 1):
+        bound = bound + lengths_ref[0, i]
+        seg = seg + jnp.where(positions >= bound, 1, 0)
+    return seg
+
+
+def block_mask(lengths_ref, row0, rows, cols):
+    q_seg = segments(lengths_ref, row0 + lax.broadcasted_iota(jnp.int32, (rows, 1), 0))
+    return seen_mask(row0, rows, cols, q_seg, segments(lengths_ref, lax.broadcasted_iota(jnp.int32, (1, cols), 1)))
 
 
 def seen_mask(row0, rows, cols, q_seg, k_seg):
@@ -823,7 +837,7 @@
 
 def front_kernel(
     line, blk, q_part, kv_part,
-    tokens_ref, grad_ref, w_gate_up_ref, gains_ref, w_qkv_ref, w_out_ref, q_seg_ref, k_seg_ref,
+    tokens_ref, grad_ref, w_gate_up_ref, gains_ref, w_qkv_ref, w_out_ref, lengths_ref,
     mid_ref, normed_two_ref, qkv_ref, attn_ref, lse_ref, tops_ref, gain_ref, normed_ref, w_qkv_all_ref, w_out_all_ref, d_mlp_all_ref, gate_up_ref,
     buf, term, core_land, land, w_qkv, w_line, w_out, gain_land, top_land, proj, d_mlp,
     *sems,
@@ -943,7 +957,7 @@
             beside.b(2)
             beside.a(3)
         rows, cols = pl.ds(i * block, block), (i + 1) * block
-        live = seen_mask(i * block, block, cols, q_seg_ref[rows, :], k_seg_ref[:, :cols])
+        live = block_mask(lengths_ref, i * block, block, cols)
         keys, values = qkv_ref[:cols, q_part : q_part + kv_part], qkv_ref[:cols, q_part + kv_part :]
         for h in range(heads):
             span = slice(h * HEAD_DIM, (h + 1) * HEAD_DIM)
@@ -1013,7 +1027,7 @@
         copy.wait()
 
 
-def front(line, tokens, grad, w_gate_up, gains, w_qkv, w_out, q_seg, k_seg):
+def front(line, tokens, grad, w_gate_up, gains, w_qkv, w_out, lengths):
     blk, width = tokens.shape
     w_rows, cols = w_out.shape[0], w_qkv.shape[2]
     size, every = 8 * blk, 8 * line
@@ -1038,7 +1052,7 @@
             out((line * 4 * blk, width), bf16),
             out((width, w_gate_up.shape[1] // every), bf16),
         ),
-        in_specs=[any_spec, vmem_spec] + [any_spec] * 4 + [vmem_spec] * 2,
+        in_specs=[any_spec, vmem_spec] + [any_spec] * 4 + [pl.BlockSpec(memory_space=pltpu.SMEM)],
         out_specs=(vmem_spec,) * 7 + (any_spec,) * 5,
         scratch_shapes=[
             pltpu.VMEM((size, width), bf16),
@@ -1066,12 +1080,12 @@
             dma((2, every)),
         ],
         compiler_params=pltpu.CompilerParams(collective_id=1, has_side_effects=True, vmem_limit_bytes=60 * MIB),
-    )(tokens, grad, w_gate_up, gains, w_qkv, w_out, q_seg, k_seg)
+    )(tokens, grad, w_gate_up, gains, w_qkv, w_out, lengths)
 
 
 def back_kernel(
     line, blk, q_part, kv_part,
-    d_attn_ref, tokens_ref, mid_ref, d_mid_ref, qkv_ref, attn_ref, lse_ref, gain_ref, gain_term_ref, q_seg_ref, k_seg_ref, normed_ref, w_qkv_ref, w_out_ref, mlp_term_ref, columns_ref,
+    d_attn_ref, tokens_ref, mid_ref, d_mid_ref, qkv_ref, attn_ref, lse_ref, gain_ref, gain_term_ref, lengths_ref, normed_ref, w_qkv_ref, w_out_ref, mlp_term_ref, columns_ref,
     mixed_ref, grad_tokens_ref, grad_qkv_ref, grad_out_ref, gain_sum_ref, grad_gate_up_ref,
     buf, term, core_land, land, w_qkv, w_out, normed, d_heads, d_qkv, dk_sum, dv_sum, stage_qkv, stage_out, qkv_land, out_land, gain_stage, gain_land, d_normed, mlp_term, mlp_land, mlp_line_land, mlp_sum, row_land, row_stage, qkv_line_land,
     *sems,
@@ -1145,7 +1159,7 @@
     dv_sum[...] = jnp.zeros_like(dv_sum)
     for i in range(size // block):
         rows, cols = pl.ds(i * block, block), (i + 1) * block
-        live = seen_mask(i * block, block, cols, q_seg_ref[rows, :], k_seg_ref[:, :cols])
+        live = block_mask(lengths_ref, i * block, block, cols)
         keys, values = qkv_ref[:cols, q_part : q_part + kv_part], qkv_ref[:cols, q_part + kv_part :]
         for h in range(heads):
             span = slice(h * HEAD_DIM, (h + 1) * HEAD_DIM)
@@ -1205,6 +1219,8 @@
         sum_qkv.join(k)
     for k in range(line - 2, -1, -1):
         beside.b(k)
+    for k in range(line - 1, 1, -1):
+        beside.c(k)
 
     gain_stage[...] = jnp.zeros_like(gain_stage)
     gain_stage[1:2, :] = gain_term_ref[0:1, :]
@@ -1241,7 +1257,7 @@
             target = grad_gate_up_ref.at[:, pl.ds(pl.multiple_of((i * at.every + j) * part_ff, part_ff), part_ff)]
             pltpu.make_async_copy(row_stage.at[span, pl.ds(i * part_ff, part_ff)], target, row_sem.at[0]).start()
 
-    for k in range(line - 1, -1, -1):
+    for k in (1, 0):
         beside.c(k)
     mixed_ref[...] = (mid_ref[...] + BRANCH * mlp_sum[...]).astype(jnp.bfloat16)
     for i in range(1, line):
@@ -1274,7 +1290,7 @@
         out_copy(i).wait_send()
 
 
-def back(line, d_attn, tokens, mid, d_mid, qkv, attn_out, lse, gain, gain_term, q_seg, k_seg, normed, w_qkv, w_out, mlp_term, columns):
+def back(line, d_attn, tokens, mid, d_mid, qkv, attn_out, lse, gain, gain_term, lengths, normed, w_qkv, w_out, mlp_term, columns):
     blk, width = tokens.shape
     w_rows, cols = w_out.shape[1], w_qkv.shape[2]
     size, every = 8 * blk, 8 * line
@@ -1285,7 +1301,7 @@
     return pl.pallas_call(
         functools.partial(back_kernel, line, blk, q_part, kv_part),
         out_shape=(out((blk, width), bf16), out((blk, width), f32), out((8, w_rows, cols), f32), out((w_rows, width), f32), out((8, 128), f32), out((w_rows, every * columns.shape[1]), f32)),
-        in_specs=[any_spec] + [vmem_spec] * 10 + [any_spec] * 5,
+        in_specs=[any_spec] + [vmem_spec] * 8 + [pl.BlockSpec(memory_space=pltpu.SMEM)] + [any_spec] * 5,
         out_specs=(vmem_spec,) * 5 + (any_spec,),
         scratch_shapes=[
             pltpu.VMEM((size, width), bf16),
@@ -1322,7 +1338,7 @@
             dma((line + 1,)),
         ],
         compiler_params=pltpu.CompilerParams(collective_id=2, has_side_effects=True, vmem_limit_bytes=63 * MIB),
-    )(d_attn, tokens, mid, d_mid, qkv, attn_out, lse, gain, gain_term, q_seg, k_seg, normed, w_qkv, w_out, mlp_term, columns)
+    )(d_attn, tokens, mid, d_mid, qkv, attn_out, lse, gain, gain_term, lengths, normed, w_qkv, w_out, mlp_term, columns)
 
 
 def split_heads(w, parts):
@@ -1434,9 +1450,6 @@
     w_rows = w_qkv.shape[0]
     rows = tokens.reshape(count, width)
     grad = cotangent.reshape(count, width)
-    size = count * 8
-    seg = segment_ids(jnp.arange(size, dtype=jnp.int32), lengths[0])
-    q_seg, k_seg = seg.reshape(size, 1), seg.reshape(1, size)
     side = lax.rem(lax.axis_index("ctx") * n_shard + lax.axis_index("shard"), 2)
 
     gains = jnp.stack([gain_attn, gain_mlp])
@@ -1444,7 +1457,7 @@
     gains = jnp.where(side == 0, jnp.concatenate([gains, none], axis=1), jnp.concatenate([none, gains], axis=1))
     gains = jnp.pad(gains, ((0, 14), (0, 0)))
     mid, normed_two, qkv, attn_out, lse, tops, gain, normed_one, qkv_mine, out_mine, d_mlp, gate_up_mine = front(
-        n_shard, rows, grad, w_gate_up, gains, split_heads(w_qkv, 8).transpose(1, 0, 2), w_out, q_seg, k_seg
+        n_shard, rows, grad, w_gate_up, gains, split_heads(w_qkv, 8).transpose(1, 0, 2), w_out, lengths
     )
     heads = HEADS // 8
     head_top = jnp.max(tops[:, 0, :heads].reshape(8, n_shard, heads), axis=1).reshape(HEADS)
@@ -1454,7 +1467,7 @@
         n_shard, normed_two, d_mlp, gate_up_mine, w_down, mid, grad, gain
     )
     mixed, grad_tokens, qkv_grad, grad_out, gain_sum, grad_gate_up = back(
-        n_shard, d_attn, rows, mid, d_mid, qkv, attn_out, lse, gain, gain_term, q_seg, k_seg, normed_one, qkv_mine, out_mine, mlp_term, gate_up_grad
+        n_shard, d_attn, rows, mid, d_mid, qkv, attn_out, lse, gain, gain_term, lengths, normed_one, qkv_mine, out_mine, mlp_term, gate_up_grad
     )
     grad_qkv = join_heads(qkv_grad.transpose(1, 0, 2), 8)
     gain_grads = jnp.where(side == 0, gain_sum[:2, :w_rows], gain_sum[:2, w_rows : 2 * w_rows])

time: 520 us -> 512 us (0.985)
  Pallas kernels: 491 us -> 485 us
    pallas_call x1, Pallas kernels: 167 us -> 161 us  [back(): pl.pallas_call(functools.partial(back_kernel, line, blk, q_part, kv_part)...]
where the time goes in v7:
time: 512 us; the launch traced here: 504 us
  Pallas kernels  485 us (95%)
  local copies, waits for them, and re-layouts  14.7 us (3%)
    pallas_call x1, Pallas kernels, front(): pl.pallas_call(functools.partial(front_kernel, line, blk, q_part, kv_part...  173 us
    pallas_call x1, Pallas kernels, back(): pl.pallas_call(functools.partial(back_kernel, line, blk, q_part, kv_part)...  161 us
    pallas_call x1, Pallas kernels, mlp_exchange(): pl.pallas_call(functools.partial(mlp_kernel, line, blk, part), out_shape=...  150 us

profile of v7, /device:TPU:0, one launch (start us, length us, event | category | flops | bytes accessed | tf_op | source)
XLA Modules:
  0.0 504.1 jit_solution(4232376281787233653)
XLA Ops:
  0.7 0.7 pad_maximum_fusion.1
  1.3 0.1 broadcast_select_fusion
  1.4 0.6 pad.6.gains_ref
  2.0 0.9 fusion.1
  2.9 0.1 reshape_reshape.6
  3.1 0.1 reshape_reshape.7
  3.2 1.0 slice.33
  4.2 0.9 maximum_bitcast_fusion.w_qkv_ref
  5.1 173.2 %shard_map.160 = (f32[128,2048]{1,0:T(8,128)}, bf16[128,2048]{1,0:T(8,128)(2,1)}, bf16[1024,384]{1,0:T(8,128)(2,1)}, bf16[1024,256]{1,0:T(8,128)(2,1)}, f32[1024...) custom-call(bf16[128,2048]{1,0:T(8,128)(2,1)} %bitcast.21, ...), custom_call_target="tpu_custom_call" | custom-call | tf_op jit(solution)/shard_map/pallas_call | solution.py:1039
  178.3 0.9 slice.43
  179.2 0.6 div.7
  179.8 150.3 %shard_map.161 = (bf16[2048,2048]{1,0:T(8,128)(2,1)}, f32[128,2048]{1,0:T(8,128)}, bf16[128,2048]{1,0:T(8,128)(2,1)}, f32[8,2048]{1,0:T(8,128)}, bf16[2048,512]{1,0:T(8,128)(2,1)}, /*index=5*/f32[256,2048]{1,0:T(8,128)}) custom-call(bf16[128,2048]{1,0:T(8,128)(2,1)} %get-tuple-element.33.normed_ref, bf16[2048,2048]{1,0:T(8,128)(2,1)} %get-tuple-element.34.d_mlp_ref, ...), custom_call_target="tpu_custom_call" | custom-call | tf_op jit(solution)/shard_map/pallas_call | solution.py:669
  330.2 161.2 %shard_map.162 = (bf16[128,2048]{1,0:T(8,128)(2,1)}, f32[128,2048]{1,0:T(8,128)}, f32[8,64,384]{2,1,0:T(8,128)}, f32[64,2048]{1,0:T(8,128)}, f32[8,128]{1,0:T(8,128)}, /*index=5*/f32[64,16384]{1,0:T(8,128)}) custom-call(bf16[128,2048]{1,0:T(8,128)(2,1)} %get-tuple-element.38.d_attn_ref, bf16[128,2048]{1,0:T(8,128)(2,1)} %bitcast.22, ...), custom_call_target="tpu_custom_call" | custom-call | tf_op jit(solution)/shard_map/pallas_call | solution.py:1301
  491.4 0.8 slice_select_fusion
  492.2 0.5 slice_bitcast_fusion.1
  492.8 1.1 slice_bitcast_fusion
  493.9 1.2 fusion
  495.1 0.2 copy.30
  495.2 0.0 copy-start.4
  495.3 0.1 reshape.61
  495.4 0.2 copy.31
  495.6 0.0 copy-start.3
  495.6 0.1 reshape.62
  495.7 0.9 pad_maximum_fusion
  496.7 0.0 copy-done.4
  496.7 0.8 copy.46
  497.5 0.0 copy-done.2
  497.5 1.0 copy.47
  498.4 0.8 copy.48
  499.2 2.1 copy.49
  501.4 1.0 copy-done.1
  502.3 1.3 copy.50
  (11 shorter events, 0.1 us)
Async XLA Ops:
  495.2 1.4 copy-start.4
  495.4 2.1 copy-start.2
  495.6 2.8 copy-start.3
  495.7 3.5 copy-start
  499.2 3.1 copy-start.1

commit v8 on v7

--- a/solution.py
+++ b/solution.py
@@ -889,6 +889,8 @@
 
         w_qkv[at.c * line + at.source(k)] = w_line[at.source(k), at.c]
 
+    inner = (at.z > 0) & (at.z < line - 1)
+    outer = jnp.logical_not(inner)
     start, turn, rest, whole, end = gather
     own[0].wait()
     start()
@@ -929,6 +931,7 @@
     at.line_spread(out_line, 0)
     beside.b(0)
     beside.a(1)
+    pl.when(inner)(lambda: beside.a(2))
     spread.start(1, 4)
     for k in range(line):
 
@@ -945,7 +948,8 @@
 
     at.line_spread(out_line, 1)
     beside.b(1)
-    beside.a(2)
+    pl.when(outer)(lambda: beside.a(2))
+    pl.when(inner)(lambda: beside.a(3))
     spread.start(2, 4)
     heads = q_part // HEAD_DIM
     block = math.gcd(size, 256)
@@ -955,7 +959,6 @@
             at.line_spread(out_line, i + 1)
         if i == 2:
             beside.b(2)
-            beside.a(3)
         rows, cols = pl.ds(i * block, block), (i + 1) * block
         live = block_mask(lengths_ref, i * block, block, cols)
         keys, values = qkv_ref[:cols, q_part : q_part + kv_part], qkv_ref[:cols, q_part + kv_part :]
@@ -979,7 +982,8 @@
 
     for k in range(size // block + 1, line):
         at.line_spread(out_line, k)
-    beside.b(3)
+    pl.when(outer)(lambda: beside.a(3))
+    pl.when(inner)(lambda: beside.b(3))
     spread.start(3, 4)
     writes[2].start()
     for i, chip in enumerate((at.qd, at.qx, at.qy, at.q)):
@@ -994,6 +998,7 @@
 
         reduce[0](i)
     reduce[1](proj)
+    pl.when(outer)(lambda: beside.b(3))
 
     own_again = pltpu.make_async_copy(tokens_ref, land.at[pl.ds(0, blk), :], own_sem.at[0])
     own_again.start()

time: 512 us -> 510 us (level)
  no operation moved by 1% of the time
where the time goes in v8:
time: 510 us; the launch traced here: 502 us
  Pallas kernels  482 us (95%)
  local copies, waits for them, and re-layouts  14.7 us (3%)
    pallas_call x1, Pallas kernels, front(): pl.pallas_call(functools.partial(front_kernel, line, blk, q_part, kv_part...  170 us
    pallas_call x1, Pallas kernels, back(): pl.pallas_call(functools.partial(back_kernel, line, blk, q_part, kv_part)...  163 us
    pallas_call x1, Pallas kernels, mlp_exchange(): pl.pallas_call(functools.partial(mlp_kernel, line, blk, part), out_shape=...  149 us

profile of v8, /device:TPU:0, one launch (start us, length us, event | category | flops | bytes accessed | tf_op | source)
XLA Modules:
  0.0 501.5 jit_solution(13270588762580068086)
XLA Ops:
  0.7 0.7 pad_maximum_fusion.1
  1.3 0.1 broadcast_select_fusion
  1.4 0.6 pad.6.gains_ref
  2.0 0.9 fusion.1
  2.9 0.1 reshape_reshape.6
  3.1 0.1 reshape_reshape.7
  3.2 1.0 slice.33
  4.2 0.9 maximum_bitcast_fusion.w_qkv_ref
  5.1 170.3 %shard_map.160 = (f32[128,2048]{1,0:T(8,128)}, bf16[128,2048]{1,0:T(8,128)(2,1)}, bf16[1024,384]{1,0:T(8,128)(2,1)}, bf16[1024,256]{1,0:T(8,128)(2,1)}, f32[1024...) custom-call(bf16[128,2048]{1,0:T(8,128)(2,1)} %bitcast.21, ...), custom_call_target="tpu_custom_call" | custom-call | tf_op jit(solution)/shard_map/pallas_call | solution.py:1044
  175.4 0.9 slice.43
  176.4 0.6 div.7
  176.9 148.6 %shard_map.161 = (bf16[2048,2048]{1,0:T(8,128)(2,1)}, f32[128,2048]{1,0:T(8,128)}, bf16[128,2048]{1,0:T(8,128)(2,1)}, f32[8,2048]{1,0:T(8,128)}, bf16[2048,512]{1,0:T(8,128)(2,1)}, /*index=5*/f32[256,2048]{1,0:T(8,128)}) custom-call(bf16[128,2048]{1,0:T(8,128)(2,1)} %get-tuple-element.33.normed_ref, bf16[2048,2048]{1,0:T(8,128)(2,1)} %get-tuple-element.34.d_mlp_ref, ...), custom_call_target="tpu_custom_call" | custom-call | tf_op jit(solution)/shard_map/pallas_call | solution.py:669
  325.6 163.3 %shard_map.162 = (bf16[128,2048]{1,0:T(8,128)(2,1)}, f32[128,2048]{1,0:T(8,128)}, f32[8,64,384]{2,1,0:T(8,128)}, f32[64,2048]{1,0:T(8,128)}, f32[8,128]{1,0:T(8,128)}, /*index=5*/f32[64,16384]{1,0:T(8,128)}) custom-call(bf16[128,2048]{1,0:T(8,128)(2,1)} %get-tuple-element.38.d_attn_ref, bf16[128,2048]{1,0:T(8,128)(2,1)} %bitcast.22, ...), custom_call_target="tpu_custom_call" | custom-call | tf_op jit(solution)/shard_map/pallas_call | solution.py:1306
  488.9 0.8 slice_select_fusion
  489.7 0.5 slice_bitcast_fusion.1
  490.2 1.1 slice_bitcast_fusion
  491.3 1.2 fusion
  492.5 0.2 copy.30
  492.7 0.0 copy-start.4
  492.7 0.1 reshape.61
  492.9 0.2 copy.31
  493.0 0.0 copy-start.3
  493.1 0.1 reshape.62
  493.2 0.9 pad_maximum_fusion
  494.1 0.0 copy-done.4
  494.1 0.8 copy.46
  494.9 1.0 copy.47
  495.9 0.0 copy-done.3
  495.9 0.8 copy.48
  496.7 2.1 copy.49
  498.8 1.0 copy-done.1
  499.8 1.3 copy.50
  (11 shorter events, 0.1 us)
Async XLA Ops:
  492.7 1.4 copy-start.4
  492.8 2.1 copy-start.2
  493.0 2.8 copy-start.3
  493.2 3.5 copy-start
  496.7 3.1 copy-start.1

commit v9 on v8

--- a/solution.py
+++ b/solution.py
@@ -1224,7 +1224,7 @@
         sum_qkv.join(k)
     for k in range(line - 2, -1, -1):
         beside.b(k)
-    for k in range(line - 1, 1, -1):
+    for k in range(line - 1, 0, -1):
         beside.c(k)
 
     gain_stage[...] = jnp.zeros_like(gain_stage)
@@ -1262,8 +1262,7 @@
             target = grad_gate_up_ref.at[:, pl.ds(pl.multiple_of((i * at.every + j) * part_ff, part_ff), part_ff)]
             pltpu.make_async_copy(row_stage.at[span, pl.ds(i * part_ff, part_ff)], target, row_sem.at[0]).start()
 
-    for k in (1, 0):
-        beside.c(k)
+    beside.c(0)
     mixed_ref[...] = (mid_ref[...] + BRANCH * mlp_sum[...]).astype(jnp.bfloat16)
     for i in range(1, line):
         out_arrival(i).wait_recv()
@@ -1275,7 +1274,12 @@
     def _(i):
         qkv_copy(i, True).wait_recv()
 
-    grad_qkv_ref[...] = qkv_land[...].astype(jnp.float32)
+    for i in range(8):
+        grads = qkv_land[i].astype(jnp.float32)
+        grad_qkv_ref[:, i * q_part : (i + 1) * q_part] = grads[:, :q_part]
+        for j in (0, 1):
+            first = 8 * q_part + (8 * j + i) * kv_part
+            grad_qkv_ref[:, first : first + kv_part] = grads[:, q_part + j * kv_part : q_part + (j + 1) * kv_part]
     at.wait_all(*gain_push, sent=False)
     gain_sum_ref[...] = jnp.sum(gain_land[...], axis=0)
     end()
@@ -1305,7 +1309,7 @@
     bf16, f32, dma, out = jnp.bfloat16, jnp.float32, pltpu.SemaphoreType.DMA, jax.ShapeDtypeStruct
     return pl.pallas_call(
         functools.partial(back_kernel, line, blk, q_part, kv_part),
-        out_shape=(out((blk, width), bf16), out((blk, width), f32), out((8, w_rows, cols), f32), out((w_rows, width), f32), out((8, 128), f32), out((w_rows, every * columns.shape[1]), f32)),
+        out_shape=(out((blk, width), bf16), out((blk, width), f32), out((w_rows, 8 * cols), f32), out((w_rows, width), f32), out((8, 128), f32), out((w_rows, every * columns.shape[1]), f32)),
         in_specs=[any_spec] + [vmem_spec] * 8 + [pl.BlockSpec(memory_space=pltpu.SMEM)] + [any_spec] * 5,
         out_specs=(vmem_spec,) * 5 + (any_spec,),
         scratch_shapes=[
@@ -1471,10 +1475,9 @@
     mlp_term, d_mid, d_attn, gain_term, gate_up_grad, grad_down = mlp_exchange(
         n_shard, normed_two, d_mlp, gate_up_mine, w_down, mid, grad, gain
     )
-    mixed, grad_tokens, qkv_grad, grad_out, gain_sum, grad_gate_up = back(
+    mixed, grad_tokens, grad_qkv, grad_out, gain_sum, grad_gate_up = back(
         n_shard, d_attn, rows, mid, d_mid, qkv, attn_out, lse, gain, gain_term, lengths, normed_one, qkv_mine, out_mine, mlp_term, gate_up_grad
     )
-    grad_qkv = join_heads(qkv_grad.transpose(1, 0, 2), 8)
     gain_grads = jnp.where(side == 0, gain_sum[:2, :w_rows], gain_sum[:2, w_rows : 2 * w_rows])
     return (mixed.reshape(1, count, width), grad_tokens.reshape(1, count, width), grad_qkv, grad_out, grad_gate_up, grad_down, gain_grads[0], gain_grads[1], clip)
 

time: 510 us -> 507 us (level)
    unnamed x16 -> x14, local copies, waits for them, and re-layouts: 8.08 us -> 10.5 us
where the time goes in v9:
time: 507 us; the launch traced here: 499 us
  Pallas kernels  480 us (95%)
  local copies, waits for them, and re-layouts  15.3 us (3%)
    pallas_call x1, Pallas kernels, front(): pl.pallas_call(functools.partial(front_kernel, line, blk, q_part, kv_part...  170 us
    pallas_call x1, Pallas kernels, back(): pl.pallas_call(functools.partial(back_kernel, line, blk, q_part, kv_part)...  161 us
    pallas_call x1, Pallas kernels, mlp_exchange(): pl.pallas_call(functools.partial(mlp_kernel, line, blk, part), out_shape=...  149 us
    unnamed x14, local copies, waits for them, and re-layouts  10.5 us

profile of v9, /device:TPU:0, one launch (start us, length us, event | category | flops | bytes accessed | tf_op | source)
XLA Modules:
  0.0 498.9 jit_solution(2406584906880314163)
XLA Ops:
  0.7 0.7 pad_maximum_fusion
  1.3 0.1 broadcast_select_fusion
  1.4 0.6 pad.6.gains_ref
  2.0 0.9 fusion
  2.9 0.1 reshape_reshape.6
  3.1 0.1 reshape_reshape.7
  3.2 1.0 slice.24
  4.2 0.9 maximum_bitcast_fusion.w_qkv_ref
  5.1 170.3 %shard_map.160 = (f32[128,2048]{1,0:T(8,128)}, bf16[128,2048]{1,0:T(8,128)(2,1)}, bf16[1024,384]{1,0:T(8,128)(2,1)}, bf16[1024,256]{1,0:T(8,128)(2,1)}, f32[1024...) custom-call(bf16[128,2048]{1,0:T(8,128)(2,1)} %bitcast.17, ...), custom_call_target="tpu_custom_call" | custom-call | tf_op jit(solution)/shard_map/pallas_call | solution.py:1044
  175.4 0.9 slice.31
  176.3 0.6 div.7
  176.9 148.6 %shard_map.161 = (bf16[2048,2048]{1,0:T(8,128)(2,1)}, f32[128,2048]{1,0:T(8,128)}, bf16[128,2048]{1,0:T(8,128)(2,1)}, f32[8,2048]{1,0:T(8,128)}, bf16[2048,512]{1,0:T(8,128)(2,1)}, /*index=5*/f32[256,2048]{1,0:T(8,128)}) custom-call(bf16[128,2048]{1,0:T(8,128)(2,1)} %get-tuple-element.33.normed_ref, bf16[2048,2048]{1,0:T(8,128)(2,1)} %get-tuple-element.34.d_mlp_ref, ...), custom_call_target="tpu_custom_call" | custom-call | tf_op jit(solution)/shard_map/pallas_call | solution.py:669
  325.6 161.1 %shard_map.162 = (bf16[128,2048]{1,0:T(8,128)(2,1)}, f32[128,2048]{1,0:T(8,128)}, f32[64,3072]{1,0:T(8,128)}, f32[64,2048]{1,0:T(8,128)}, f32[8,128]{1,0:T(8,128)}, /*index=5*/f32[64,16384]{1,0:T(8,128)}) custom-call(bf16[128,2048]{1,0:T(8,128)(2,1)} %get-tuple-element.38.d_attn_ref, bf16[128,2048]{1,0:T(8,128)(2,1)} %bitcast.18, ...), custom_call_target="tpu_custom_call" | custom-call | tf_op jit(solution)/shard_map/pallas_call | solution.py:1310
  486.6 0.0 copy-start.2
  486.6 0.8 slice_select_fusion
  487.5 0.5 slice_bitcast_fusion
  488.0 0.0 copy-start.3
  488.0 1.9 copy.40
  489.9 0.0 copy-start
  489.9 2.4 copy.41
  492.4 0.0 copy-done.2
  492.4 0.9 copy.42
  493.3 0.0 copy-done.3
  493.3 0.8 copy.43
  494.1 0.0 copy-done
  494.1 0.0 copy-start.1
  494.1 2.1 copy.44
  496.2 1.0 copy-done.1
  497.2 1.3 copy.45
  (5 shorter events, 0.1 us)
Async XLA Ops:
  486.6 5.7 %copy-start.2 = (f32[64,3072]{1,0:T(8,128)S(1)}, f32[64,3072]{1,0:T(8,128)}, u32[]{:S(2)}) copy-start(f32[64,3072]{1,0:T(8,128)} %get-tuple-element.72) | copy-start | bytes 2359300
  488.0 5.3 %copy-start.3 = (f32[64,2048]{1,0:T(8,128)S(1)}, f32[64,2048]{1,0:T(8,128)}, u32[]{:S(2)}) copy-start(f32[64,2048]{1,0:T(8,128)} %get-tuple-element.73) | copy-start | bytes 1572868
  489.9 4.1 copy-start
  494.1 3.1 copy-start.1
